TPU v7x, 768 devices: a whole 4x8x12 slice. The times are simulated.
768 devices in a mesh: dp: 24 (over z_lo, x, core), seq: 32 (over y, z_hi).
Axes of the slice: x: 4, y: 8, z: 12 (z_hi: 4, z_lo: 3; z = z_hi * 3 + z_lo), core: 2. Of those that a mesh axis runs over, the one named last changes fastest.
Arguments:
- byte_states: bfloat16 [196608, 1024], P(('dp', 'seq')), parts along dimension 0, may hold values from -20 to 20
- w_qkv: bfloat16 [1024, 3072], replicated
- w_out: bfloat16 [1024, 1024], replicated, may hold values from -0.75 to 0.75
- patch_start: int32 [196608], P(('dp', 'seq')), parts along dimension 0, may hold values from 0 to 1, as said below
- latent_q: bfloat16 [24576, 2048], P(('dp', 'seq')), parts along dimension 0, may hold values from -100 to 100
- latent_k: bfloat16 [24576, 2048], P(('dp', 'seq')), parts along dimension 0, may hold values from -5 to 5
- latent_v: bfloat16 [24576, 2048], P(('dp', 'seq')), parts along dimension 0, may hold values from -6 to 6
Outputs:
- encoded: bfloat16 [196608, 1024], P(('dp', 'seq')), parts along dimension 0
- patch_embed: bfloat16 [24576, 1024], P(('dp', 'seq')), parts along dimension 0
- latent_out: bfloat16 [24576, 2048], P(('dp', 'seq')), parts along dimension 0
There are 24 independent parts, one for each index of `dp`. A program takes and returns all parts, laid end to end along the dimension named above; an argument that names none is the same for every part. Nothing has to cross between parts.
Inputs may be any that keep to these rules, and one draw needn't show every extreme that they name: `patch_start`: byte 0 opens a patch. Each block of 256 bytes holds between 16 and 32 opening bytes, and some block holds exactly 32.
All inputs are finite; a program needn't handle non-finite values.
Results may differ from a plain program's by a relative error of at most 0.007.
Values may be sent and summed in bfloat16 or wider, within the bound.
No kernel may reach another device: no remote copies, remote signals or barrier semaphores. Data moves between devices by JAX's collectives and lax.ppermute only.
A program may use at most 64 MiB of HBM per device.

v0:
```python
import jax
import jax.numpy as jnp
from jax import lax
from jax.sharding import PartitionSpec as P

BYTE_HEAD = 64
WINDOW = 512
LAT_HEADS = 16
LAT_HEAD = 128


NEGATIVE = -1e30


def from_behind(shard, axis, by):
    count = lax.axis_size(axis)
    pairs = [(i, i + by) for i in range(count) if 0 <= i + by < count]
    return lax.ppermute(shard, axis, pairs)


def attend(query_heads, key_heads, value_heads, visible, head_size):
    scores = jnp.einsum(
        "qhd,khd->hqk", query_heads, key_heads, preferred_element_type=jnp.float32
    ) * head_size ** (-0.5)
    scores = jnp.where(visible[None], scores, NEGATIVE)
    row_peak = jnp.max(scores, axis=-1, keepdims=True)
    weights = jnp.where(visible[None], jnp.exp(scores - row_peak), 0.0)
    normalizer = jnp.sum(weights, axis=-1)
    summed = jnp.einsum(
        "hqk,khd->qhd",
        weights.astype(jnp.bfloat16),
        value_heads,
        preferred_element_type=jnp.float32,
    )
    return (summed / jnp.transpose(normalizer)[:, :, None]).astype(jnp.bfloat16)


def local(byte_states, w_qkv, w_out, patch_start, latent_q, latent_k, latent_v):
    shard_rows, feature_width = byte_states.shape
    device = lax.axis_index("seq")
    hop_total = -(-WINDOW // shard_rows)
    projected = jnp.dot(byte_states, w_qkv, preferred_element_type=jnp.float32).astype(jnp.bfloat16)
    queries = projected[:, :feature_width]
    key_values = projected[:, feature_width:]
    arrived = []
    for hop_index in range(hop_total, 0, -1):
        arrived.append(from_behind(key_values, "seq", hop_index))
    previous = jnp.concatenate(arrived, axis=0)
    window_keys = jnp.concatenate([previous, key_values], axis=0)
    head_count = feature_width // BYTE_HEAD
    key_rows = window_keys.shape[0]
    query_pos = device * shard_rows + jnp.arange(shard_rows, dtype=jnp.int32)
    key_pos = (device - hop_total) * shard_rows + jnp.arange(key_rows, dtype=jnp.int32)
    visible = (
        (key_pos[None, :] >= 0)
        & (key_pos[None, :] <= query_pos[:, None])
        & (key_pos[None, :] > query_pos[:, None] - WINDOW)
    )
    attended = attend(
        queries.reshape(shard_rows, head_count, BYTE_HEAD),
        window_keys[:, :feature_width].reshape(key_rows, head_count, BYTE_HEAD),
        window_keys[:, feature_width:].reshape(key_rows, head_count, BYTE_HEAD),
        visible,
        BYTE_HEAD,
    ).reshape(shard_rows, feature_width)
    encoded = (
        byte_states.astype(jnp.float32)
        + jnp.dot(attended, w_out, preferred_element_type=jnp.float32)
    ).astype(jnp.bfloat16)
    slot_total = latent_q.shape[0]
    slot_ids = jnp.arange(slot_total, dtype=jnp.int32)
    local_slot = jnp.cumsum(patch_start) - 1
    onehot = (local_slot[:, None] == slot_ids[None, :]).astype(jnp.bfloat16)
    slot_sums = jnp.einsum("rc,rw->cw", onehot, encoded, preferred_element_type=jnp.float32)
    counts = jnp.sum(onehot.astype(jnp.float32), axis=0)
    leading = (local_slot < 0).astype(jnp.bfloat16)
    tail_sum = jnp.dot(leading[None, :], encoded, preferred_element_type=jnp.float32)
    tail_count = jnp.sum(leading.astype(jnp.float32), keepdims=True)
    received_sum, received_count = from_behind((tail_sum, tail_count), "seq", -1)
    patch_total = jnp.sum(patch_start)
    last_slot = (slot_ids == patch_total - 1).astype(jnp.float32)
    slot_sums = slot_sums + last_slot[:, None] * received_sum
    counts = counts + last_slot * received_count
    patch_embed = jnp.where(
        counts[:, None] > 0, slot_sums / jnp.maximum(counts, 1.0)[:, None], 0.0
    ).astype(jnp.bfloat16)
    slot_valid = slot_ids < patch_total
    key_valid = slot_valid.astype(jnp.bfloat16)
    latent_queries = latent_q.reshape(slot_total, LAT_HEADS, LAT_HEAD)
    query_index = device * slot_total + slot_ids
    running = jnp.full((LAT_HEADS, slot_total), NEGATIVE, jnp.float32)
    piece_keys = lax.all_gather(latent_k, "seq", axis=0, tiled=True)
    piece_values = lax.all_gather(latent_v, "seq", axis=0, tiled=True)
    piece_valid = lax.all_gather(key_valid, "seq", axis=0, tiled=True)
    piece_rows = piece_keys.shape[0]
    key_index = jnp.arange(piece_rows, dtype=jnp.int32)
    seen = (key_index[None, :] <= query_index[:, None]) & (piece_valid[None, :] > 0)
    scores = jnp.einsum(
        "qhd,khd->hqk",
        latent_queries,
        piece_keys.reshape(piece_rows, LAT_HEADS, LAT_HEAD),
        preferred_element_type=jnp.float32,
    ) * LAT_HEAD ** (-0.5)
    scores = jnp.where(seen[None], scores, NEGATIVE)
    updated = jnp.maximum(running, jnp.max(scores, axis=-1))
    weights = jnp.where(seen[None], jnp.exp(scores - updated[:, :, None]), 0.0)
    normalizer = jnp.sum(weights, axis=-1)
    summed = jnp.einsum(
        "hqk,khd->hqd",
        weights.astype(jnp.bfloat16),
        piece_values.reshape(piece_rows, LAT_HEADS, LAT_HEAD),
        preferred_element_type=jnp.float32,
    )
    latent_heads = (summed / normalizer[:, :, None]).astype(jnp.bfloat16)
    latent_heads = jnp.transpose(latent_heads, (1, 0, 2)).reshape(slot_total, LAT_HEADS * LAT_HEAD)
    latent_out = jnp.where(slot_valid[:, None], latent_heads, jnp.zeros((), jnp.bfloat16))
    return (encoded, patch_embed, latent_out)


def solution(mesh):
    return jax.shard_map(
        local,
        mesh=mesh,
        in_specs=(
            P(("dp", "seq"), None),
            P(),
            P(),
            P(("dp", "seq")),
            P(("dp", "seq"), None),
            P(("dp", "seq"), None),
            P(("dp", "seq"), None),
        ),
        out_specs=(P(("dp", "seq"), None), P(("dp", "seq"), None), P(("dp", "seq"), None)),
        check_vma=False,
    )
```

profile of v0, /device:TPU:64, one launch (start us, length us, event | category | flops | bytes accessed | tf_op | source)
XLA Modules:
  0.0 409.4 jit_solution(2913429245067481790)
XLA Ops:
  7.2 0.0 copy-start
  7.2 0.0 all-gather.3.cloned.1.call-start
  7.2 0.7 all-gather.3.cloned.1.call-update
  7.9 0.0 all-gather.5.cloned.1.call-start
  8.0 0.7 all-gather.5.cloned.1.call-update
  8.7 4.8 %convolution_convert_fusion = bf16[256,3072]{1,0:T(8,128)(2,1)S(1)} fusion(bf16[256,1024]{1,0:T(8,128)(2,1)} %param.7, bf16[1024,3072]{1,0:T(8,128)(2,1)} %param.8), kind=kOutput, calls=%fused_computation.9 | convolution fusion | flops 1611399168 | bytes 8388608 | tf_op jit(solution)/shard_map/dot_general | solution.py:42
  13.4 0.0 copy-start.3
  13.4 0.0 copy-start.7
  13.5 0.1 slice.25
  13.5 1.0 copy-done.3
  14.6 15.2 %collective-permute-start = (bf16[256,2048]{1,0:T(8,128)(2,1)S(1)}, bf16[256,2048]{1,0:T(8,128)(2,1)}, u32[]{:S(2)}, u32[]{:S(2)}) collective-permute-start(bf16[256,2048]{1,0:T(8,128)(2,1)S(1)} %slice.25), channel_id=1, source_target_pairs={{0,2},{1,3},{2,4},{3,5},{4,6},{5,7},{6,8},{7,9},{8,10},{9,11},{10,... | collective-permute-start | bytes 3145736 | tf_op jit(solution)/shard_map/ppermute | solution.py:18
  29.8 6.8 %collective-permute-start.1 = (bf16[256,2048]{1,0:T(8,128)(2,1)S(1)}, bf16[256,2048]{1,0:T(8,128)(2,1)}, u32[]{:S(2)}, u32[]{:S(2)}) collective-permute-start(bf16[256,2048]{1,0:T(8,128)(2,1)S(1)} %slice.25), channel_id=1, source_target_pairs={{0,1},{1,2},{2,3},{3,4},{4,5},{5,6},{6,7},{7,8},{8,9},{9,10},{10,1... | collective-permute-start | bytes 3145736 | tf_op jit(solution)/shard_map/ppermute | solution.py:18
  36.6 0.0 copy-done.7
  36.6 0.3 reduce-window.9
  36.9 0.1 slice.23
  37.0 0.1 slice_reduce_fusion
  37.1 0.7 convert_reduce_fusion.1
  37.8 1.3 collective-permute-start.2
  39.1 0.6 reduce_sum.47
  39.7 0.6 fusion.45
  40.4 0.7 iota_compare_fusion.5
  41.1 0.1 broadcast_compare_fusion.2
  41.2 1.9 slice.27
  43.0 2.1 copy.33
  45.7 1.3 dynamic-slice
  47.7 0.2 dynamic-update-slice
  47.9 215.1 %all-reduce = bf16[1024]{0:T(1024)(128)(2,1)S(1)} all-reduce(bf16[1024]{0:T(1024)(128)(2,1)S(1)} %dynamic-update-slice), channel_id=1, replica_groups=mesh['dp'=24,'seq'=32] {'seq'}, use_global_device_ids=true, to_apply=%add | all-reduce | flops 1024 | bytes 4096
  263.0 0.1 convert_reduce_fusion
  263.1 0.1 fusion.34
  263.2 0.3 compare_and_fusion
  263.5 0.0 collective-permute-done.2
  263.5 0.6 broadcast_compare_fusion.3
  264.1 0.0 collective-permute-done
  264.1 0.0 collective-permute-done.1
  264.2 1.7 pad_maximum_fusion
  265.9 2.0 fusion.48
  267.8 2.6 copy.34
  270.4 0.0 copy-start.5
  270.4 2.7 copy.32
  273.1 0.0 copy-done.5
  273.1 8.5 %fusion.49 = (f32[16,256]{1,0:T(8,128)S(1)}, bf16[16,256,768]{2,1,0:T(8,128)(2,1)}) fusion(pred[256,768]{1,0:T(8,128)(4,1)S(1)} %compare_and_fusion, bf16[256,16,64]{0,2,1:T(8,128)(2,1)S(1)} %bitcast.64, bf16[768,16,64]{0,2,1:T(8,128)(2,1)} %bitcast.61), kind=kOutput, calls=%fused_computation.70 | convolution fusion | flops 421528320 | bytes 8601600 | tf_op jit(solution)/shard_map/sub | solution.py:27
  281.6 0.0 copy-start.4
  281.6 5.4 %fusion.16 = bf16[256,16,64]{0,2,1:T(8,128)(2,1)S(1)} fusion(bf16[768,16,64]{0,2,1:T(8,128)(2,1)} %bitcast.62, bf16[16,256,768]{2,1,0:T(8,128)(2,1)} %get-tuple-element.10, f32[256,16]{0,1:T(8,128)S(1)} %bitcast.68), kind=kOutput, calls=%fused_computation.19 | convolution fusion | flops 403177472 | bytes 8404992 | tf_op jit(solution)/shard_map/hqk,khd->qhd/dot_general | solution.py:29
  286.9 0.0 copy-done
  286.9 0.0 copy-done.4
  287.0 0.7 fusion.19
  287.7 0.0 copy-start.2
  287.7 0.2 fusion.50
  287.9 1.5 collective-permute-start.3
  289.4 7.3 %collective-permute-done.3 = f32[1,1024]{1,0:T(1,128)S(1)} collective-permute-done((f32[1,1024]{1,0:T(1,128)S(1)}, f32[1,1024]{1,0:T(1,128)S(1)}, u32[]{:S(2)}, u32[]{:S(2)}) %collective-permute-start.3) | collective-permute-done | bytes 4128 | tf_op jit(solution)/shard_map/ppermute | solution.py:18
  296.7 0.8 select_convert_fusion
  297.5 0.0 copy-start.6
  297.5 0.0 all-gather.3.cloned.1.call-done
  297.5 6.4 %copy.35 = bf16[1024,2048]{0,1:T(8,128)(2,1)} copy(bf16[1024,2048]{1,0:T(8,128)(2,1)} %all-gather.3.cloned.1.call-done) | data formatting | bytes 8388608 | tf_op jit(solution)/shard_map/all_gather | solution.py:92
  303.9 0.0 copy-done.2
  303.9 0.0 copy-done.6
  303.9 3.1 fusion.7
  307.0 0.0 copy-start.1
  307.0 1.3 copy-done.1
  308.3 0.7 fusion.8
  309.0 82.0 %all-gather.5.cloned.1.call-done = bf16[1024,2048]{1,0:T(8,128)(2,1)} async-done(((bf16[32,2048]{1,0:T(8,128)(2,1)}), bf16[1024,2048]{1,0:T(8,128)(2,1)}) %all-gather.5.cloned.1.call-update) | async-done | bytes 4194320 | tf_op jit(solution)/shard_map/all_gather | solution.py:93
  391.0 6.4 %copy.38 = bf16[1024,2048]{0,1:T(8,128)(2,1)} copy(bf16[1024,2048]{1,0:T(8,128)(2,1)} %all-gather.5.cloned.1.call-done) | data formatting | bytes 8388608 | tf_op jit(solution)/shard_map/all_gather | solution.py:93
  397.4 4.4 %fusion.24 = bf16[16,4,8,128]{3,2,1,0:T(8,128)(2,1)S(1)} fusion(bf16[1024,16,128]{0,2,1:T(8,128)(2,1)} %bitcast.60, f32[16,32,1024]{2,1,0:T(8,128)} %copy-done.1, f32[16,32]{1,0:T(8,128)S(1)} %broadcast_maximum_fusion, pred[32,1024]{1,0:T(8,128)(4,1)S(1)} %fusion.34, f32[32,16]{0,1:T(8,128)S(1)} %bitcast.65), kind=kOutput, calls=%fused_computation.25 | convolution fusion | flops 136970240 | bytes 6459392 | tf_op jit(solution)/shard_map/hqk,khd->hqd/dot_general | solution.py:108
  401.8 0.7 bitcast_select_fusion
  (10 shorter events, 0.1 us)
Async XLA Ops:
  7.2 279.8 %copy-start = (bf16[1024,1024]{1,0:T(8,128)(2,1)S(1)}, bf16[1024,1024]{1,0:T(8,128)(2,1)}, u32[]{:S(2)}) copy-start(bf16[1024,1024]{1,0:T(8,128)(2,1)} %param.9) | copy-start | bytes 6291460
  7.2 290.3 %all-gather.3.cloned.1.call-start = ((), (), s32[]{:S(2)}) async-start(), calls=%async_computation | async-start | bytes 4325376 | tf_op jit(solution)/shard_map/all_gather | solution.py:92
  7.9 383.1 %all-gather.5.cloned.1.call-start = ((), (), s32[]{:S(2)}) async-start(), calls=%async_computation.1 | async-start | bytes 4325376 | tf_op jit(solution)/shard_map/all_gather | solution.py:93
  13.4 1.2 copy-start.3
  13.4 23.1 %copy-start.7 = (s32[256]{0:T(256)S(1)}, s32[256]{0:T(256)}, u32[]{:S(2)}) copy-start(s32[256]{0:T(256)} %param.10) | copy-start | bytes 3076
  14.6 249.5 %collective-permute-start = (bf16[256,2048]{1,0:T(8,128)(2,1)S(1)}, bf16[256,2048]{1,0:T(8,128)(2,1)}, u32[]{:S(2)}, u32[]{:S(2)}) collective-permute-start(bf16[256,2048]{1,0:T(8,128)(2,1)S(1)} %slice.25), channel_id=1, source_target_pairs={{0,2},{1,3},{2,4},{3,5},{4,6},{5,7},{6,8},{7,9},{8,10},{9,11},{10,... | collective-permute-start | bytes 3145736 | tf_op jit(solution)/shard_map/ppermute | solution.py:18
  29.8 234.3 %collective-permute-start.1 = (bf16[256,2048]{1,0:T(8,128)(2,1)S(1)}, bf16[256,2048]{1,0:T(8,128)(2,1)}, u32[]{:S(2)}, u32[]{:S(2)}) collective-permute-start(bf16[256,2048]{1,0:T(8,128)(2,1)S(1)} %slice.25), channel_id=1, source_target_pairs={{0,1},{1,2},{2,3},{3,4},{4,5},{5,6},{6,7},{7,8},{8,9},{9,10},{10,1... | collective-permute-start | bytes 3145736 | tf_op jit(solution)/shard_map/ppermute | solution.py:18
  37.8 225.7 %collective-permute-start.2 = (f32[1]{0:T(128)}, f32[1]{0:T(128)}, u32[]{:S(2)}, u32[]{:S(2)}) collective-permute-start(f32[1]{0:T(128)} %bitcast.8), channel_id=1, source_target_pairs={{1,0},{2,1},{3,2},{4,3},{5,4},{6,5},{7,6},{8,7},{9,8},{10,9},{11,1... | collective-permute-start | bytes 20 | tf_op jit(solution)/shard_map/ppermute | solution.py:18
  270.4 2.7 copy-start.5
  281.6 5.4 %copy-start.4 = (bf16[256,1024]{1,0:T(8,128)(2,1)S(1)}, bf16[256,1024]{1,0:T(8,128)(2,1)}, u32[]{:S(2)}) copy-start(bf16[256,1024]{1,0:T(8,128)(2,1)} %param.7) | copy-start | bytes 1572868
  287.7 16.2 %copy-start.2 = (bf16[256,1024]{1,0:T(8,128)(2,1)}, bf16[256,1024]{1,0:T(8,128)(2,1)S(1)}, u32[]{:S(2)}) copy-start(bf16[256,1024]{1,0:T(8,128)(2,1)S(1)} %fusion.19) | copy-start | bytes 1572868
  287.9 8.8 %collective-permute-start.3 = (f32[1,1024]{1,0:T(1,128)S(1)}, f32[1,1024]{1,0:T(1,128)S(1)}, u32[]{:S(2)}, u32[]{:S(2)}) collective-permute-start(f32[1,1024]{1,0:T(1,128)S(1)} %fusion.50), channel_id=1, source_target_pairs={{1,0},{2,1},{3,2},{4,3},{5,4},{6,5},{7,6},{8,7},{9,8},{10,9},{11,1... | collective-permute-start | bytes 12296 | tf_op jit(solution)/shard_map/ppermute | solution.py:18
  297.5 6.4 %copy-start.6 = (bf16[32,2048]{1,0:T(8,128)(2,1)S(1)}, bf16[32,2048]{1,0:T(8,128)(2,1)}, u32[]{:S(2)}) copy-start(bf16[32,2048]{1,0:T(8,128)(2,1)} %param.11) | copy-start | bytes 393220
  307.0 1.3 copy-start.1
Sparse Core Ops, SparseCore 0:
  11.8 254.4 all-gather.2
  270.0 121.0 all-gather.4
where the time goes:
time: 410 us; the launch traced here: 409 us
  blocking collectives  215 us (52%)
  waiting for transfers between devices  90.7 us (22%)
  local copies, waits for them, and re-layouts  28.2 us (7%)
  matrix products  27.8 us (7%)
  starting transfers between devices  24.8 us (6%)
  between operations  15.6 us (4%)
  other arithmetic  7.27 us (2%)
    unnamed x1, blocking collectives  215 us
    all_gather x1, waiting for transfers between devices, local(): piece_values = lax.all_gather(latent_v, 'seq', axis=0, tiled=True)  82 us
    ppermute x4, starting transfers between devices, from_behind(): return lax.ppermute(shard, axis, pairs)  24.7 us
    sub x1, matrix products, attend(): weights = jnp.where(visible[None], jnp.exp(scores - row_peak), 0.0)  8.48 us
  transfers between devices with their start and end apart: 6, of which 2 were waited for; matrix products, arithmetic and copies ran while one was open for 12% of the time, Pallas kernels for 0%

commit v1 on v0

v1 whole, which is shorter than its diff:
```python
import functools

import jax
import jax.numpy as jnp
from jax import lax
from jax.experimental import pallas as pl
from jax.experimental.pallas import tpu as pltpu
from jax.sharding import Mesh, PartitionSpec as P

BYTE_HEAD = 64
LAT_HEAD = 128
GROUP = 256
NEGATIVE = -1e30
MARK = 1024.0
SEQ = ("yh", "yl", "zh")
VMEM_LIMIT = 48 * 1024 * 1024

NT = (((1,), (1,)), ((), ()))


def shift(x, by):
    count = lax.axis_size(SEQ)
    return lax.ppermute(x, SEQ, [(i, i + by) for i in range(count) if 0 <= i + by < count])


def dot(a, b):
    return jnp.dot(a, b, preferred_element_type=jnp.float32)


def dot_nt(a, b):
    return lax.dot_general(a, b, NT, preferred_element_type=jnp.float32)


def params(*semantics):
    if semantics:
        return pltpu.CompilerParams(vmem_limit_bytes=VMEM_LIMIT, dimension_semantics=semantics)
    return pltpu.CompilerParams(vmem_limit_bytes=VMEM_LIMIT)


def pack_kernel(start_ref, q_ref, k_ref, v_ref, out_ref):
    used = jnp.sum(start_ref[...])
    rows = q_ref.shape[0]
    for head in range(out_ref.shape[0]):
        cols = pl.ds(head * LAT_HEAD, LAT_HEAD)
        out_ref[head, 0:rows] = q_ref[:, cols]
        slot = lax.broadcasted_iota(jnp.int32, (rows, LAT_HEAD), 0)
        key = k_ref[:, cols].astype(jnp.float32)
        out_ref[head, rows : 2 * rows] = jnp.where(slot < used, key, MARK).astype(jnp.bfloat16)
        out_ref[head, 2 * rows : 3 * rows] = v_ref[:, cols]


def pack(start_row, q, k, v):
    rows, width = q.shape
    return pl.pallas_call(
        pack_kernel,
        out_shape=jax.ShapeDtypeStruct((width // LAT_HEAD, 3 * rows, LAT_HEAD), jnp.bfloat16),
        compiler_params=params(),
        cost_estimate=pl.CostEstimate(flops=1000, bytes_accessed=6 * rows * width * 2, transcendentals=0),
        name="latent_pack",
    )(start_row, q, k, v)


def latent_kernel(side_ref, own_ref, other_ref, out_ref):
    blocks, rows3, _ = own_ref.shape
    rows = rows3 // 3
    total = blocks * rows
    side = side_ref[0]
    q = own_ref[:, 0:rows].reshape(total, LAT_HEAD)
    scale = LAT_HEAD ** (-0.5)
    pick = (lax.broadcasted_iota(jnp.int32, (16, LAT_HEAD), 1) == 0).astype(jnp.bfloat16)

    def position(index, parity):
        block = index // rows
        return ((block // 4) * 8 + parity * 4 + block % 4) * rows + index % rows

    query_pos = position(lax.broadcasted_iota(jnp.int32, (total, 1), 0), side)
    scores = []
    for which, (ref, parity) in enumerate(((own_ref, side), (other_ref, 1 - side))):
        base = rows if which == 0 else 0
        key = ref[:, base : base + rows].reshape(total, LAT_HEAD)
        mark = dot_nt(pick, key)[0:1]
        key_pos = position(lax.broadcasted_iota(jnp.int32, (1, total), 1), parity)
        key_pos = jnp.where(mark < MARK / 2, key_pos, 1 << 30)
        s = dot_nt(q, key) * scale
        scores.append(jnp.where(key_pos <= query_pos, s, NEGATIVE))
    peak = jnp.maximum(jnp.max(scores[0], axis=1, keepdims=True), jnp.max(scores[1], axis=1, keepdims=True))
    norm = jnp.zeros_like(peak)
    summed = jnp.zeros((total, LAT_HEAD), jnp.float32)
    for which, ref in enumerate((own_ref, other_ref)):
        base = 2 * rows if which == 0 else rows
        value = ref[:, base : base + rows].reshape(total, LAT_HEAD)
        weight = jnp.exp(scores[which] - peak)
        norm = norm + jnp.sum(weight, axis=1, keepdims=True)
        summed = summed + dot(weight.astype(jnp.bfloat16), value)
    out_ref[...] = (summed / norm).astype(jnp.bfloat16).reshape(blocks, rows, LAT_HEAD)


def latent_attend(side, own, other):
    blocks, rows3, width = own.shape
    rows = rows3 // 3
    total = blocks * rows
    return pl.pallas_call(
        latent_kernel,
        out_shape=jax.ShapeDtypeStruct((blocks, rows, width), jnp.bfloat16),
        in_specs=[
            pl.BlockSpec(memory_space=pltpu.SMEM),
            pl.BlockSpec(memory_space=pltpu.VMEM),
            pl.BlockSpec(memory_space=pltpu.VMEM),
        ],
        compiler_params=params(),
        cost_estimate=pl.CostEstimate(
            flops=8 * total * total * width, bytes_accessed=12 * total * width, transcendentals=2 * total * total
        ),
        name="latent_attend",
    )(side, own, other)


def unpack_kernel(start_ref, heads_ref, out_ref):
    used = jnp.sum(start_ref[...])
    rows = out_ref.shape[0]
    for head in range(heads_ref.shape[0]):
        slot = lax.broadcasted_iota(jnp.int32, (rows, LAT_HEAD), 0)
        value = heads_ref[head].astype(jnp.float32)
        out_ref[:, pl.ds(head * LAT_HEAD, LAT_HEAD)] = jnp.where(slot < used, value, 0.0).astype(jnp.bfloat16)


def unpack(start_row, heads):
    count, rows, width = heads.shape
    return pl.pallas_call(
        unpack_kernel,
        out_shape=jax.ShapeDtypeStruct((rows, count * width), jnp.bfloat16),
        compiler_params=params(),
        cost_estimate=pl.CostEstimate(flops=1000, bytes_accessed=4 * count * rows * width, transcendentals=0),
        name="latent_unpack",
    )(start_row, heads)


def in_head(shape, head):
    column = lax.broadcasted_iota(jnp.int32, shape, 1)
    return (column >= head * BYTE_HEAD) & (column < (head + 1) * BYTE_HEAD)


def near_kernel(block_ref, own_ref, before_ref, wq_ref, wk_ref, wv_ref, q_ref, acc_ref, stat_ref):
    rows = own_ref.shape[0]
    own = own_ref[...]
    before = before_ref[...]
    q = dot(own, wq_ref[...]).astype(jnp.bfloat16)
    q = (q.astype(jnp.float32) * BYTE_HEAD ** (-0.5)).astype(jnp.bfloat16)
    q_ref[...] = q
    keys = [dot(x, wk_ref[...]).astype(jnp.bfloat16) for x in (own, before)]
    values = [dot(x, wv_ref[...]).astype(jnp.bfloat16) for x in (own, before)]
    row = lax.broadcasted_iota(jnp.int32, (rows, rows), 0)
    col = lax.broadcasted_iota(jnp.int32, (rows, rows), 1)
    own_seen = col <= row
    before_bias = jnp.where(block_ref[0] >= 1, 0.0, NEGATIVE)
    lane = lax.broadcasted_iota(jnp.int32, (rows, 128), 1)
    acc = jnp.zeros((rows, GROUP), jnp.float32)
    stat = jnp.zeros((rows, 128), jnp.float32)
    heads = GROUP // BYTE_HEAD
    for head in range(heads):
        mask = in_head((rows, GROUP), head)
        qh = jnp.where(mask, q, jnp.zeros_like(q))
        s0 = jnp.where(own_seen, dot_nt(qh, keys[0]), NEGATIVE)
        s1 = dot_nt(qh, keys[1]) + before_bias
        peak = jnp.maximum(jnp.max(s0, axis=1, keepdims=True), jnp.max(s1, axis=1, keepdims=True))
        w0 = jnp.exp(s0 - peak)
        w1 = jnp.exp(s1 - peak)
        norm = jnp.sum(w0, axis=1, keepdims=True) + jnp.sum(w1, axis=1, keepdims=True)
        summed = dot(w0.astype(jnp.bfloat16), values[0]) + dot(w1.astype(jnp.bfloat16), values[1])
        acc = jnp.where(mask, summed, acc)
        stat = jnp.where(lane == head, peak, stat)
        stat = jnp.where(lane == heads + head, norm, stat)
    acc_ref[...] = acc
    stat_ref[...] = stat


def near(block, own, before, w_qkv):
    rows, width = own.shape
    steps = width // GROUP

    def weight(part):
        return pl.BlockSpec((width, GROUP), lambda i: (0, part * steps + i))

    whole = pl.BlockSpec((rows, width), lambda i: (0, 0))
    return pl.pallas_call(
        near_kernel,
        grid=(steps,),
        out_shape=(
            jax.ShapeDtypeStruct((rows, width), jnp.bfloat16),
            jax.ShapeDtypeStruct((rows, width), jnp.float32),
            jax.ShapeDtypeStruct((rows, steps * 128), jnp.float32),
        ),
        in_specs=[pl.BlockSpec(memory_space=pltpu.SMEM), whole, whole, weight(0), weight(1), weight(2)],
        out_specs=(
            pl.BlockSpec((rows, GROUP), lambda i: (0, i)),
            pl.BlockSpec((rows, GROUP), lambda i: (0, i)),
            pl.BlockSpec((rows, 128), lambda i: (0, i)),
        ),
        compiler_params=params("arbitrary"),
        cost_estimate=pl.CostEstimate(
            flops=10 * rows * width * width + 64 * rows * rows * GROUP,
            bytes_accessed=6 * width * width + 8 * rows * width,
            transcendentals=32 * rows * rows,
        ),
        name="near_attention",
    )(block, own, before, w_qkv, w_qkv, w_qkv)


def far_kernel(
    block_ref, start_ref, own_ref, far_ref, q_ref, acc_ref, stat_ref, wk_ref, wv_ref, wo_ref,
    enc_ref, sums_ref, lead_ref, count_ref, total_ref,
):
    step = pl.program_id(0)
    rows = own_ref.shape[0]
    far = far_ref[...]
    key = dot(far, wk_ref[...]).astype(jnp.bfloat16)
    value = dot(far, wv_ref[...]).astype(jnp.bfloat16)
    q = q_ref[...]
    acc = acc_ref[...]
    stat = stat_ref[...]
    row = lax.broadcasted_iota(jnp.int32, (rows, rows), 0)
    col = lax.broadcasted_iota(jnp.int32, (rows, rows), 1)
    first = jnp.where(block_ref[0] >= 2, 0, 2 * rows)
    seen = col > row + first
    heads = GROUP // BYTE_HEAD
    attended = jnp.zeros((rows, GROUP), jnp.float32)
    for head in range(heads):
        mask = in_head((rows, GROUP), head)
        qh = jnp.where(mask, q, jnp.zeros_like(q))
        s = jnp.where(seen, dot_nt(qh, key), NEGATIVE)
        peak = stat[:, head : head + 1]
        norm = stat[:, heads + head : heads + head + 1]
        newer = jnp.maximum(peak, jnp.max(s, axis=1, keepdims=True))
        weight = jnp.exp(s - newer)
        fade = jnp.exp(peak - newer)
        norm = norm * fade + jnp.sum(weight, axis=1, keepdims=True)
        summed = acc * fade + dot(weight.astype(jnp.bfloat16), value)
        attended = jnp.where(mask, summed / norm, attended)
    product = dot(attended.astype(jnp.bfloat16), wo_ref[...])

    @pl.when(step == 0)
    def _():
        total_ref[...] = product

    @pl.when(step > 0)
    def _():
        total_ref[...] += product

    @pl.when(step == pl.num_programs(0) - 1)
    def _():
        encoded = (own_ref[...].astype(jnp.float32) + total_ref[...]).astype(jnp.bfloat16)
        enc_ref[...] = encoded
        slots = sums_ref.shape[0]
        start = jnp.broadcast_to(start_ref[...].astype(jnp.float32), (16, rows)).astype(jnp.bfloat16)
        before_or_at = (row <= col).astype(jnp.float32).astype(jnp.bfloat16)
        rank = dot(start, before_or_at)[0:1].astype(jnp.int32) - 1
        slot = lax.broadcasted_iota(jnp.int32, (slots + 16, rows), 0)
        slot = jnp.where(slot >= slots, slots - 1 - slot, slot)
        onehot = (rank == slot).astype(jnp.float32)
        summed = dot(onehot.astype(jnp.bfloat16), encoded)
        counts = jnp.sum(onehot, axis=1, keepdims=True)
        sums_ref[...] = summed[0:slots]
        count_ref[...] = jnp.broadcast_to(counts[0:slots], (slots, 128))
        width = own_ref.shape[1]
        lead_ref[:, 0:width] = summed[slots : slots + 1]
        lead_ref[:, width : width + 128] = jnp.broadcast_to(counts[slots : slots + 1], (1, 128))


def far_attend(block, start_row, own, far, q, acc, stat, w_qkv, w_out, slots):
    rows, width = own.shape
    steps = width // GROUP

    def weight(part):
        return pl.BlockSpec((width, GROUP), lambda i: (0, part * steps + i))

    def full(shape):
        return pl.BlockSpec(shape, lambda i: (0, 0))

    piece = pl.BlockSpec((rows, GROUP), lambda i: (0, i))
    return pl.pallas_call(
        far_kernel,
        grid=(steps,),
        out_shape=(
            jax.ShapeDtypeStruct((rows, width), jnp.bfloat16),
            jax.ShapeDtypeStruct((slots, width), jnp.float32),
            jax.ShapeDtypeStruct((1, width + 128), jnp.float32),
            jax.ShapeDtypeStruct((slots, 128), jnp.float32),
        ),
        in_specs=[
            pl.BlockSpec(memory_space=pltpu.SMEM),
            full((1, rows)),
            full((rows, width)),
            full((rows, width)),
            piece,
            piece,
            pl.BlockSpec((rows, 128), lambda i: (0, i)),
            weight(1),
            weight(2),
            pl.BlockSpec((GROUP, width), lambda i: (i, 0)),
        ],
        out_specs=(full((rows, width)), full((slots, width)), full((1, width + 128)), full((slots, 128))),
        scratch_shapes=[pltpu.VMEM((rows, width), jnp.float32)],
        compiler_params=params("arbitrary"),
        cost_estimate=pl.CostEstimate(
            flops=6 * rows * width * width + 32 * rows * rows * GROUP,
            bytes_accessed=6 * width * width + 12 * rows * width,
            transcendentals=16 * rows * rows,
        ),
        name="far_attention",
    )(block, start_row, own, far, q, acc, stat, w_qkv, w_qkv, w_out)


def pool_kernel(start_ref, sums_ref, count_ref, extra_ref, out_ref):
    slots, width = sums_ref.shape
    used = jnp.sum(start_ref[...])
    last = lax.broadcasted_iota(jnp.int32, (slots, 1), 0) == used - 1
    extra = extra_ref[...]
    sums = sums_ref[...] + jnp.where(last, extra[:, 0:width], 0.0)
    count = count_ref[:, 0:1] + jnp.where(last, extra[:, width : width + 1], 0.0)
    mean = sums / jnp.maximum(count, 1.0)
    out_ref[...] = jnp.where(count > 0, mean, 0.0).astype(jnp.bfloat16)


def pool(start_row, sums, count, extra):
    return pl.pallas_call(
        pool_kernel,
        out_shape=jax.ShapeDtypeStruct(sums.shape, jnp.bfloat16),
        compiler_params=params(),
        name="patch_pool",
    )(start_row, sums, count, extra)


def local(byte_states, w_qkv, w_out, patch_start, latent_q, latent_k, latent_v):
    rows, _ = byte_states.shape
    slots = latent_q.shape[0]
    block = lax.axis_index(SEQ).astype(jnp.int32).reshape(1)
    side = lax.axis_index("yl").astype(jnp.int32).reshape(1)
    start_row = patch_start.reshape(1, rows)

    before = shift(byte_states, 1)
    far = shift(byte_states, 2)

    packed = pack(start_row, latent_q, latent_k, latent_v)
    own = lax.all_to_all(packed, ("yh", "zh"), 0, 0, tiled=True)
    other = lax.ppermute(own[:, slots:], "yl", [(0, 1), (1, 0)])
    q, acc, stat = near(block, byte_states, before, w_qkv)
    heads = latent_attend(side, own, other)
    returned = lax.all_to_all(heads, ("yh", "zh"), 0, 0, tiled=True)
    latent_out = unpack(start_row, returned)

    encoded, sums, lead, count = far_attend(
        block, start_row, byte_states, far, q, acc, stat, w_qkv, w_out, slots
    )
    extra = shift(lead, -1)
    patch_embed = pool(start_row, sums, count, extra)
    return encoded, patch_embed, latent_out


def solution(mesh):
    folded = Mesh(mesh.devices.reshape(mesh.shape["dp"], 4, 2, 4), ("dp", "yh", "yl", "zh"))
    spec = P(("dp", *SEQ), None)
    return jax.shard_map(
        local,
        mesh=folded,
        in_specs=(spec, P(), P(), P(("dp", *SEQ)), spec, spec, spec),
        out_specs=(spec, spec, spec),
        check_vma=False,
    )
```

time: 410 us -> 147 us (0.36)
  the two profiles are of different devices: /device:TPU:64 before, /device:TPU:18 now
where the time goes in v1:
time: 147 us; the launch traced here: 146 us
  waiting for transfers between devices  65.3 us (44%)
  starting transfers between devices  43.4 us (30%)
  Pallas kernels  32.6 us (22%)
  local copies, waits for them, and re-layouts  4.45 us (3%)
    ppermute x3, waiting for transfers between devices, shift(): lax.ppermute(x, SEQ, [(i, i + by) for i in range(count) if 0 <= i + by <...  49.7 us
    all_to_all x1, starting transfers between devices, local(): own = lax.all_to_all(packed, ('yh', 'zh'), 0, 0, tiled=True)  20.1 us
    pallas_call x1, Pallas kernels, far_attend(): pl.pallas_call(far_kernel, grid=(steps,), out_shape=(jax.ShapeDtypeStruct...  18.6 us
    ppermute x3, starting transfers between devices, shift(): lax.ppermute(x, SEQ, [(i, i + by) for i in range(count) if 0 <= i + by <...  12.5 us
    all_to_all x1, waiting for transfers between devices, local(): own = lax.all_to_all(packed, ('yh', 'zh'), 0, 0, tiled=True)  11.5 us
    pallas_call x1, Pallas kernels, near(): pl.pallas_call(near_kernel, grid=(steps,), out_shape=(jax.ShapeDtypeStruc...  9.2 us
    all_to_all x1, starting transfers between devices, local(): returned = lax.all_to_all(heads, ('yh', 'zh'), 0, 0, tiled=True)  8.01 us
    unnamed x14, local copies, waits for them, and re-layouts  4.43 us
  transfers between devices with their start and end apart: 6, of which 4 were waited for; matrix products, arithmetic and copies ran while one was open for 0% of the time, Pallas kernels for 21%

profile of v1, /device:TPU:18, one launch (start us, length us, event | category | flops | bytes accessed | tf_op | source)
XLA Modules:
  0.0 146.4 jit_solution(2692658351034496141)
XLA Ops:
  0.6 0.0 copy-start.2
  0.6 0.9 copy-done.2
  1.5 0.0 copy-start.3
  1.5 0.9 copy-done.3
  2.4 0.0 copy-start.4
  2.4 0.9 copy-done.4
  3.3 0.0 copy-start.5
  3.3 0.7 copy-done.5
  4.0 0.9 latent_pack.1
  4.9 20.1 %all-to-all-start = ((bf16[16,96,128]{2,1,0:T(8,128)(2,1)}), bf16[16,96,128]{2,1,0:T(8,128)(2,1)S(1)}, u32[]{:S(2)}, u32[]{:S(2)}) async-start(bf16[16,96,128]{2,1,0:T(8,128)(2,1)} %latent_pack.1), calls=%async_computation | async-start | bytes 786432 | tf_op jit(solution)/shard_map/all_to_all | solution.py:344
  25.0 5.2 %collective-permute-start.1 = (bf16[256,1024]{1,0:T(8,128)(2,1)}, bf16[256,1024]{1,0:T(8,128)(2,1)S(1)}, u32[]{:S(2)}, u32[]{:S(2)}) collective-permute-start(bf16[256,1024]{1,0:T(8,128)(2,1)} %own_ref.3), channel_id=1, source_target_pairs={{0,1},{1,2},{2,3},{3,4},{4,5},{5,6},{6,7},{7,8},{8,9},{9,10},{10,1... | collective-permute-start | bytes 1572872 | tf_op jit(solution)/shard_map/ppermute | solution.py:23
  30.2 11.5 %all-to-all-done.own_ref = bf16[16,96,128]{2,1,0:T(8,128)(2,1)S(1)} async-done(((bf16[16,96,128]{2,1,0:T(8,128)(2,1)}), bf16[16,96,128]{2,1,0:T(8,128)(2,1)S(1)}, u32[]{:S(2)}, u32[]{:S(2)}) %all-to-all-start) | async-done | bytes 393248 | tf_op jit(solution)/shard_map/all_to_all | solution.py:344
  41.8 2.8 %collective-permute-start.3 = (bf16[16,64,128]{2,1,0:T(8,128)(2,1)S(1)}, bf16[16,64,128]{2,1,0:T(8,128)(2,1)S(1)}, u32[]{:S(2)}, u32[]{:S(2)}) collective-permute-start(bf16[16,64,128]{2,1,0:T(8,128)(2,1)S(1)} %slice.4), channel_id=1, source_target_pairs={{0,4},{4,0},{1,5},{5,1},{2,6},{6,2},{3,7},{7,3},{8,12},{12,8},{9,1... | collective-permute-start | bytes 786440 | tf_op jit(solution)/shard_map/ppermute | solution.py:345
  44.6 5.4 %collective-permute-start = (bf16[256,1024]{1,0:T(8,128)(2,1)}, bf16[256,1024]{1,0:T(8,128)(2,1)S(1)}, u32[]{:S(2)}, u32[]{:S(2)}) collective-permute-start(bf16[256,1024]{1,0:T(8,128)(2,1)} %own_ref.3), channel_id=1, source_target_pairs={{0,2},{1,3},{2,4},{3,5},{4,6},{5,7},{6,8},{7,9},{8,10},{9,11},{10,... | collective-permute-start | bytes 1572872 | tf_op jit(solution)/shard_map/ppermute | solution.py:23
  50.0 4.0 %collective-permute-done.3.other_ref = bf16[16,64,128]{2,1,0:T(8,128)(2,1)S(1)} collective-permute-done((bf16[16,64,128]{2,1,0:T(8,128)(2,1)S(1)}, bf16[16,64,128]{2,1,0:T(8,128)(2,1)S(1)}, u32[]{:S(2)}, u32[]{:S(2)}) %collective-permute-start.3) | collective-permute-done | bytes 262176 | tf_op jit(solution)/shard_map/ppermute | solution.py:345
  54.0 2.2 %latent_attend.1 = bf16[16,32,128]{2,1,0:T(8,128)(2,1)} custom-call(s32[1]{0:T(128)} %bitcast.2.side_ref, bf16[16,96,128]{2,1,0:T(8,128)(2,1)S(1)} %all-to-all-done.own_ref, bf16[16,64,128]{2,1,0:T(8,128)(2,1)S(1)} %collective-permute-done.3.other_ref), custom_call_target="tpu_custom_call" | custom-call | flops 268435456 | bytes 786432 | tf_op jit(solution)/shard_map/latent_attend/pallas_call | solution.py:102
  56.2 8.0 %all-to-all-start.1 = ((bf16[16,32,128]{2,1,0:T(8,128)(2,1)}), bf16[16,32,128]{2,1,0:T(8,128)(2,1)S(1)}, u32[]{:S(2)}, u32[]{:S(2)}) async-start(bf16[16,32,128]{2,1,0:T(8,128)(2,1)} %latent_attend.1), calls=%async_computation.1 | async-start | bytes 262144 | tf_op jit(solution)/shard_map/all_to_all | solution.py:348
  64.2 0.0 collective-permute-done.1.before_ref
  64.2 0.0 copy-start
  64.3 1.0 copy-done
  65.3 0.0 copy-start.1
  65.3 0.0 copy-start.6
  65.3 9.2 %near_attention.1 = (bf16[256,1024]{1,0:T(8,128)(2,1)S(1)}, f32[256,1024]{1,0:T(8,128)S(1)}, f32[256,512]{1,0:T(8,128)S(1)}) custom-call(s32[1]{0:T(128)} %bitcast.block_ref, bf16[256,1024]{1,0:T(8,128)(2,1)S(1)} %copy-done, bf16[256,1024]{1,0:T(8,128)(2,1)S(1)} %collective-permute-done.1.before_ref, bf16[1024,3072]{1,0:T(8,128)(2,1)} %wv_ref.3, ...), custom_call_target="tpu_custom_call" | custom-call | flops 3758096384 | bytes 8388608 | tf_op jit(solution)/shard_map/near_attention/pallas_call | solution.py:185
  74.5 27.3 %collective-permute-done.far_ref = bf16[256,1024]{1,0:T(8,128)(2,1)S(1)} collective-permute-done((bf16[256,1024]{1,0:T(8,128)(2,1)}, bf16[256,1024]{1,0:T(8,128)(2,1)S(1)}, u32[]{:S(2)}, u32[]{:S(2)}) %collective-permute-start) | collective-permute-done | bytes 524320 | tf_op jit(solution)/shard_map/ppermute | solution.py:23
  101.8 0.0 copy-done.1
  101.9 0.0 copy-done.6
  101.9 18.6 %far_attention.1 = (bf16[256,1024]{1,0:T(8,128)(2,1)}, f32[32,1024]{1,0:T(8,128)S(1)}, f32[1,1152]{1,0:T(1,128)S(1)}, f32[32,128]{1,0:T(8,128)S(1)}) custom-call(s32[1]{0:T(128)} %bitcast.block_ref, s32[1,256]{1,0:T(1,128)S(1)} %bitcast.4, bf16[256,1024]{1,0:T(8,128)(2,1)S(1)} %copy-done, bf16[256,1024]{1,0:T(8,128)(2,1)S(1)} %collective-permute-done.far_ref, ...), custom_call_target="tpu_custom_call" | custom-call | flops 2147483648 | bytes 9437184 | tf_op jit(solution)/shard_map/far_attention/pallas_call | solution.py:280
  120.4 1.9 %collective-permute-start.2 = (f32[1,1152]{1,0:T(1,128)S(1)}, f32[1,1152]{1,0:T(1,128)S(1)}, u32[]{:S(2)}, u32[]{:S(2)}) collective-permute-start(f32[1,1152]{1,0:T(1,128)S(1)} %get-tuple-element.16), channel_id=1, source_target_pairs={{1,0},{2,1},{3,2},{4,3},{5,4},{6,5},{7,6},{8,7},{9,8},{10,9},{11,1... | collective-permute-start | bytes 13832 | tf_op jit(solution)/shard_map/ppermute | solution.py:23
  122.3 22.4 %collective-permute-done.2.extra_ref = f32[1,1152]{1,0:T(1,128)S(1)} collective-permute-done((f32[1,1152]{1,0:T(1,128)S(1)}, f32[1,1152]{1,0:T(1,128)S(1)}, u32[]{:S(2)}, u32[]{:S(2)}) %collective-permute-start.2) | collective-permute-done | bytes 4640 | tf_op jit(solution)/shard_map/ppermute | solution.py:23
  144.7 0.9 patch_pool.1
  145.6 0.0 all-to-all-done.1.heads_ref
  145.6 0.8 latent_unpack.1
  (1 shorter events, 0.0 us)
Async XLA Ops:
  0.6 0.9 copy-start.2
  1.5 0.9 copy-start.3
  2.4 0.9 copy-start.4
  3.3 0.7 copy-start.5
  4.9 36.8 %all-to-all-start = ((bf16[16,96,128]{2,1,0:T(8,128)(2,1)}), bf16[16,96,128]{2,1,0:T(8,128)(2,1)S(1)}, u32[]{:S(2)}, u32[]{:S(2)}) async-start(bf16[16,96,128]{2,1,0:T(8,128)(2,1)} %latent_pack.1), calls=%async_computation | async-start | bytes 786432 | tf_op jit(solution)/shard_map/all_to_all | solution.py:344
  25.0 39.2 %collective-permute-start.1 = (bf16[256,1024]{1,0:T(8,128)(2,1)}, bf16[256,1024]{1,0:T(8,128)(2,1)S(1)}, u32[]{:S(2)}, u32[]{:S(2)}) collective-permute-start(bf16[256,1024]{1,0:T(8,128)(2,1)} %own_ref.3), channel_id=1, source_target_pairs={{0,1},{1,2},{2,3},{3,4},{4,5},{5,6},{6,7},{7,8},{8,9},{9,10},{10,1... | collective-permute-start | bytes 1572872 | tf_op jit(solution)/shard_map/ppermute | solution.py:23
  41.8 12.2 %collective-permute-start.3 = (bf16[16,64,128]{2,1,0:T(8,128)(2,1)S(1)}, bf16[16,64,128]{2,1,0:T(8,128)(2,1)S(1)}, u32[]{:S(2)}, u32[]{:S(2)}) collective-permute-start(bf16[16,64,128]{2,1,0:T(8,128)(2,1)S(1)} %slice.4), channel_id=1, source_target_pairs={{0,4},{4,0},{1,5},{5,1},{2,6},{6,2},{3,7},{7,3},{8,12},{12,8},{9,1... | collective-permute-start | bytes 786440 | tf_op jit(solution)/shard_map/ppermute | solution.py:345
  44.6 57.3 %collective-permute-start = (bf16[256,1024]{1,0:T(8,128)(2,1)}, bf16[256,1024]{1,0:T(8,128)(2,1)S(1)}, u32[]{:S(2)}, u32[]{:S(2)}) collective-permute-start(bf16[256,1024]{1,0:T(8,128)(2,1)} %own_ref.3), channel_id=1, source_target_pairs={{0,2},{1,3},{2,4},{3,5},{4,6},{5,7},{6,8},{7,9},{8,10},{9,11},{10,... | collective-permute-start | bytes 1572872 | tf_op jit(solution)/shard_map/ppermute | solution.py:23
  56.2 89.3 %all-to-all-start.1 = ((bf16[16,32,128]{2,1,0:T(8,128)(2,1)}), bf16[16,32,128]{2,1,0:T(8,128)(2,1)S(1)}, u32[]{:S(2)}, u32[]{:S(2)}) async-start(bf16[16,32,128]{2,1,0:T(8,128)(2,1)} %latent_attend.1), calls=%async_computation.1 | async-start | bytes 262144 | tf_op jit(solution)/shard_map/all_to_all | solution.py:348
  64.2 1.0 copy-start
  65.3 36.6 %copy-start.1 = (bf16[1024,1024]{1,0:T(8,128)(2,1)S(1)}, bf16[1024,1024]{1,0:T(8,128)(2,1)}, u32[]{:S(2)}) copy-start(bf16[1024,1024]{1,0:T(8,128)(2,1)} %wo_ref.1) | copy-start | bytes 6291460
  65.3 36.6 %copy-start.6 = (s32[256]{0:T(256)S(1)}, s32[256]{0:T(256)}, u32[]{:S(2)}) copy-start(s32[256]{0:T(256)} %param.10) | copy-start | bytes 3076
  120.4 24.3 %collective-permute-start.2 = (f32[1,1152]{1,0:T(1,128)S(1)}, f32[1,1152]{1,0:T(1,128)S(1)}, u32[]{:S(2)}, u32[]{:S(2)}) collective-permute-start(f32[1,1152]{1,0:T(1,128)S(1)} %get-tuple-element.16), channel_id=1, source_target_pairs={{1,0},{2,1},{3,2},{4,3},{5,4},{6,5},{7,6},{8,7},{9,8},{10,9},{11,1... | collective-permute-start | bytes 13832 | tf_op jit(solution)/shard_map/ppermute | solution.py:23

commit v2 on v1

--- a/solution.py
+++ b/solution.py
@@ -11,6 +11,7 @@
 LAT_HEAD = 128
 GROUP = 256
 NEGATIVE = -1e30
+UP_ROWS = 128
 MARK = 1024.0
 SEQ = ("yh", "yl", "zh")
 VMEM_LIMIT = 48 * 1024 * 1024
@@ -21,6 +22,18 @@
 def shift(x, by):
     count = lax.axis_size(SEQ)
     return lax.ppermute(x, SEQ, [(i, i + by) for i in range(count) if 0 <= i + by < count])
+
+
+def down(x, reach):
+    count, ring = lax.axis_size(SEQ), lax.axis_size("zh")
+
+    def after(source, steps):
+        return source - source % ring + (source - steps) % ring
+
+    sources = range(count - reach)
+    for step in range(1, ring - reach):
+        x = lax.ppermute(x, SEQ, [(after(s, step - 1), after(s, step)) for s in sources])
+    return lax.ppermute(x, SEQ, [(after(s, ring - reach - 1), s + reach) for s in sources])
 
 
 def dot(a, b):
@@ -55,7 +68,7 @@
         pack_kernel,
         out_shape=jax.ShapeDtypeStruct((width // LAT_HEAD, 3 * rows, LAT_HEAD), jnp.bfloat16),
         compiler_params=params(),
-        cost_estimate=pl.CostEstimate(flops=1000, bytes_accessed=6 * rows * width * 2, transcendentals=0),
+        cost_estimate=pl.CostEstimate(flops=1000, bytes_accessed=1000, transcendentals=0),
         name="latent_pack",
     )(start_row, q, k, v)
 
@@ -108,9 +121,7 @@
             pl.BlockSpec(memory_space=pltpu.VMEM),
         ],
         compiler_params=params(),
-        cost_estimate=pl.CostEstimate(
-            flops=8 * total * total * width, bytes_accessed=12 * total * width, transcendentals=2 * total * total
-        ),
+        cost_estimate=pl.CostEstimate(flops=1000, bytes_accessed=1000, transcendentals=0),
         name="latent_attend",
     )(side, own, other)
 
@@ -130,17 +141,25 @@
         unpack_kernel,
         out_shape=jax.ShapeDtypeStruct((rows, count * width), jnp.bfloat16),
         compiler_params=params(),
-        cost_estimate=pl.CostEstimate(flops=1000, bytes_accessed=4 * count * rows * width, transcendentals=0),
+        cost_estimate=pl.CostEstimate(flops=1000, bytes_accessed=1000, transcendentals=0),
         name="latent_unpack",
     )(start_row, heads)
 
 
-def in_head(shape, head):
-    column = lax.broadcasted_iota(jnp.int32, shape, 1)
-    return (column >= head * BYTE_HEAD) & (column < (head + 1) * BYTE_HEAD)
-
-
-def near_kernel(block_ref, own_ref, before_ref, wq_ref, wk_ref, wv_ref, q_ref, acc_ref, stat_ref):
+def halves():
+    return [slice(start, start + 128) for start in range(0, GROUP, 128)]
+
+
+def low_lanes(rows):
+    return lax.broadcasted_iota(jnp.int32, (rows, 128), 1) < BYTE_HEAD
+
+
+def split_heads(x, low, fill):
+    other = jnp.full_like(x, fill)
+    return jnp.where(low, x, other), jnp.where(low, other, x)
+
+
+def near_kernel(block_ref, own_ref, before_ref, wq_ref, wk_ref, wv_ref, q_ref, acc_ref, peak_ref, norm_ref):
     rows = own_ref.shape[0]
     own = own_ref[...]
     before = before_ref[...]
@@ -153,25 +172,21 @@
     col = lax.broadcasted_iota(jnp.int32, (rows, rows), 1)
     own_seen = col <= row
     before_bias = jnp.where(block_ref[0] >= 1, 0.0, NEGATIVE)
-    lane = lax.broadcasted_iota(jnp.int32, (rows, 128), 1)
-    acc = jnp.zeros((rows, GROUP), jnp.float32)
-    stat = jnp.zeros((rows, 128), jnp.float32)
-    heads = GROUP // BYTE_HEAD
-    for head in range(heads):
-        mask = in_head((rows, GROUP), head)
-        qh = jnp.where(mask, q, jnp.zeros_like(q))
-        s0 = jnp.where(own_seen, dot_nt(qh, keys[0]), NEGATIVE)
-        s1 = dot_nt(qh, keys[1]) + before_bias
-        peak = jnp.maximum(jnp.max(s0, axis=1, keepdims=True), jnp.max(s1, axis=1, keepdims=True))
-        w0 = jnp.exp(s0 - peak)
-        w1 = jnp.exp(s1 - peak)
-        norm = jnp.sum(w0, axis=1, keepdims=True) + jnp.sum(w1, axis=1, keepdims=True)
-        summed = dot(w0.astype(jnp.bfloat16), values[0]) + dot(w1.astype(jnp.bfloat16), values[1])
-        acc = jnp.where(mask, summed, acc)
-        stat = jnp.where(lane == head, peak, stat)
-        stat = jnp.where(lane == heads + head, norm, stat)
-    acc_ref[...] = acc
-    stat_ref[...] = stat
+    low = low_lanes(rows)
+    for half in halves():
+        split_values = [split_heads(v[:, half], low, 1.0) for v in values]
+        peaks, products = [], []
+        for head, qh in enumerate(split_heads(q[:, half], low, 0.0)):
+            s0 = jnp.where(own_seen, dot_nt(qh, keys[0][:, half]), NEGATIVE)
+            s1 = dot_nt(qh, keys[1][:, half]) + before_bias
+            peak = jnp.max(jnp.maximum(s0, s1), axis=1, keepdims=True)
+            w0 = jnp.exp(s0 - peak).astype(jnp.bfloat16)
+            w1 = jnp.exp(s1 - peak).astype(jnp.bfloat16)
+            peaks.append(peak)
+            products.append(dot(w0, split_values[0][head]) + dot(w1, split_values[1][head]))
+        acc_ref[:, half] = jnp.where(low, products[0], products[1])
+        norm_ref[:, half] = pltpu.roll(jnp.where(low, products[1], products[0]), BYTE_HEAD, 1)
+        peak_ref[:, half] = jnp.where(low, peaks[0], peaks[1])
 
 
 def near(block, own, before, w_qkv):
@@ -188,55 +203,49 @@
         out_shape=(
             jax.ShapeDtypeStruct((rows, width), jnp.bfloat16),
             jax.ShapeDtypeStruct((rows, width), jnp.float32),
-            jax.ShapeDtypeStruct((rows, steps * 128), jnp.float32),
+            jax.ShapeDtypeStruct((rows, width), jnp.float32),
+            jax.ShapeDtypeStruct((rows, width), jnp.float32),
         ),
         in_specs=[pl.BlockSpec(memory_space=pltpu.SMEM), whole, whole, weight(0), weight(1), weight(2)],
-        out_specs=(
-            pl.BlockSpec((rows, GROUP), lambda i: (0, i)),
-            pl.BlockSpec((rows, GROUP), lambda i: (0, i)),
-            pl.BlockSpec((rows, 128), lambda i: (0, i)),
-        ),
+        out_specs=(pl.BlockSpec((rows, GROUP), lambda i: (0, i)),) * 4,
         compiler_params=params("arbitrary"),
-        cost_estimate=pl.CostEstimate(
-            flops=10 * rows * width * width + 64 * rows * rows * GROUP,
-            bytes_accessed=6 * width * width + 8 * rows * width,
-            transcendentals=32 * rows * rows,
-        ),
+        cost_estimate=pl.CostEstimate(flops=10000000000, bytes_accessed=1000, transcendentals=0),
         name="near_attention",
     )(block, own, before, w_qkv, w_qkv, w_qkv)
 
 
 def far_kernel(
-    block_ref, start_ref, own_ref, far_ref, q_ref, acc_ref, stat_ref, wk_ref, wv_ref, wo_ref,
+    block_ref, start_ref, own_ref, up_ref, down_ref, q_ref, acc_ref, peak_ref, norm_ref, wk_ref, wv_ref, wo_ref,
     enc_ref, sums_ref, lead_ref, count_ref, total_ref,
 ):
     step = pl.program_id(0)
     rows = own_ref.shape[0]
-    far = far_ref[...]
+    far = jnp.concatenate([up_ref[...], down_ref[...]], axis=0)
     key = dot(far, wk_ref[...]).astype(jnp.bfloat16)
     value = dot(far, wv_ref[...]).astype(jnp.bfloat16)
-    q = q_ref[...]
-    acc = acc_ref[...]
-    stat = stat_ref[...]
     row = lax.broadcasted_iota(jnp.int32, (rows, rows), 0)
     col = lax.broadcasted_iota(jnp.int32, (rows, rows), 1)
     first = jnp.where(block_ref[0] >= 2, 0, 2 * rows)
     seen = col > row + first
-    heads = GROUP // BYTE_HEAD
-    attended = jnp.zeros((rows, GROUP), jnp.float32)
-    for head in range(heads):
-        mask = in_head((rows, GROUP), head)
-        qh = jnp.where(mask, q, jnp.zeros_like(q))
-        s = jnp.where(seen, dot_nt(qh, key), NEGATIVE)
-        peak = stat[:, head : head + 1]
-        norm = stat[:, heads + head : heads + head + 1]
-        newer = jnp.maximum(peak, jnp.max(s, axis=1, keepdims=True))
-        weight = jnp.exp(s - newer)
-        fade = jnp.exp(peak - newer)
-        norm = norm * fade + jnp.sum(weight, axis=1, keepdims=True)
-        summed = acc * fade + dot(weight.astype(jnp.bfloat16), value)
-        attended = jnp.where(mask, summed / norm, attended)
-    product = dot(attended.astype(jnp.bfloat16), wo_ref[...])
+    low = low_lanes(rows)
+    attended = []
+    for half in halves():
+        values = split_heads(value[:, half], low, 1.0)
+        peak = peak_ref[:, half]
+        peaks, products = [], []
+        for head, qh in enumerate(split_heads(q_ref[:, half], low, 0.0)):
+            s = jnp.where(seen, dot_nt(qh, key[:, half]), NEGATIVE)
+            lane = head * BYTE_HEAD
+            newer = jnp.maximum(peak[:, lane : lane + 1], jnp.max(s, axis=1, keepdims=True))
+            weight = jnp.exp(s - newer).astype(jnp.bfloat16)
+            peaks.append(newer)
+            products.append(dot(weight, values[head]))
+        fade = jnp.exp(peak - jnp.where(low, peaks[0], peaks[1]))
+        summed = acc_ref[:, half] * fade + jnp.where(low, products[0], products[1])
+        norm = pltpu.roll(jnp.where(low, products[1], products[0]), BYTE_HEAD, 1)
+        attended.append((summed / (norm_ref[:, half] * fade + norm)).astype(jnp.bfloat16))
+    attended = jnp.concatenate(attended, axis=1)
+    product = dot(attended, wo_ref[...])
 
     @pl.when(step == 0)
     def _():
@@ -266,7 +275,7 @@
         lead_ref[:, width : width + 128] = jnp.broadcast_to(counts[slots : slots + 1], (1, 128))
 
 
-def far_attend(block, start_row, own, far, q, acc, stat, w_qkv, w_out, slots):
+def far_attend(block, start_row, own, far_up, far_down, near_parts, w_qkv, w_out, slots):
     rows, width = own.shape
     steps = width // GROUP
 
@@ -290,10 +299,12 @@
             pl.BlockSpec(memory_space=pltpu.SMEM),
             full((1, rows)),
             full((rows, width)),
-            full((rows, width)),
+            full(far_up.shape),
+            full(far_down.shape),
             piece,
             piece,
-            pl.BlockSpec((rows, 128), lambda i: (0, i)),
+            piece,
+            piece,
             weight(1),
             weight(2),
             pl.BlockSpec((GROUP, width), lambda i: (i, 0)),
@@ -301,13 +312,9 @@
         out_specs=(full((rows, width)), full((slots, width)), full((1, width + 128)), full((slots, 128))),
         scratch_shapes=[pltpu.VMEM((rows, width), jnp.float32)],
         compiler_params=params("arbitrary"),
-        cost_estimate=pl.CostEstimate(
-            flops=6 * rows * width * width + 32 * rows * rows * GROUP,
-            bytes_accessed=6 * width * width + 12 * rows * width,
-            transcendentals=16 * rows * rows,
-        ),
+        cost_estimate=pl.CostEstimate(flops=20000000000, bytes_accessed=1000, transcendentals=0),
         name="far_attention",
-    )(block, start_row, own, far, q, acc, stat, w_qkv, w_qkv, w_out)
+    )(block, start_row, own, far_up, far_down, *near_parts, w_qkv, w_qkv, w_out)
 
 
 def pool_kernel(start_ref, sums_ref, count_ref, extra_ref, out_ref):
@@ -338,18 +345,19 @@
     start_row = patch_start.reshape(1, rows)
 
     before = shift(byte_states, 1)
-    far = shift(byte_states, 2)
+    far_down = down(byte_states[UP_ROWS:], 2)
+    far_up = shift(before[:UP_ROWS], 1)
+    near_parts = near(block, byte_states, before, w_qkv)
 
     packed = pack(start_row, latent_q, latent_k, latent_v)
     own = lax.all_to_all(packed, ("yh", "zh"), 0, 0, tiled=True)
     other = lax.ppermute(own[:, slots:], "yl", [(0, 1), (1, 0)])
-    q, acc, stat = near(block, byte_states, before, w_qkv)
     heads = latent_attend(side, own, other)
     returned = lax.all_to_all(heads, ("yh", "zh"), 0, 0, tiled=True)
     latent_out = unpack(start_row, returned)
 
     encoded, sums, lead, count = far_attend(
-        block, start_row, byte_states, far, q, acc, stat, w_qkv, w_out, slots
+        block, start_row, byte_states, far_up, far_down, near_parts, w_qkv, w_out, slots
     )
     extra = shift(lead, -1)
     patch_embed = pool(start_row, sums, count, extra)

time: 147 us -> 138 us (0.939)
  the two profiles are of different devices: /device:TPU:18 before, /device:TPU:50 now
where the time goes in v2:
time: 138 us; the launch traced here: 137 us
  starting transfers between devices  73.2 us (53%)
  Pallas kernels  26.9 us (19%)
  waiting for transfers between devices  25.5 us (18%)
  local copies, waits for them, and re-layouts  10.5 us (8%)
    ppermute x3, starting transfers between devices, shift(): lax.ppermute(x, SEQ, [(i, i + by) for i in range(count) if 0 <= i + by <...  27.6 us
    ppermute x1, waiting for transfers between devices, down(): lax.ppermute(x, SEQ, [(after(s, step - 1), after(s, step)) for s in sourc...  24.2 us
    all_to_all x1, starting transfers between devices, local(): own = lax.all_to_all(packed, ('yh', 'zh'), 0, 0, tiled=True)  19.7 us
    all_to_all x1, starting transfers between devices, local(): returned = lax.all_to_all(heads, ('yh', 'zh'), 0, 0, tiled=True)  16.8 us
    pallas_call x1, Pallas kernels, far_attend(): pl.pallas_call(far_kernel, grid=(steps,), out_shape=(jax.ShapeDtypeStruct...  11.4 us
    pallas_call x1, Pallas kernels, near(): pl.pallas_call(near_kernel, grid=(steps,), out_shape=(jax.ShapeDtypeStruc...  10.7 us
    unnamed x22, local copies, waits for them, and re-layouts  8.83 us
    ppermute x1, starting transfers between devices, down(): lax.ppermute(x, SEQ, [(after(s, step - 1), after(s, step)) for s in sourc...  3.8 us
  transfers between devices with their start and end apart: 8, of which 2 were waited for; matrix products, arithmetic and copies ran while one was open for 1% of the time, Pallas kernels for 18%

profile of v2, /device:TPU:50, one launch (start us, length us, event | category | flops | bytes accessed | tf_op | source)
XLA Modules:
  0.0 137.0 jit_solution(6239758775348703542)
XLA Ops:
  0.6 0.0 copy-start.2
  0.6 0.9 copy-done.2
  1.5 0.0 copy-start.3
  1.5 0.9 copy-done.3
  2.4 0.0 copy-start.4
  2.4 0.9 copy-done.4
  3.3 0.0 copy-start.5
  3.3 0.7 copy-done.5
  4.0 0.9 latent_pack.1
  4.9 19.7 %all-to-all-start = ((bf16[16,96,128]{2,1,0:T(8,128)(2,1)}), bf16[16,96,128]{2,1,0:T(8,128)(2,1)S(1)}, u32[]{:S(2)}, u32[]{:S(2)}) async-start(bf16[16,96,128]{2,1,0:T(8,128)(2,1)} %latent_pack.1), calls=%async_computation | async-start | bytes 786432 | tf_op jit(solution)/shard_map/all_to_all | solution.py:353
  24.6 5.2 %collective-permute-start = (bf16[256,1024]{1,0:T(8,128)(2,1)}, bf16[256,1024]{1,0:T(8,128)(2,1)S(1)}, u32[]{:S(2)}, u32[]{:S(2)}) collective-permute-start(bf16[256,1024]{1,0:T(8,128)(2,1)} %own_ref.3), channel_id=1, source_target_pairs={{0,1},{1,2},{2,3},{3,4},{4,5},{5,6},{6,7},{7,8},{8,9},{9,10},{10,1... | collective-permute-start | bytes 1572872 | tf_op jit(solution)/shard_map/ppermute | solution.py:24
  29.7 1.0 slice.10
  30.7 3.8 %collective-permute-start.2 = (bf16[128,1024]{1,0:T(8,128)(2,1)S(1)}, bf16[128,1024]{1,0:T(8,128)(2,1)}, u32[]{:S(2)}, u32[]{:S(2)}) collective-permute-start(bf16[128,1024]{1,0:T(8,128)(2,1)S(1)} %slice.10), channel_id=1, source_target_pairs={{0,3},{1,0},{2,1},{3,2},{4,7},{5,4},{6,5},{7,6},{8,11},{9,8},{10,9... | collective-permute-start | bytes 786440 | tf_op jit(solution)/shard_map/ppermute | solution.py:35
  34.5 24.2 %collective-permute-done.2 = bf16[128,1024]{1,0:T(8,128)(2,1)} collective-permute-done((bf16[128,1024]{1,0:T(8,128)(2,1)S(1)}, bf16[128,1024]{1,0:T(8,128)(2,1)}, u32[]{:S(2)}, u32[]{:S(2)}) %collective-permute-start.2) | collective-permute-done | bytes 262176 | tf_op jit(solution)/shard_map/ppermute | solution.py:35
  58.7 3.5 %collective-permute-start.3 = (bf16[128,1024]{1,0:T(8,128)(2,1)}, bf16[128,1024]{1,0:T(8,128)(2,1)S(1)}, u32[]{:S(2)}, u32[]{:S(2)}) collective-permute-start(bf16[128,1024]{1,0:T(8,128)(2,1)} %collective-permute-done.2), channel_id=1, source_target_pairs={{3,2},{0,3},{1,4},{2,5},{7,6},{4,7},{5,8},{6,9},{11,10},{8,11},{9,... | collective-permute-start | bytes 786440 | tf_op jit(solution)/shard_map/ppermute | solution.py:36
  62.2 0.0 collective-permute-done.before_ref
  62.2 0.7 slice.12
  62.9 14.4 %collective-permute-start.1 = (bf16[128,1024]{1,0:T(8,128)(2,1)}, bf16[128,1024]{1,0:T(8,128)(2,1)S(1)}, u32[]{:S(2)}, u32[]{:S(2)}) collective-permute-start(bf16[128,1024]{1,0:T(8,128)(2,1)} %slice.12), channel_id=1, source_target_pairs={{0,1},{1,2},{2,3},{3,4},{4,5},{5,6},{6,7},{7,8},{8,9},{9,10},{10,1... | collective-permute-start | bytes 786440 | tf_op jit(solution)/shard_map/ppermute | solution.py:24
  77.3 0.0 all-to-all-done.own_ref
  77.4 1.9 %collective-permute-start.5 = (bf16[16,64,128]{2,1,0:T(8,128)(2,1)S(1)}, bf16[16,64,128]{2,1,0:T(8,128)(2,1)S(1)}, u32[]{:S(2)}, u32[]{:S(2)}) collective-permute-start(bf16[16,64,128]{2,1,0:T(8,128)(2,1)S(1)} %slice.13), channel_id=1, source_target_pairs={{0,4},{4,0},{1,5},{5,1},{2,6},{6,2},{3,7},{7,3},{8,12},{12,8},{9,1... | collective-permute-start | bytes 786440 | tf_op jit(solution)/shard_map/ppermute | solution.py:354
  79.3 0.0 copy-start
  79.3 1.0 copy-done
  80.3 0.0 copy-start.1
  80.3 0.0 copy-start.6
  80.3 10.7 %near_attention.1 = (bf16[256,1024]{1,0:T(8,128)(2,1)S(1)}, f32[256,1024]{1,0:T(8,128)S(1)}, f32[256,1024]{1,0:T(8,128)S(1)}, f32[256,1024]{1,0:T(8,128)S(1)}) custom-call(s32[1]{0:T(128)} %bitcast.block_ref, bf16[256,1024]{1,0:T(8,128)(2,1)S(1)} %copy-done, bf16[256,1024]{1,0:T(8,128)(2,1)S(1)} %collective-permute-done.before_ref, ...), custom_call_target="tpu_custom_call" | custom-call | flops 10000000000 | bytes 1000 | tf_op jit(solution)/shard_map/near_attention/pallas_call | solution.py:200
  91.0 0.0 copy-start.7
  91.1 1.0 copy-done.7
  92.1 0.0 copy-start.9
  92.1 1.0 copy-done.9
  93.0 0.0 collective-permute-done.5.other_ref
  93.0 2.2 %latent_attend.1 = bf16[16,32,128]{2,1,0:T(8,128)(2,1)} custom-call(s32[1]{0:T(128)} %bitcast.2.side_ref, bf16[16,96,128]{2,1,0:T(8,128)(2,1)S(1)} %all-to-all-done.own_ref, bf16[16,64,128]{2,1,0:T(8,128)(2,1)S(1)} %collective-permute-done.5.other_ref), custom_call_target="tpu_custom_call" | custom-call | flops 1000 | bytes 1000 | tf_op jit(solution)/shard_map/latent_attend/pallas_call | solution.py:115
  95.3 16.8 %all-to-all-start.1 = ((bf16[16,32,128]{2,1,0:T(8,128)(2,1)}), bf16[16,32,128]{2,1,0:T(8,128)(2,1)S(1)}, u32[]{:S(2)}, u32[]{:S(2)}) async-start(bf16[16,32,128]{2,1,0:T(8,128)(2,1)} %latent_attend.1), calls=%async_computation.1 | async-start | bytes 262144 | tf_op jit(solution)/shard_map/all_to_all | solution.py:356
  112.0 0.0 collective-permute-done.3.down_ref
  112.1 0.0 collective-permute-done.1.up_ref
  112.1 0.0 copy-done.1
  112.1 0.0 copy-done.6
  112.1 0.0 copy-start.8
  112.1 1.2 copy-done.8
  113.3 0.0 copy-start.10
  113.3 1.2 copy-done.10
  114.5 11.4 %far_attention.1 = (bf16[256,1024]{1,0:T(8,128)(2,1)}, f32[32,1024]{1,0:T(8,128)S(1)}, f32[1,1152]{1,0:T(1,128)S(1)}, f32[32,128]{1,0:T(8,128)S(1)}) custom-call(s32[1]{0:T(128)} %bitcast.block_ref, s32[1,256]{1,0:T(1,128)S(1)} %bitcast.4, bf16[256,1024]{1,0:T(8,128)(2,1)S(1)} %copy-done.1, bf16[128,1024]{1,0:T(8,128)(2,1)S(1)} %collective-permute-done.1.up_ref, ...), custom_call_target="tpu_custom_call" | custom-call | flops 20000000000 | bytes 1000 | tf_op jit(solution)/shard_map/far_attention/pallas_call | solution.py:289
  126.0 8.1 %collective-permute-start.4 = (f32[1,1152]{1,0:T(1,128)S(1)}, f32[1,1152]{1,0:T(1,128)S(1)}, u32[]{:S(2)}, u32[]{:S(2)}) collective-permute-start(f32[1,1152]{1,0:T(1,128)S(1)} %get-tuple-element.18), channel_id=1, source_target_pairs={{1,0},{2,1},{3,2},{4,3},{5,4},{6,5},{7,6},{8,7},{9,8},{10,9},{11,1... | collective-permute-start | bytes 13832 | tf_op jit(solution)/shard_map/ppermute | solution.py:24
  134.0 1.3 collective-permute-done.4.extra_ref
  135.3 0.9 patch_pool.1
  136.2 0.0 all-to-all-done.1.heads_ref
  136.2 0.8 latent_unpack.1
  (1 shorter events, 0.0 us)
Async XLA Ops:
  0.6 0.9 copy-start.2
  1.5 0.9 copy-start.3
  2.4 0.9 copy-start.4
  3.3 0.7 copy-start.5
  4.9 72.4 %all-to-all-start = ((bf16[16,96,128]{2,1,0:T(8,128)(2,1)}), bf16[16,96,128]{2,1,0:T(8,128)(2,1)S(1)}, u32[]{:S(2)}, u32[]{:S(2)}) async-start(bf16[16,96,128]{2,1,0:T(8,128)(2,1)} %latent_pack.1), calls=%async_computation | async-start | bytes 786432 | tf_op jit(solution)/shard_map/all_to_all | solution.py:353
  24.6 37.6 %collective-permute-start = (bf16[256,1024]{1,0:T(8,128)(2,1)}, bf16[256,1024]{1,0:T(8,128)(2,1)S(1)}, u32[]{:S(2)}, u32[]{:S(2)}) collective-permute-start(bf16[256,1024]{1,0:T(8,128)(2,1)} %own_ref.3), channel_id=1, source_target_pairs={{0,1},{1,2},{2,3},{3,4},{4,5},{5,6},{6,7},{7,8},{8,9},{9,10},{10,1... | collective-permute-start | bytes 1572872 | tf_op jit(solution)/shard_map/ppermute | solution.py:24
  30.7 28.0 %collective-permute-start.2 = (bf16[128,1024]{1,0:T(8,128)(2,1)S(1)}, bf16[128,1024]{1,0:T(8,128)(2,1)}, u32[]{:S(2)}, u32[]{:S(2)}) collective-permute-start(bf16[128,1024]{1,0:T(8,128)(2,1)S(1)} %slice.10), channel_id=1, source_target_pairs={{0,3},{1,0},{2,1},{3,2},{4,7},{5,4},{6,5},{7,6},{8,11},{9,8},{10,9... | collective-permute-start | bytes 786440 | tf_op jit(solution)/shard_map/ppermute | solution.py:35
  58.7 53.3 %collective-permute-start.3 = (bf16[128,1024]{1,0:T(8,128)(2,1)}, bf16[128,1024]{1,0:T(8,128)(2,1)S(1)}, u32[]{:S(2)}, u32[]{:S(2)}) collective-permute-start(bf16[128,1024]{1,0:T(8,128)(2,1)} %collective-permute-done.2), channel_id=1, source_target_pairs={{3,2},{0,3},{1,4},{2,5},{7,6},{4,7},{5,8},{6,9},{11,10},{8,11},{9,... | collective-permute-start | bytes 786440 | tf_op jit(solution)/shard_map/ppermute | solution.py:36
  62.9 49.1 %collective-permute-start.1 = (bf16[128,1024]{1,0:T(8,128)(2,1)}, bf16[128,1024]{1,0:T(8,128)(2,1)S(1)}, u32[]{:S(2)}, u32[]{:S(2)}) collective-permute-start(bf16[128,1024]{1,0:T(8,128)(2,1)} %slice.12), channel_id=1, source_target_pairs={{0,1},{1,2},{2,3},{3,4},{4,5},{5,6},{6,7},{7,8},{8,9},{9,10},{10,1... | collective-permute-start | bytes 786440 | tf_op jit(solution)/shard_map/ppermute | solution.py:24
  77.4 15.7 %collective-permute-start.5 = (bf16[16,64,128]{2,1,0:T(8,128)(2,1)S(1)}, bf16[16,64,128]{2,1,0:T(8,128)(2,1)S(1)}, u32[]{:S(2)}, u32[]{:S(2)}) collective-permute-start(bf16[16,64,128]{2,1,0:T(8,128)(2,1)S(1)} %slice.13), channel_id=1, source_target_pairs={{0,4},{4,0},{1,5},{5,1},{2,6},{6,2},{3,7},{7,3},{8,12},{12,8},{9,1... | collective-permute-start | bytes 786440 | tf_op jit(solution)/shard_map/ppermute | solution.py:354
  79.3 1.0 copy-start
  80.3 31.7 %copy-start.1 = (bf16[256,1024]{1,0:T(8,128)(2,1)S(1)}, bf16[256,1024]{1,0:T(8,128)(2,1)}, u32[]{:S(2)}) copy-start(bf16[256,1024]{1,0:T(8,128)(2,1)} %own_ref.3) | copy-start | bytes 1572868
  80.3 31.7 %copy-start.6 = (s32[256]{0:T(256)S(1)}, s32[256]{0:T(256)}, u32[]{:S(2)}) copy-start(s32[256]{0:T(256)} %param.10) | copy-start | bytes 3076
  91.0 1.0 copy-start.7
  92.1 1.0 copy-start.9
  95.3 40.9 %all-to-all-start.1 = ((bf16[16,32,128]{2,1,0:T(8,128)(2,1)}), bf16[16,32,128]{2,1,0:T(8,128)(2,1)S(1)}, u32[]{:S(2)}, u32[]{:S(2)}) async-start(bf16[16,32,128]{2,1,0:T(8,128)(2,1)} %latent_attend.1), calls=%async_computation.1 | async-start | bytes 262144 | tf_op jit(solution)/shard_map/all_to_all | solution.py:356
  112.1 1.2 copy-start.8
  113.3 1.2 copy-start.10
  126.0 9.4 %collective-permute-start.4 = (f32[1,1152]{1,0:T(1,128)S(1)}, f32[1,1152]{1,0:T(1,128)S(1)}, u32[]{:S(2)}, u32[]{:S(2)}) collective-permute-start(f32[1,1152]{1,0:T(1,128)S(1)} %get-tuple-element.18), channel_id=1, source_target_pairs={{1,0},{2,1},{3,2},{4,3},{5,4},{6,5},{7,6},{8,7},{9,8},{10,9},{11,1... | collective-permute-start | bytes 13832 | tf_op jit(solution)/shard_map/ppermute | solution.py:24

commit v3 on v2

--- a/solution.py
+++ b/solution.py
@@ -14,7 +14,14 @@
 UP_ROWS = 128
 MARK = 1024.0
 SEQ = ("yh", "yl", "zh")
-VMEM_LIMIT = 48 * 1024 * 1024
+PACK_COST = 1000
+OWN_COST = 30_000_000_000
+BEFORE_COST = 10_000_000_000
+LATENT_COST = 1000
+UNPACK_COST = 1000
+FAR_COST = 30_000_000_000
+VMEM_ALL = 62 * 1024 * 1024
+VMEM_SOME = 16 * 1024 * 1024
 
 NT = (((1,), (1,)), ((), ()))
 
@@ -24,16 +31,15 @@
     return lax.ppermute(x, SEQ, [(i, i + by) for i in range(count) if 0 <= i + by < count])
 
 
-def down(x, reach):
+def down(x):
     count, ring = lax.axis_size(SEQ), lax.axis_size("zh")
 
     def after(source, steps):
         return source - source % ring + (source - steps) % ring
 
-    sources = range(count - reach)
-    for step in range(1, ring - reach):
-        x = lax.ppermute(x, SEQ, [(after(s, step - 1), after(s, step)) for s in sources])
-    return lax.ppermute(x, SEQ, [(after(s, ring - reach - 1), s + reach) for s in sources])
+    sources = range(count - 2)
+    relayed = lax.ppermute(x, SEQ, [(s, after(s, 1)) for s in sources])
+    return relayed, lax.ppermute(relayed, SEQ, [(after(s, 1), s + ring - 2) for s in sources])
 
 
 def dot(a, b):
@@ -44,10 +50,8 @@
     return lax.dot_general(a, b, NT, preferred_element_type=jnp.float32)
 
 
-def params(*semantics):
-    if semantics:
-        return pltpu.CompilerParams(vmem_limit_bytes=VMEM_LIMIT, dimension_semantics=semantics)
-    return pltpu.CompilerParams(vmem_limit_bytes=VMEM_LIMIT)
+def params(limit):
+    return pltpu.CompilerParams(vmem_limit_bytes=limit)
 
 
 def pack_kernel(start_ref, q_ref, k_ref, v_ref, out_ref):
@@ -67,8 +71,8 @@
     return pl.pallas_call(
         pack_kernel,
         out_shape=jax.ShapeDtypeStruct((width // LAT_HEAD, 3 * rows, LAT_HEAD), jnp.bfloat16),
-        compiler_params=params(),
-        cost_estimate=pl.CostEstimate(flops=1000, bytes_accessed=1000, transcendentals=0),
+        compiler_params=params(VMEM_ALL),
+        cost_estimate=pl.CostEstimate(flops=PACK_COST, bytes_accessed=1000, transcendentals=0),
         name="latent_pack",
     )(start_row, q, k, v)
 
@@ -120,8 +124,8 @@
             pl.BlockSpec(memory_space=pltpu.VMEM),
             pl.BlockSpec(memory_space=pltpu.VMEM),
         ],
-        compiler_params=params(),
-        cost_estimate=pl.CostEstimate(flops=1000, bytes_accessed=1000, transcendentals=0),
+        compiler_params=params(VMEM_SOME),
+        cost_estimate=pl.CostEstimate(flops=LATENT_COST, bytes_accessed=1000, transcendentals=0),
         name="latent_attend",
     )(side, own, other)
 
@@ -140,8 +144,8 @@
     return pl.pallas_call(
         unpack_kernel,
         out_shape=jax.ShapeDtypeStruct((rows, count * width), jnp.bfloat16),
-        compiler_params=params(),
-        cost_estimate=pl.CostEstimate(flops=1000, bytes_accessed=1000, transcendentals=0),
+        compiler_params=params(VMEM_SOME),
+        cost_estimate=pl.CostEstimate(flops=UNPACK_COST, bytes_accessed=1000, transcendentals=0),
         name="latent_unpack",
     )(start_row, heads)
 
@@ -159,59 +163,102 @@
     return jnp.where(low, x, other), jnp.where(low, other, x)
 
 
-def near_kernel(block_ref, own_ref, before_ref, wq_ref, wk_ref, wv_ref, q_ref, acc_ref, peak_ref, norm_ref):
+def own_kernel(own_ref, wq_ref, wk_ref, wv_ref, q_ref, acc_ref, peak_ref, norm_ref):
     rows = own_ref.shape[0]
     own = own_ref[...]
-    before = before_ref[...]
     q = dot(own, wq_ref[...]).astype(jnp.bfloat16)
     q = (q.astype(jnp.float32) * BYTE_HEAD ** (-0.5)).astype(jnp.bfloat16)
     q_ref[...] = q
-    keys = [dot(x, wk_ref[...]).astype(jnp.bfloat16) for x in (own, before)]
-    values = [dot(x, wv_ref[...]).astype(jnp.bfloat16) for x in (own, before)]
+    key = dot(own, wk_ref[...]).astype(jnp.bfloat16)
+    value = dot(own, wv_ref[...]).astype(jnp.bfloat16)
     row = lax.broadcasted_iota(jnp.int32, (rows, rows), 0)
     col = lax.broadcasted_iota(jnp.int32, (rows, rows), 1)
-    own_seen = col <= row
-    before_bias = jnp.where(block_ref[0] >= 1, 0.0, NEGATIVE)
+    seen = col <= row
     low = low_lanes(rows)
     for half in halves():
-        split_values = [split_heads(v[:, half], low, 1.0) for v in values]
+        values = split_heads(value[:, half], low, 1.0)
         peaks, products = [], []
         for head, qh in enumerate(split_heads(q[:, half], low, 0.0)):
-            s0 = jnp.where(own_seen, dot_nt(qh, keys[0][:, half]), NEGATIVE)
-            s1 = dot_nt(qh, keys[1][:, half]) + before_bias
-            peak = jnp.max(jnp.maximum(s0, s1), axis=1, keepdims=True)
-            w0 = jnp.exp(s0 - peak).astype(jnp.bfloat16)
-            w1 = jnp.exp(s1 - peak).astype(jnp.bfloat16)
+            s = jnp.where(seen, dot_nt(qh, key[:, half]), NEGATIVE)
+            peak = jnp.max(s, axis=1, keepdims=True)
             peaks.append(peak)
-            products.append(dot(w0, split_values[0][head]) + dot(w1, split_values[1][head]))
+            products.append(dot(jnp.exp(s - peak).astype(jnp.bfloat16), values[head]))
         acc_ref[:, half] = jnp.where(low, products[0], products[1])
         norm_ref[:, half] = pltpu.roll(jnp.where(low, products[1], products[0]), BYTE_HEAD, 1)
         peak_ref[:, half] = jnp.where(low, peaks[0], peaks[1])
 
 
-def near(block, own, before, w_qkv):
+def earlier_block(x, half, q_ref, acc_ref, peak_ref, norm_ref, key, value, seen):
+    low = low_lanes(x)
+    values = split_heads(value[:, half], low, 1.0)
+    peak = peak_ref[:, half]
+    peaks, products = [], []
+    for head, qh in enumerate(split_heads(q_ref[:, half], low, 0.0)):
+        s = jnp.where(seen, dot_nt(qh, key[:, half]), NEGATIVE)
+        lane = head * BYTE_HEAD
+        newer = jnp.maximum(peak[:, lane : lane + 1], jnp.max(s, axis=1, keepdims=True))
+        peaks.append(newer)
+        products.append(dot(jnp.exp(s - newer).astype(jnp.bfloat16), values[head]))
+    newest = jnp.where(low, peaks[0], peaks[1])
+    fade = jnp.exp(peak - newest)
+    acc = acc_ref[:, half] * fade + jnp.where(low, products[0], products[1])
+    norm = pltpu.roll(jnp.where(low, products[1], products[0]), BYTE_HEAD, 1)
+    return acc, newest, norm_ref[:, half] * fade + norm
+
+
+def before_kernel(
+    block_ref, before_ref, q_ref, acc_ref, peak_ref, norm_ref, wk_ref, wv_ref, acc_out, peak_out, norm_out
+):
+    rows = before_ref.shape[0]
+    before = before_ref[...]
+    key = dot(before, wk_ref[...]).astype(jnp.bfloat16)
+    value = dot(before, wv_ref[...]).astype(jnp.bfloat16)
+    first = jnp.where(block_ref[0] >= 1, 0, rows)
+    seen = lax.broadcasted_iota(jnp.int32, (rows, rows), 1) >= first
+    for half in halves():
+        acc, peak, norm = earlier_block(rows, half, q_ref, acc_ref, peak_ref, norm_ref, key, value, seen)
+        acc_out[:, half] = acc
+        peak_out[:, half] = peak
+        norm_out[:, half] = norm
+
+
+def weight_part(width, part):
+    steps = width // GROUP
+    return pl.BlockSpec((width, GROUP), lambda i: (0, part * steps + i))
+
+
+def own_attend(own, w_qkv):
     rows, width = own.shape
-    steps = width // GROUP
-
-    def weight(part):
-        return pl.BlockSpec((width, GROUP), lambda i: (0, part * steps + i))
-
-    whole = pl.BlockSpec((rows, width), lambda i: (0, 0))
-    return pl.pallas_call(
-        near_kernel,
-        grid=(steps,),
-        out_shape=(
-            jax.ShapeDtypeStruct((rows, width), jnp.bfloat16),
-            jax.ShapeDtypeStruct((rows, width), jnp.float32),
-            jax.ShapeDtypeStruct((rows, width), jnp.float32),
-            jax.ShapeDtypeStruct((rows, width), jnp.float32),
-        ),
-        in_specs=[pl.BlockSpec(memory_space=pltpu.SMEM), whole, whole, weight(0), weight(1), weight(2)],
-        out_specs=(pl.BlockSpec((rows, GROUP), lambda i: (0, i)),) * 4,
-        compiler_params=params("arbitrary"),
-        cost_estimate=pl.CostEstimate(flops=10000000000, bytes_accessed=1000, transcendentals=0),
-        name="near_attention",
-    )(block, own, before, w_qkv, w_qkv, w_qkv)
+    piece = pl.BlockSpec((rows, GROUP), lambda i: (0, i))
+    kept = jax.ShapeDtypeStruct((rows, width), jnp.float32)
+    return pl.pallas_call(
+        own_kernel,
+        grid=(width // GROUP,),
+        out_shape=(jax.ShapeDtypeStruct((rows, width), jnp.bfloat16), kept, kept, kept),
+        in_specs=[pl.BlockSpec((rows, width), lambda i: (0, 0))] + [weight_part(width, part) for part in range(3)],
+        out_specs=(piece,) * 4,
+        compiler_params=params(VMEM_ALL),
+        cost_estimate=pl.CostEstimate(flops=OWN_COST, bytes_accessed=1000, transcendentals=0),
+        name="own_attention",
+    )(own, w_qkv, w_qkv, w_qkv)
+
+
+def before_attend(block, before, parts, w_qkv):
+    rows, width = before.shape
+    piece = pl.BlockSpec((rows, GROUP), lambda i: (0, i))
+    kept = jax.ShapeDtypeStruct((rows, width), jnp.float32)
+    return pl.pallas_call(
+        before_kernel,
+        grid=(width // GROUP,),
+        out_shape=(kept, kept, kept),
+        in_specs=[pl.BlockSpec(memory_space=pltpu.SMEM), pl.BlockSpec((rows, width), lambda i: (0, 0))]
+        + [piece] * 4
+        + [weight_part(width, part) for part in (1, 2)],
+        out_specs=(piece,) * 3,
+        compiler_params=params(VMEM_ALL),
+        cost_estimate=pl.CostEstimate(flops=BEFORE_COST, bytes_accessed=1000, transcendentals=0),
+        name="before_attention",
+    )(block, before, *parts, w_qkv, w_qkv)
 
 
 def far_kernel(
@@ -227,23 +274,10 @@
     col = lax.broadcasted_iota(jnp.int32, (rows, rows), 1)
     first = jnp.where(block_ref[0] >= 2, 0, 2 * rows)
     seen = col > row + first
-    low = low_lanes(rows)
     attended = []
     for half in halves():
-        values = split_heads(value[:, half], low, 1.0)
-        peak = peak_ref[:, half]
-        peaks, products = [], []
-        for head, qh in enumerate(split_heads(q_ref[:, half], low, 0.0)):
-            s = jnp.where(seen, dot_nt(qh, key[:, half]), NEGATIVE)
-            lane = head * BYTE_HEAD
-            newer = jnp.maximum(peak[:, lane : lane + 1], jnp.max(s, axis=1, keepdims=True))
-            weight = jnp.exp(s - newer).astype(jnp.bfloat16)
-            peaks.append(newer)
-            products.append(dot(weight, values[head]))
-        fade = jnp.exp(peak - jnp.where(low, peaks[0], peaks[1]))
-        summed = acc_ref[:, half] * fade + jnp.where(low, products[0], products[1])
-        norm = pltpu.roll(jnp.where(low, products[1], products[0]), BYTE_HEAD, 1)
-        attended.append((summed / (norm_ref[:, half] * fade + norm)).astype(jnp.bfloat16))
+        acc, _, norm = earlier_block(rows, half, q_ref, acc_ref, peak_ref, norm_ref, key, value, seen)
+        attended.append((acc / norm).astype(jnp.bfloat16))
     attended = jnp.concatenate(attended, axis=1)
     product = dot(attended, wo_ref[...])
 
@@ -275,7 +309,7 @@
         lead_ref[:, width : width + 128] = jnp.broadcast_to(counts[slots : slots + 1], (1, 128))
 
 
-def far_attend(block, start_row, own, far_up, far_down, near_parts, w_qkv, w_out, slots):
+def far_attend(block, start_row, own, far_up, far_down, parts, w_qkv, w_out, slots):
     rows, width = own.shape
     steps = width // GROUP
 
@@ -311,10 +345,10 @@
         ],
         out_specs=(full((rows, width)), full((slots, width)), full((1, width + 128)), full((slots, 128))),
         scratch_shapes=[pltpu.VMEM((rows, width), jnp.float32)],
-        compiler_params=params("arbitrary"),
-        cost_estimate=pl.CostEstimate(flops=20000000000, bytes_accessed=1000, transcendentals=0),
+        compiler_params=params(VMEM_ALL),
+        cost_estimate=pl.CostEstimate(flops=FAR_COST, bytes_accessed=1000, transcendentals=0),
         name="far_attention",
-    )(block, start_row, own, far_up, far_down, *near_parts, w_qkv, w_qkv, w_out)
+    )(block, start_row, own, far_up, far_down, *parts, w_qkv, w_qkv, w_out)
 
 
 def pool_kernel(start_ref, sums_ref, count_ref, extra_ref, out_ref):
@@ -332,7 +366,7 @@
     return pl.pallas_call(
         pool_kernel,
         out_shape=jax.ShapeDtypeStruct(sums.shape, jnp.bfloat16),
-        compiler_params=params(),
+        compiler_params=params(VMEM_SOME),
         name="patch_pool",
     )(start_row, sums, count, extra)
 
@@ -345,9 +379,10 @@
     start_row = patch_start.reshape(1, rows)
 
     before = shift(byte_states, 1)
-    far_down = down(byte_states[UP_ROWS:], 2)
+    relayed, far_down = down(byte_states[UP_ROWS:])
     far_up = shift(before[:UP_ROWS], 1)
-    near_parts = near(block, byte_states, before, w_qkv)
+    query, *parts = own_attend(byte_states, w_qkv)
+    parts = before_attend(block, before, (query, *parts), w_qkv)
 
     packed = pack(start_row, latent_q, latent_k, latent_v)
     own = lax.all_to_all(packed, ("yh", "zh"), 0, 0, tiled=True)
@@ -357,7 +392,7 @@
     latent_out = unpack(start_row, returned)
 
     encoded, sums, lead, count = far_attend(
-        block, start_row, byte_states, far_up, far_down, near_parts, w_qkv, w_out, slots
+        block, start_row, byte_states, far_up, far_down, (query, *parts), w_qkv, w_out, slots
     )
     extra = shift(lead, -1)
     patch_embed = pool(start_row, sums, count, extra)

time: 138 us -> 128 us (0.928)
  the two profiles are of different devices: /device:TPU:50 before, /device:TPU:52 now
where the time goes in v3:
time: 128 us; the launch traced here: 127 us
  starting transfers between devices  74.7 us (58%)
  Pallas kernels  37.6 us (29%)
  waiting for transfers between devices  11.6 us (9%)
  local copies, waits for them, and re-layouts  2.65 us (2%)
    ppermute x3, starting transfers between devices, shift(): lax.ppermute(x, SEQ, [(i, i + by) for i in range(count) if 0 <= i + by <...  38.8 us
    pallas_call x1, Pallas kernels, far_attend(): pl.pallas_call(far_kernel, grid=(steps,), out_shape=(jax.ShapeDtypeStruct...  12.3 us
    all_to_all x1, starting transfers between devices, local(): own = lax.all_to_all(packed, ('yh', 'zh'), 0, 0, tiled=True)  12 us
    pallas_call x1, Pallas kernels, before_attend(): pl.pallas_call(before_kernel, grid=(width // GROUP,), out_shape=(kept, ke...  10.9 us
    all_to_all x1, waiting for transfers between devices, local(): own = lax.all_to_all(packed, ('yh', 'zh'), 0, 0, tiled=True)  9.49 us
    ppermute x1, starting transfers between devices, down(): relayed = lax.ppermute(x, SEQ, [(s, after(s, 1)) for s in sources])  8.59 us
    pallas_call x1, Pallas kernels, own_attend(): pl.pallas_call(own_kernel, grid=(width // GROUP,), out_shape=(jax.ShapeDt...  8.56 us
    ppermute x1, starting transfers between devices, down(): lax.ppermute(relayed, SEQ, [(after(s, 1), s + ring - 2) for s in sources])  6.95 us
  transfers between devices with their start and end apart: 8, of which 3 were waited for; matrix products, arithmetic and copies ran while one was open for 1% of the time, Pallas kernels for 29%

profile of v3, /device:TPU:52, one launch (start us, length us, event | category | flops | bytes accessed | tf_op | source)
XLA Modules:
  0.0 127.3 jit_solution(12599561470219740414)
XLA Ops:
  0.6 7.9 %collective-permute-start = (bf16[256,1024]{1,0:T(8,128)(2,1)}, bf16[256,1024]{1,0:T(8,128)(2,1)S(1)}, u32[]{:S(2)}, u32[]{:S(2)}) collective-permute-start(bf16[256,1024]{1,0:T(8,128)(2,1)} %own_ref.3), channel_id=1, source_target_pairs={{0,1},{1,2},{2,3},{3,4},{4,5},{5,6},{6,7},{7,8},{8,9},{9,10},{10,1... | collective-permute-start | bytes 1572872 | tf_op jit(solution)/shard_map/ppermute | solution.py:31
  8.5 1.0 slice.10
  9.5 8.6 %collective-permute-start.2 = (bf16[128,1024]{1,0:T(8,128)(2,1)S(1)}, bf16[128,1024]{1,0:T(8,128)(2,1)S(1)}, u32[]{:S(2)}, u32[]{:S(2)}) collective-permute-start(bf16[128,1024]{1,0:T(8,128)(2,1)S(1)} %slice.10), channel_id=1, source_target_pairs={{0,3},{1,0},{2,1},{3,2},{4,7},{5,4},{6,5},{7,6},{8,11},{9,8},{10,9... | collective-permute-start | bytes 786440 | tf_op jit(solution)/shard_map/ppermute | solution.py:41
  18.1 2.0 %latent_pack.1 = bf16[16,96,128]{2,1,0:T(8,128)(2,1)} custom-call(s32[1,256]{1,0:T(1,128)} %bitcast.3, bf16[32,2048]{1,0:T(8,128)(2,1)} %q_ref.1, bf16[32,2048]{1,0:T(8,128)(2,1)} %k_ref.1, bf16[32,2048]{1,0:T(8,128)(2,1)} %v_ref.1), custom_call_target="tpu_custom_call" | custom-call | flops 1000 | bytes 1000 | tf_op jit(solution)/shard_map/latent_pack/pallas_call | solution.py:71
  20.1 12.0 %all-to-all-start = ((bf16[16,96,128]{2,1,0:T(8,128)(2,1)}), bf16[16,96,128]{2,1,0:T(8,128)(2,1)S(1)}, u32[]{:S(2)}, u32[]{:S(2)}) async-start(bf16[16,96,128]{2,1,0:T(8,128)(2,1)} %latent_pack.1), calls=%async_computation | async-start | bytes 786432 | tf_op jit(solution)/shard_map/all_to_all | solution.py:388
  32.1 8.6 %own_attention.1 = (bf16[256,1024]{1,0:T(8,128)(2,1)}, f32[256,1024]{1,0:T(8,128)}, f32[256,1024]{1,0:T(8,128)}, f32[256,1024]{1,0:T(8,128)}) custom-call(bf16[256,1024]{1,0:T(8,128)(2,1)} %own_ref.3, bf16[1024,3072]{1,0:T(8,128)(2,1)} %wv_ref.5, bf16[1024,3072]{1,0:T(8,128)(2,1)} %wv_ref.5, bf16[1024,3072]{1,0:T(8,128)(2,1)} %wv_ref.5), custom_call_target="tpu_custom_call" | custom-call | flops 30000001024 | bytes 1000 | tf_op jit(solution)/shard_map/own_attention/pallas_call | solution.py:234
  40.7 0.0 collective-permute-done.2
  40.7 7.0 %collective-permute-start.3 = (bf16[128,1024]{1,0:T(8,128)(2,1)S(1)}, bf16[128,1024]{1,0:T(8,128)(2,1)}, u32[]{:S(2)}, u32[]{:S(2)}) collective-permute-start(bf16[128,1024]{1,0:T(8,128)(2,1)S(1)} %collective-permute-done.2), channel_id=1, source_target_pairs={{3,2},{0,3},{1,4},{2,5},{7,6},{4,7},{5,8},{6,9},{11,10},{8,11},{9,... | collective-permute-start | bytes 786440 | tf_op jit(solution)/shard_map/ppermute | solution.py:42
  47.6 0.6 collective-permute-done.before_ref
  48.2 0.0 copy-start.3
  48.3 22.6 %collective-permute-start.1 = (bf16[128,1024]{1,0:T(8,128)(2,1)S(1)}, bf16[128,1024]{1,0:T(8,128)(2,1)}, u32[]{:S(2)}, u32[]{:S(2)}) collective-permute-start(bf16[128,1024]{1,0:T(8,128)(2,1)S(1)} %slice.12), channel_id=1, source_target_pairs={{0,1},{1,2},{2,3},{3,4},{4,5},{5,6},{6,7},{7,8},{8,9},{9,10},{10,1... | collective-permute-start | bytes 786440 | tf_op jit(solution)/shard_map/ppermute | solution.py:31
  70.9 9.5 %all-to-all-done.own_ref = bf16[16,96,128]{2,1,0:T(8,128)(2,1)S(1)} async-done(((bf16[16,96,128]{2,1,0:T(8,128)(2,1)}), bf16[16,96,128]{2,1,0:T(8,128)(2,1)S(1)}, u32[]{:S(2)}, u32[]{:S(2)}) %all-to-all-start) | async-done | bytes 393248 | tf_op jit(solution)/shard_map/all_to_all | solution.py:388
  80.4 2.3 %collective-permute-start.5 = (bf16[16,64,128]{2,1,0:T(8,128)(2,1)S(1)}, bf16[16,64,128]{2,1,0:T(8,128)(2,1)S(1)}, u32[]{:S(2)}, u32[]{:S(2)}) collective-permute-start(bf16[16,64,128]{2,1,0:T(8,128)(2,1)S(1)} %slice.13), channel_id=1, source_target_pairs={{0,4},{4,0},{1,5},{5,1},{2,6},{6,2},{3,7},{7,3},{8,12},{12,8},{9,1... | collective-permute-start | bytes 786440 | tf_op jit(solution)/shard_map/ppermute | solution.py:389
  82.7 0.0 copy-done.3
  82.7 10.9 %before_attention.1 = (f32[256,1024]{1,0:T(8,128)}, f32[256,1024]{1,0:T(8,128)}, f32[256,1024]{1,0:T(8,128)}) custom-call(s32[1]{0:T(128)} %bitcast.block_ref, bf16[256,1024]{1,0:T(8,128)(2,1)} %copy-done.3, bf16[256,1024]{1,0:T(8,128)(2,1)} %get-tuple-element.14.q_ref, f32[256,1024]{1,0:T(8,128)} %get-tuple-element.15.acc_ref, ...), custom_call_target="tpu_custom_call" | custom-call | flops 10000000000 | bytes 1000 | tf_op jit(solution)/shard_map/before_attention/pallas_call | solution.py:250
  93.6 0.0 collective-permute-done.5.other_ref
  93.6 2.3 %latent_attend.1 = bf16[16,32,128]{2,1,0:T(8,128)(2,1)} custom-call(s32[1]{0:T(128)} %bitcast.2.side_ref, bf16[16,96,128]{2,1,0:T(8,128)(2,1)S(1)} %all-to-all-done.own_ref, bf16[16,64,128]{2,1,0:T(8,128)(2,1)S(1)} %collective-permute-done.5.other_ref), custom_call_target="tpu_custom_call" | custom-call | flops 1000 | bytes 1000 | tf_op jit(solution)/shard_map/latent_attend/pallas_call | solution.py:119
  95.9 6.0 %all-to-all-start.1 = ((bf16[16,32,128]{2,1,0:T(8,128)(2,1)}), bf16[16,32,128]{2,1,0:T(8,128)(2,1)S(1)}, u32[]{:S(2)}, u32[]{:S(2)}) async-start(bf16[16,32,128]{2,1,0:T(8,128)(2,1)} %latent_attend.1), calls=%async_computation.1 | async-start | bytes 262144 | tf_op jit(solution)/shard_map/all_to_all | solution.py:391
  101.9 0.0 collective-permute-done.3.down_ref
  101.9 0.0 collective-permute-done.1.up_ref
  101.9 0.0 copy-start.2
  101.9 12.3 %far_attention.1 = (bf16[256,1024]{1,0:T(8,128)(2,1)}, f32[32,1024]{1,0:T(8,128)}, f32[1,1152]{1,0:T(1,128)}, f32[32,128]{1,0:T(8,128)}) custom-call(s32[1]{0:T(128)} %bitcast.block_ref, s32[1,256]{1,0:T(1,128)} %bitcast.4, bf16[256,1024]{1,0:T(8,128)(2,1)} %own_ref.3, bf16[128,1024]{1,0:T(8,128)(2,1)} %collective-permute-done.1.up_ref, ...), custom_call_target="tpu_custom_call" | custom-call | flops 30000001024 | bytes 1000 | tf_op jit(solution)/shard_map/far_attention/pallas_call | solution.py:323
  114.2 8.3 %collective-permute-start.4 = (f32[1,1152]{1,0:T(1,128)}, f32[1,1152]{1,0:T(1,128)S(1)}, u32[]{:S(2)}, u32[]{:S(2)}) collective-permute-start(f32[1,1152]{1,0:T(1,128)} %get-tuple-element.24), channel_id=1, source_target_pairs={{1,0},{2,1},{3,2},{4,3},{5,4},{6,5},{7,6},{8,7},{9,8},{10,9},{11,1... | collective-permute-start | bytes 13832 | tf_op jit(solution)/shard_map/ppermute | solution.py:31
  122.5 1.5 %collective-permute-done.4.extra_ref = f32[1,1152]{1,0:T(1,128)S(1)} collective-permute-done((f32[1,1152]{1,0:T(1,128)}, f32[1,1152]{1,0:T(1,128)S(1)}, u32[]{:S(2)}, u32[]{:S(2)}) %collective-permute-start.4) | collective-permute-done | bytes 4640 | tf_op jit(solution)/shard_map/ppermute | solution.py:31
  124.1 0.0 copy-done.2
  124.1 0.0 copy-start
  124.1 0.9 copy-done
  125.0 0.0 copy-start.1
  125.0 0.7 copy-done.1
  125.7 0.9 patch_pool.1
  126.5 0.0 all-to-all-done.1.heads_ref
  126.5 0.8 latent_unpack.1
  (2 shorter events, 0.0 us)
Async XLA Ops:
  0.6 47.6 %collective-permute-start = (bf16[256,1024]{1,0:T(8,128)(2,1)}, bf16[256,1024]{1,0:T(8,128)(2,1)S(1)}, u32[]{:S(2)}, u32[]{:S(2)}) collective-permute-start(bf16[256,1024]{1,0:T(8,128)(2,1)} %own_ref.3), channel_id=1, source_target_pairs={{0,1},{1,2},{2,3},{3,4},{4,5},{5,6},{6,7},{7,8},{8,9},{9,10},{10,1... | collective-permute-start | bytes 1572872 | tf_op jit(solution)/shard_map/ppermute | solution.py:31
  9.5 31.1 %collective-permute-start.2 = (bf16[128,1024]{1,0:T(8,128)(2,1)S(1)}, bf16[128,1024]{1,0:T(8,128)(2,1)S(1)}, u32[]{:S(2)}, u32[]{:S(2)}) collective-permute-start(bf16[128,1024]{1,0:T(8,128)(2,1)S(1)} %slice.10), channel_id=1, source_target_pairs={{0,3},{1,0},{2,1},{3,2},{4,7},{5,4},{6,5},{7,6},{8,11},{9,8},{10,9... | collective-permute-start | bytes 786440 | tf_op jit(solution)/shard_map/ppermute | solution.py:41
  20.1 60.3 %all-to-all-start = ((bf16[16,96,128]{2,1,0:T(8,128)(2,1)}), bf16[16,96,128]{2,1,0:T(8,128)(2,1)S(1)}, u32[]{:S(2)}, u32[]{:S(2)}) async-start(bf16[16,96,128]{2,1,0:T(8,128)(2,1)} %latent_pack.1), calls=%async_computation | async-start | bytes 786432 | tf_op jit(solution)/shard_map/all_to_all | solution.py:388
  40.7 61.2 %collective-permute-start.3 = (bf16[128,1024]{1,0:T(8,128)(2,1)S(1)}, bf16[128,1024]{1,0:T(8,128)(2,1)}, u32[]{:S(2)}, u32[]{:S(2)}) collective-permute-start(bf16[128,1024]{1,0:T(8,128)(2,1)S(1)} %collective-permute-done.2), channel_id=1, source_target_pairs={{3,2},{0,3},{1,4},{2,5},{7,6},{4,7},{5,8},{6,9},{11,10},{8,11},{9,... | collective-permute-start | bytes 786440 | tf_op jit(solution)/shard_map/ppermute | solution.py:42
  48.2 34.5 %copy-start.3 = (bf16[256,1024]{1,0:T(8,128)(2,1)}, bf16[256,1024]{1,0:T(8,128)(2,1)S(1)}, u32[]{:S(2)}) copy-start(bf16[256,1024]{1,0:T(8,128)(2,1)S(1)} %collective-permute-done.before_ref) | copy-start | bytes 1572868
  48.3 53.6 %collective-permute-start.1 = (bf16[128,1024]{1,0:T(8,128)(2,1)S(1)}, bf16[128,1024]{1,0:T(8,128)(2,1)}, u32[]{:S(2)}, u32[]{:S(2)}) collective-permute-start(bf16[128,1024]{1,0:T(8,128)(2,1)S(1)} %slice.12), channel_id=1, source_target_pairs={{0,1},{1,2},{2,3},{3,4},{4,5},{5,6},{6,7},{7,8},{8,9},{9,10},{10,1... | collective-permute-start | bytes 786440 | tf_op jit(solution)/shard_map/ppermute | solution.py:31
  80.4 13.2 %collective-permute-start.5 = (bf16[16,64,128]{2,1,0:T(8,128)(2,1)S(1)}, bf16[16,64,128]{2,1,0:T(8,128)(2,1)S(1)}, u32[]{:S(2)}, u32[]{:S(2)}) collective-permute-start(bf16[16,64,128]{2,1,0:T(8,128)(2,1)S(1)} %slice.13), channel_id=1, source_target_pairs={{0,4},{4,0},{1,5},{5,1},{2,6},{6,2},{3,7},{7,3},{8,12},{12,8},{9,1... | collective-permute-start | bytes 786440 | tf_op jit(solution)/shard_map/ppermute | solution.py:389
  95.9 30.6 %all-to-all-start.1 = ((bf16[16,32,128]{2,1,0:T(8,128)(2,1)}), bf16[16,32,128]{2,1,0:T(8,128)(2,1)S(1)}, u32[]{:S(2)}, u32[]{:S(2)}) async-start(bf16[16,32,128]{2,1,0:T(8,128)(2,1)} %latent_attend.1), calls=%async_computation.1 | async-start | bytes 262144 | tf_op jit(solution)/shard_map/all_to_all | solution.py:391
  101.9 22.2 %copy-start.2 = (s32[256]{0:T(256)S(1)}, s32[256]{0:T(256)}, u32[]{:S(2)}) copy-start(s32[256]{0:T(256)} %param.10) | copy-start | bytes 3076
  114.2 9.8 %collective-permute-start.4 = (f32[1,1152]{1,0:T(1,128)}, f32[1,1152]{1,0:T(1,128)S(1)}, u32[]{:S(2)}, u32[]{:S(2)}) collective-permute-start(f32[1,1152]{1,0:T(1,128)} %get-tuple-element.24), channel_id=1, source_target_pairs={{1,0},{2,1},{3,2},{4,3},{5,4},{6,5},{7,6},{8,7},{9,8},{10,9},{11,1... | collective-permute-start | bytes 13832 | tf_op jit(solution)/shard_map/ppermute | solution.py:31
  124.1 0.9 copy-start
  125.0 0.7 copy-start.1

commit v4 on v3

--- a/solution.py
+++ b/solution.py
@@ -11,7 +11,7 @@
 LAT_HEAD = 128
 GROUP = 256
 NEGATIVE = -1e30
-UP_ROWS = 128
+UP_ROWS = 96
 MARK = 1024.0
 SEQ = ("yh", "yl", "zh")
 PACK_COST = 1000
@@ -128,6 +128,24 @@
         cost_estimate=pl.CostEstimate(flops=LATENT_COST, bytes_accessed=1000, transcendentals=0),
         name="latent_attend",
     )(side, own, other)
+
+
+def split_kernel(own_ref, after_ref, out_ref):
+    del after_ref
+    rows = out_ref.shape[1] // 2
+    out_ref[...] = own_ref[:, rows : 3 * rows]
+
+
+def split(own, after):
+    blocks, rows3, width = own.shape
+    return pl.pallas_call(
+        split_kernel,
+        out_shape=jax.ShapeDtypeStruct((blocks, rows3 // 3 * 2, width), jnp.bfloat16),
+        in_specs=[pl.BlockSpec(memory_space=pltpu.VMEM), pl.BlockSpec(memory_space=pl.ANY)],
+        compiler_params=params(VMEM_SOME),
+        cost_estimate=pl.CostEstimate(flops=1000, bytes_accessed=1000, transcendentals=0),
+        name="latent_split",
+    )(own, after)
 
 
 def unpack_kernel(start_ref, heads_ref, out_ref):
@@ -207,9 +225,14 @@
 
 
 def before_kernel(
-    block_ref, before_ref, q_ref, acc_ref, peak_ref, norm_ref, wk_ref, wv_ref, acc_out, peak_out, norm_out
+    block_ref, before_ref, q_ref, acc_ref, peak_ref, norm_ref, wk_ref, wv_ref, acc_out, peak_out, norm_out, up_out
 ):
     rows = before_ref.shape[0]
+
+    @pl.when(pl.program_id(0) == 0)
+    def _():
+        up_out[...] = before_ref[0:UP_ROWS]
+
     before = before_ref[...]
     key = dot(before, wk_ref[...]).astype(jnp.bfloat16)
     value = dot(before, wv_ref[...]).astype(jnp.bfloat16)
@@ -250,11 +273,11 @@
     return pl.pallas_call(
         before_kernel,
         grid=(width // GROUP,),
-        out_shape=(kept, kept, kept),
+        out_shape=(kept, kept, kept, jax.ShapeDtypeStruct((UP_ROWS, width), before.dtype)),
         in_specs=[pl.BlockSpec(memory_space=pltpu.SMEM), pl.BlockSpec((rows, width), lambda i: (0, 0))]
         + [piece] * 4
         + [weight_part(width, part) for part in (1, 2)],
-        out_specs=(piece,) * 3,
+        out_specs=(piece,) * 3 + (pl.BlockSpec((UP_ROWS, width), lambda i: (0, 0)),),
         compiler_params=params(VMEM_ALL),
         cost_estimate=pl.CostEstimate(flops=BEFORE_COST, bytes_accessed=1000, transcendentals=0),
         name="before_attention",
@@ -380,13 +403,13 @@
 
     before = shift(byte_states, 1)
     relayed, far_down = down(byte_states[UP_ROWS:])
-    far_up = shift(before[:UP_ROWS], 1)
     query, *parts = own_attend(byte_states, w_qkv)
-    parts = before_attend(block, before, (query, *parts), w_qkv)
+    *parts, up = before_attend(block, before, (query, *parts), w_qkv)
+    far_up = shift(up, 1)
 
     packed = pack(start_row, latent_q, latent_k, latent_v)
     own = lax.all_to_all(packed, ("yh", "zh"), 0, 0, tiled=True)
-    other = lax.ppermute(own[:, slots:], "yl", [(0, 1), (1, 0)])
+    other = lax.ppermute(split(own, up), "yl", [(0, 1), (1, 0)])
     heads = latent_attend(side, own, other)
     returned = lax.all_to_all(heads, ("yh", "zh"), 0, 0, tiled=True)
     latent_out = unpack(start_row, returned)

time: 128 us -> 121 us (0.945)
  starting transfers between devices: 74.7 us -> 59.7 us
  waiting for transfers between devices: 11.6 us -> 18 us
  local copies, waits for them, and re-layouts: 2.65 us -> 4.19 us
    ppermute x3, starting transfers between devices: 38.8 us -> 18 us  [shift(): lax.ppermute(x, SEQ, [(i, i + by) for i in range(count) if 0 <= i + by <...]
    ppermute x1, waiting for transfers between devices: 0.01 us -> 12.8 us  [down(): relayed = lax.ppermute(x, SEQ, [(s, after(s, 1)) for s in sources])]
    all_to_all x1, waiting for transfers between devices: 9.49 us -> 0.01 us  [local(): own = lax.all_to_all(packed, ('yh', 'zh'), 0, 0, tiled=True)]
    ppermute x1, starting transfers between devices: 6.95 us -> 10.8 us  [down(): lax.ppermute(relayed, SEQ, [(after(s, 1), s + ring - 2) for s in sources])]
    ppermute x1, waiting for transfers between devices: 0.01 us -> 3.64 us  [local(): other = lax.ppermute(split(own, up), 'yl', [(0, 1), (1, 0)])]
    all_to_all x1, starting transfers between devices: 5.98 us -> 8.3 us  [local(): returned = lax.all_to_all(heads, ('yh', 'zh'), 0, 0, tiled=True)]
    unnamed x8 -> x12, local copies, waits for them, and re-layouts: 1.63 us -> 3.18 us
  transfers between devices with their start and end apart: 8 -> 8, of which waited for: 3 -> 3; matrix products, arithmetic and copies ran while one was open for 1% -> 1% of each run, Pallas kernels for 29% -> 31%
where the time goes in v4:
time: 121 us; the launch traced here: 120 us
  starting transfers between devices  59.7 us (49%)
  Pallas kernels  37.7 us (31%)
  waiting for transfers between devices  18 us (15%)
  local copies, waits for them, and re-layouts  4.19 us (3%)
    ppermute x3, starting transfers between devices, shift(): lax.ppermute(x, SEQ, [(i, i + by) for i in range(count) if 0 <= i + by <...  18 us
    ppermute x1, waiting for transfers between devices, down(): relayed = lax.ppermute(x, SEQ, [(s, after(s, 1)) for s in sources])  12.8 us
    pallas_call x1, Pallas kernels, far_attend(): pl.pallas_call(far_kernel, grid=(steps,), out_shape=(jax.ShapeDtypeStruct...  12.3 us
    all_to_all x1, starting transfers between devices, local(): own = lax.all_to_all(packed, ('yh', 'zh'), 0, 0, tiled=True)  12 us
    pallas_call x1, Pallas kernels, before_attend(): pl.pallas_call(before_kernel, grid=(width // GROUP,), out_shape=(kept, ke...  11 us
    ppermute x1, starting transfers between devices, down(): lax.ppermute(relayed, SEQ, [(after(s, 1), s + ring - 2) for s in sources])  10.8 us
    ppermute x1, starting transfers between devices, down(): relayed = lax.ppermute(x, SEQ, [(s, after(s, 1)) for s in sources])  8.59 us
    pallas_call x1, Pallas kernels, own_attend(): pl.pallas_call(own_kernel, grid=(width // GROUP,), out_shape=(jax.ShapeDt...  8.55 us
  transfers between devices with their start and end apart: 8, of which 3 were waited for; matrix products, arithmetic and copies ran while one was open for 1% of the time, Pallas kernels for 31%

profile of v4, /device:TPU:52, one launch (start us, length us, event | category | flops | bytes accessed | tf_op | source)
XLA Modules:
  0.0 120.3 jit_solution(4306967275585501760)
XLA Ops:
  0.6 7.9 %collective-permute-start = (bf16[256,1024]{1,0:T(8,128)(2,1)}, bf16[256,1024]{1,0:T(8,128)(2,1)S(1)}, u32[]{:S(2)}, u32[]{:S(2)}) collective-permute-start(bf16[256,1024]{1,0:T(8,128)(2,1)} %own_ref.3), channel_id=1, source_target_pairs={{0,1},{1,2},{2,3},{3,4},{4,5},{5,6},{6,7},{7,8},{8,9},{9,10},{10,1... | collective-permute-start | bytes 1572872 | tf_op jit(solution)/shard_map/ppermute | solution.py:31
  8.5 1.0 slice.3
  9.5 8.6 %collective-permute-start.2 = (bf16[160,1024]{1,0:T(8,128)(2,1)S(1)}, bf16[160,1024]{1,0:T(8,128)(2,1)S(1)}, u32[]{:S(2)}, u32[]{:S(2)}) collective-permute-start(bf16[160,1024]{1,0:T(8,128)(2,1)S(1)} %slice.3), channel_id=1, source_target_pairs={{0,3},{1,0},{2,1},{3,2},{4,7},{5,4},{6,5},{7,6},{8,11},{9,8},{10,9... | collective-permute-start | bytes 983048 | tf_op jit(solution)/shard_map/ppermute | solution.py:41
  18.1 1.9 %latent_pack.1 = bf16[16,96,128]{2,1,0:T(8,128)(2,1)} custom-call(s32[1,256]{1,0:T(1,128)} %bitcast.3, bf16[32,2048]{1,0:T(8,128)(2,1)} %q_ref.1, bf16[32,2048]{1,0:T(8,128)(2,1)} %k_ref.1, bf16[32,2048]{1,0:T(8,128)(2,1)} %v_ref.1), custom_call_target="tpu_custom_call" | custom-call | flops 1000 | bytes 1000 | tf_op jit(solution)/shard_map/latent_pack/pallas_call | solution.py:71
  20.1 12.0 %all-to-all-start = ((bf16[16,96,128]{2,1,0:T(8,128)(2,1)}), bf16[16,96,128]{2,1,0:T(8,128)(2,1)S(1)}, u32[]{:S(2)}, u32[]{:S(2)}) async-start(bf16[16,96,128]{2,1,0:T(8,128)(2,1)} %latent_pack.1), calls=%async_computation | async-start | bytes 786432 | tf_op jit(solution)/shard_map/all_to_all | solution.py:411
  32.1 8.6 %own_attention.1 = (bf16[256,1024]{1,0:T(8,128)(2,1)}, f32[256,1024]{1,0:T(8,128)}, f32[256,1024]{1,0:T(8,128)}, f32[256,1024]{1,0:T(8,128)}) custom-call(bf16[256,1024]{1,0:T(8,128)(2,1)} %own_ref.3, bf16[1024,3072]{1,0:T(8,128)(2,1)} %wv_ref.5, bf16[1024,3072]{1,0:T(8,128)(2,1)} %wv_ref.5, bf16[1024,3072]{1,0:T(8,128)(2,1)} %wv_ref.5), custom_call_target="tpu_custom_call" | custom-call | flops 30000001024 | bytes 1000 | tf_op jit(solution)/shard_map/own_attention/pallas_call | solution.py:257
  40.7 12.8 %collective-permute-done.2 = bf16[160,1024]{1,0:T(8,128)(2,1)S(1)} collective-permute-done((bf16[160,1024]{1,0:T(8,128)(2,1)S(1)}, bf16[160,1024]{1,0:T(8,128)(2,1)S(1)}, u32[]{:S(2)}, u32[]{:S(2)}) %collective-permute-start.2) | collective-permute-done | bytes 327712 | tf_op jit(solution)/shard_map/ppermute | solution.py:41
  53.5 10.8 %collective-permute-start.3 = (bf16[160,1024]{1,0:T(8,128)(2,1)S(1)}, bf16[160,1024]{1,0:T(8,128)(2,1)S(1)}, u32[]{:S(2)}, u32[]{:S(2)}) collective-permute-start(bf16[160,1024]{1,0:T(8,128)(2,1)S(1)} %collective-permute-done.2), channel_id=1, source_target_pairs={{3,2},{0,3},{1,4},{2,5},{7,6},{4,7},{5,8},{6,9},{11,10},{8,11},{9,... | collective-permute-start | bytes 983048 | tf_op jit(solution)/shard_map/ppermute | solution.py:42
  64.3 0.0 collective-permute-done.before_ref
  64.3 0.0 copy-start.3
  64.3 0.8 copy-done.3
  65.1 11.0 %before_attention.1 = (f32[256,1024]{1,0:T(8,128)}, f32[256,1024]{1,0:T(8,128)}, f32[256,1024]{1,0:T(8,128)}, bf16[96,1024]{1,0:T(8,128)(2,1)}) custom-call(s32[1]{0:T(128)} %bitcast.block_ref, bf16[256,1024]{1,0:T(8,128)(2,1)} %copy-done.3, bf16[256,1024]{1,0:T(8,128)(2,1)} %get-tuple-element.15.q_ref, f32[256,1024]{1,0:T(8,128)} %get-tuple-element.16.acc_ref, ...), custom_call_target="tpu_custom_call" | custom-call | flops 10000000000 | bytes 1000 | tf_op jit(solution)/shard_map/before_attention/pallas_call | solution.py:273
  76.0 0.0 all-to-all-done.own_ref
  76.1 1.9 %collective-permute-start.5 = (bf16[16,64,128]{2,1,0:T(8,128)(2,1)S(1)}, bf16[16,64,128]{2,1,0:T(8,128)(2,1)S(1)}, u32[]{:S(2)}, u32[]{:S(2)}) collective-permute-start(bf16[16,64,128]{2,1,0:T(8,128)(2,1)S(1)} %latent_split.1), channel_id=1, source_target_pairs={{0,4},{4,0},{1,5},{5,1},{2,6},{6,2},{3,7},{7,3},{8,12},{12,8},{9,1... | collective-permute-start | bytes 786440 | tf_op jit(solution)/shard_map/ppermute | solution.py:412
  78.0 2.7 %collective-permute-start.1 = (bf16[96,1024]{1,0:T(8,128)(2,1)}, bf16[96,1024]{1,0:T(8,128)(2,1)S(1)}, u32[]{:S(2)}, u32[]{:S(2)}) collective-permute-start(bf16[96,1024]{1,0:T(8,128)(2,1)} %get-tuple-element.19.after_ref), channel_id=1, source_target_pairs={{0,1},{1,2},{2,3},{3,4},{4,5},{5,6},{6,7},{7,8},{8,9},{9,10},{10,1... | collective-permute-start | bytes 589832 | tf_op jit(solution)/shard_map/ppermute | solution.py:31
  80.7 3.6 %collective-permute-done.5.other_ref = bf16[16,64,128]{2,1,0:T(8,128)(2,1)S(1)} collective-permute-done((bf16[16,64,128]{2,1,0:T(8,128)(2,1)S(1)}, bf16[16,64,128]{2,1,0:T(8,128)(2,1)S(1)}, u32[]{:S(2)}, u32[]{:S(2)}) %collective-permute-start.5) | collective-permute-done | bytes 262176 | tf_op jit(solution)/shard_map/ppermute | solution.py:412
  84.3 2.2 %latent_attend.1 = bf16[16,32,128]{2,1,0:T(8,128)(2,1)} custom-call(s32[1]{0:T(128)} %bitcast.2.side_ref, bf16[16,96,128]{2,1,0:T(8,128)(2,1)S(1)} %all-to-all-done.own_ref, bf16[16,64,128]{2,1,0:T(8,128)(2,1)S(1)} %collective-permute-done.5.other_ref), custom_call_target="tpu_custom_call" | custom-call | flops 1000 | bytes 1000 | tf_op jit(solution)/shard_map/latent_attend/pallas_call | solution.py:119
  86.6 8.3 %all-to-all-start.1 = ((bf16[16,32,128]{2,1,0:T(8,128)(2,1)}), bf16[16,32,128]{2,1,0:T(8,128)(2,1)S(1)}, u32[]{:S(2)}, u32[]{:S(2)}) async-start(bf16[16,32,128]{2,1,0:T(8,128)(2,1)} %latent_attend.1), calls=%async_computation.1 | async-start | bytes 262144 | tf_op jit(solution)/shard_map/all_to_all | solution.py:414
  94.9 0.0 collective-permute-done.3.down_ref
  94.9 0.0 copy-start.4
  94.9 0.0 collective-permute-done.1.up_ref
  94.9 0.0 copy-start.5
  94.9 0.7 copy-done.4
  95.6 0.1 copy-done.5
  95.7 0.0 copy-start.2
  95.7 12.3 %far_attention.1 = (bf16[256,1024]{1,0:T(8,128)(2,1)}, f32[32,1024]{1,0:T(8,128)}, f32[1,1152]{1,0:T(1,128)}, f32[32,128]{1,0:T(8,128)}) custom-call(s32[1]{0:T(128)} %bitcast.block_ref, s32[1,256]{1,0:T(1,128)} %bitcast.4, bf16[256,1024]{1,0:T(8,128)(2,1)} %own_ref.3, bf16[96,1024]{1,0:T(8,128)(2,1)} %copy-done.5, bf16[160,1024]{1,0:T(8,128)(2,1)} %copy-done.4, ...), custom_call_target="tpu_custom_call" | custom-call | flops 30000001024 | bytes 1000 | tf_op jit(solution)/shard_map/far_attention/pallas_call | solution.py:346
  108.0 7.5 %collective-permute-start.4 = (f32[1,1152]{1,0:T(1,128)}, f32[1,1152]{1,0:T(1,128)S(1)}, u32[]{:S(2)}, u32[]{:S(2)}) collective-permute-start(f32[1,1152]{1,0:T(1,128)} %get-tuple-element.26), channel_id=1, source_target_pairs={{1,0},{2,1},{3,2},{4,3},{5,4},{6,5},{7,6},{8,7},{9,8},{10,9},{11,1... | collective-permute-start | bytes 13832 | tf_op jit(solution)/shard_map/ppermute | solution.py:31
  115.5 1.5 %collective-permute-done.4.extra_ref = f32[1,1152]{1,0:T(1,128)S(1)} collective-permute-done((f32[1,1152]{1,0:T(1,128)}, f32[1,1152]{1,0:T(1,128)S(1)}, u32[]{:S(2)}, u32[]{:S(2)}) %collective-permute-start.4) | collective-permute-done | bytes 4640 | tf_op jit(solution)/shard_map/ppermute | solution.py:31
  117.0 0.0 copy-done.2
  117.0 0.0 copy-start
  117.0 0.9 copy-done
  117.9 0.0 copy-start.1
  117.9 0.7 copy-done.1
  118.6 0.9 patch_pool.1
  119.5 0.0 all-to-all-done.1.heads_ref
  119.5 0.8 latent_unpack.1
  (1 shorter events, 0.0 us)
Async XLA Ops:
  0.6 63.6 %collective-permute-start = (bf16[256,1024]{1,0:T(8,128)(2,1)}, bf16[256,1024]{1,0:T(8,128)(2,1)S(1)}, u32[]{:S(2)}, u32[]{:S(2)}) collective-permute-start(bf16[256,1024]{1,0:T(8,128)(2,1)} %own_ref.3), channel_id=1, source_target_pairs={{0,1},{1,2},{2,3},{3,4},{4,5},{5,6},{6,7},{7,8},{8,9},{9,10},{10,1... | collective-permute-start | bytes 1572872 | tf_op jit(solution)/shard_map/ppermute | solution.py:31
  9.5 44.0 %collective-permute-start.2 = (bf16[160,1024]{1,0:T(8,128)(2,1)S(1)}, bf16[160,1024]{1,0:T(8,128)(2,1)S(1)}, u32[]{:S(2)}, u32[]{:S(2)}) collective-permute-start(bf16[160,1024]{1,0:T(8,128)(2,1)S(1)} %slice.3), channel_id=1, source_target_pairs={{0,3},{1,0},{2,1},{3,2},{4,7},{5,4},{6,5},{7,6},{8,11},{9,8},{10,9... | collective-permute-start | bytes 983048 | tf_op jit(solution)/shard_map/ppermute | solution.py:41
  20.1 55.9 %all-to-all-start = ((bf16[16,96,128]{2,1,0:T(8,128)(2,1)}), bf16[16,96,128]{2,1,0:T(8,128)(2,1)S(1)}, u32[]{:S(2)}, u32[]{:S(2)}) async-start(bf16[16,96,128]{2,1,0:T(8,128)(2,1)} %latent_pack.1), calls=%async_computation | async-start | bytes 786432 | tf_op jit(solution)/shard_map/all_to_all | solution.py:411
  53.5 41.4 %collective-permute-start.3 = (bf16[160,1024]{1,0:T(8,128)(2,1)S(1)}, bf16[160,1024]{1,0:T(8,128)(2,1)S(1)}, u32[]{:S(2)}, u32[]{:S(2)}) collective-permute-start(bf16[160,1024]{1,0:T(8,128)(2,1)S(1)} %collective-permute-done.2), channel_id=1, source_target_pairs={{3,2},{0,3},{1,4},{2,5},{7,6},{4,7},{5,8},{6,9},{11,10},{8,11},{9,... | collective-permute-start | bytes 983048 | tf_op jit(solution)/shard_map/ppermute | solution.py:42
  64.3 0.8 copy-start.3
  76.1 8.3 %collective-permute-start.5 = (bf16[16,64,128]{2,1,0:T(8,128)(2,1)S(1)}, bf16[16,64,128]{2,1,0:T(8,128)(2,1)S(1)}, u32[]{:S(2)}, u32[]{:S(2)}) collective-permute-start(bf16[16,64,128]{2,1,0:T(8,128)(2,1)S(1)} %latent_split.1), channel_id=1, source_target_pairs={{0,4},{4,0},{1,5},{5,1},{2,6},{6,2},{3,7},{7,3},{8,12},{12,8},{9,1... | collective-permute-start | bytes 786440 | tf_op jit(solution)/shard_map/ppermute | solution.py:412
  78.0 16.9 %collective-permute-start.1 = (bf16[96,1024]{1,0:T(8,128)(2,1)}, bf16[96,1024]{1,0:T(8,128)(2,1)S(1)}, u32[]{:S(2)}, u32[]{:S(2)}) collective-permute-start(bf16[96,1024]{1,0:T(8,128)(2,1)} %get-tuple-element.19.after_ref), channel_id=1, source_target_pairs={{0,1},{1,2},{2,3},{3,4},{4,5},{5,6},{6,7},{7,8},{8,9},{9,10},{10,1... | collective-permute-start | bytes 589832 | tf_op jit(solution)/shard_map/ppermute | solution.py:31
  86.6 32.9 %all-to-all-start.1 = ((bf16[16,32,128]{2,1,0:T(8,128)(2,1)}), bf16[16,32,128]{2,1,0:T(8,128)(2,1)S(1)}, u32[]{:S(2)}, u32[]{:S(2)}) async-start(bf16[16,32,128]{2,1,0:T(8,128)(2,1)} %latent_attend.1), calls=%async_computation.1 | async-start | bytes 262144 | tf_op jit(solution)/shard_map/all_to_all | solution.py:414
  94.9 0.7 copy-start.4
  94.9 0.8 copy-start.5
  95.7 21.3 %copy-start.2 = (s32[256]{0:T(256)S(1)}, s32[256]{0:T(256)}, u32[]{:S(2)}) copy-start(s32[256]{0:T(256)} %param.10) | copy-start | bytes 3076
  108.0 9.0 %collective-permute-start.4 = (f32[1,1152]{1,0:T(1,128)}, f32[1,1152]{1,0:T(1,128)S(1)}, u32[]{:S(2)}, u32[]{:S(2)}) collective-permute-start(f32[1,1152]{1,0:T(1,128)} %get-tuple-element.26), channel_id=1, source_target_pairs={{1,0},{2,1},{3,2},{4,3},{5,4},{6,5},{7,6},{8,7},{9,8},{10,9},{11,1... | collective-permute-start | bytes 13832 | tf_op jit(solution)/shard_map/ppermute | solution.py:31
  117.0 0.9 copy-start
  117.9 0.7 copy-start.1

commit v5 on v3

--- a/solution.py
+++ b/solution.py
@@ -11,7 +11,6 @@
 LAT_HEAD = 128
 GROUP = 256
 NEGATIVE = -1e30
-UP_ROWS = 128
 MARK = 1024.0
 SEQ = ("yh", "yl", "zh")
 PACK_COST = 1000
@@ -29,17 +28,6 @@
 def shift(x, by):
     count = lax.axis_size(SEQ)
     return lax.ppermute(x, SEQ, [(i, i + by) for i in range(count) if 0 <= i + by < count])
-
-
-def down(x):
-    count, ring = lax.axis_size(SEQ), lax.axis_size("zh")
-
-    def after(source, steps):
-        return source - source % ring + (source - steps) % ring
-
-    sources = range(count - 2)
-    relayed = lax.ppermute(x, SEQ, [(s, after(s, 1)) for s in sources])
-    return relayed, lax.ppermute(relayed, SEQ, [(after(s, 1), s + ring - 2) for s in sources])
 
 
 def dot(a, b):
@@ -262,12 +250,12 @@
 
 
 def far_kernel(
-    block_ref, start_ref, own_ref, up_ref, down_ref, q_ref, acc_ref, peak_ref, norm_ref, wk_ref, wv_ref, wo_ref,
+    block_ref, start_ref, own_ref, far_ref, q_ref, acc_ref, peak_ref, norm_ref, wk_ref, wv_ref, wo_ref,
     enc_ref, sums_ref, lead_ref, count_ref, total_ref,
 ):
     step = pl.program_id(0)
     rows = own_ref.shape[0]
-    far = jnp.concatenate([up_ref[...], down_ref[...]], axis=0)
+    far = far_ref[...]
     key = dot(far, wk_ref[...]).astype(jnp.bfloat16)
     value = dot(far, wv_ref[...]).astype(jnp.bfloat16)
     row = lax.broadcasted_iota(jnp.int32, (rows, rows), 0)
@@ -309,7 +297,7 @@
         lead_ref[:, width : width + 128] = jnp.broadcast_to(counts[slots : slots + 1], (1, 128))
 
 
-def far_attend(block, start_row, own, far_up, far_down, parts, w_qkv, w_out, slots):
+def far_attend(block, start_row, own, far, parts, w_qkv, w_out, slots):
     rows, width = own.shape
     steps = width // GROUP
 
@@ -333,8 +321,7 @@
             pl.BlockSpec(memory_space=pltpu.SMEM),
             full((1, rows)),
             full((rows, width)),
-            full(far_up.shape),
-            full(far_down.shape),
+            full((rows, width)),
             piece,
             piece,
             piece,
@@ -348,7 +335,7 @@
         compiler_params=params(VMEM_ALL),
         cost_estimate=pl.CostEstimate(flops=FAR_COST, bytes_accessed=1000, transcendentals=0),
         name="far_attention",
-    )(block, start_row, own, far_up, far_down, *parts, w_qkv, w_qkv, w_out)
+    )(block, start_row, own, far, *parts, w_qkv, w_qkv, w_out)
 
 
 def pool_kernel(start_ref, sums_ref, count_ref, extra_ref, out_ref):
@@ -379,8 +366,7 @@
     start_row = patch_start.reshape(1, rows)
 
     before = shift(byte_states, 1)
-    relayed, far_down = down(byte_states[UP_ROWS:])
-    far_up = shift(before[:UP_ROWS], 1)
+    far = shift(byte_states, 2)
     query, *parts = own_attend(byte_states, w_qkv)
     parts = before_attend(block, before, (query, *parts), w_qkv)
 
@@ -392,7 +378,7 @@
     latent_out = unpack(start_row, returned)
 
     encoded, sums, lead, count = far_attend(
-        block, start_row, byte_states, far_up, far_down, (query, *parts), w_qkv, w_out, slots
+        block, start_row, byte_states, far, (query, *parts), w_qkv, w_out, slots
     )
     extra = shift(lead, -1)
     patch_embed = pool(start_row, sums, count, extra)

time: 128 us -> 151 us (1.18)
  the two profiles are of different devices: /device:TPU:52 before, /device:TPU:54 now
where the time goes in v5:
time: 151 us
  waiting for transfers between devices  64.5 us (43%)
  starting transfers between devices  44.8 us (30%)
  Pallas kernels  37.5 us (25%)
  local copies, waits for them, and re-layouts  3.23 us (2%)
    all_to_all x1, waiting for transfers between devices, local(): own = lax.all_to_all(packed, ('yh', 'zh'), 0, 0, tiled=True)  62.9 us
    ppermute x3, starting transfers between devices, shift(): lax.ppermute(x, SEQ, [(i, i + by) for i in range(count) if 0 <= i + by <...  28.9 us
    pallas_call x1, Pallas kernels, far_attend(): pl.pallas_call(far_kernel, grid=(steps,), out_shape=(jax.ShapeDtypeStruct...  12.3 us
    pallas_call x1, Pallas kernels, before_attend(): pl.pallas_call(before_kernel, grid=(width // GROUP,), out_shape=(kept, ke...  10.9 us
    pallas_call x1, Pallas kernels, own_attend(): pl.pallas_call(own_kernel, grid=(width // GROUP,), out_shape=(jax.ShapeDt...  8.53 us
    all_to_all x1, starting transfers between devices, local(): own = lax.all_to_all(packed, ('yh', 'zh'), 0, 0, tiled=True)  7.08 us
    all_to_all x1, starting transfers between devices, local(): returned = lax.all_to_all(heads, ('yh', 'zh'), 0, 0, tiled=True)  6.37 us
    unnamed x10, local copies, waits for them, and re-layouts  3.21 us
  transfers between devices with their start and end apart: 6, of which 2 were waited for; matrix products, arithmetic and copies ran while one was open for 0% of the time, Pallas kernels for 24%

profile of v5, /device:TPU:54, one launch (start us, length us, event | category | flops | bytes accessed | tf_op | source)
XLA Modules:
  0.0 150.7 jit_solution(8496801595318936497)
XLA Ops:
  0.6 7.9 %collective-permute-start.1 = (bf16[256,1024]{1,0:T(8,128)(2,1)}, bf16[256,1024]{1,0:T(8,128)(2,1)S(1)}, u32[]{:S(2)}, u32[]{:S(2)}) collective-permute-start(bf16[256,1024]{1,0:T(8,128)(2,1)} %own_ref.3), channel_id=1, source_target_pairs={{0,1},{1,2},{2,3},{3,4},{4,5},{5,6},{6,7},{7,8},{8,9},{9,10},{10,1... | collective-permute-start | bytes 1572872 | tf_op jit(solution)/shard_map/ppermute | solution.py:30
  8.5 13.0 %collective-permute-start = (bf16[256,1024]{1,0:T(8,128)(2,1)}, bf16[256,1024]{1,0:T(8,128)(2,1)S(1)}, u32[]{:S(2)}, u32[]{:S(2)}) collective-permute-start(bf16[256,1024]{1,0:T(8,128)(2,1)} %own_ref.3), channel_id=1, source_target_pairs={{0,2},{1,3},{2,4},{3,5},{4,6},{5,7},{6,8},{7,9},{8,10},{9,11},{10,... | collective-permute-start | bytes 1572872 | tf_op jit(solution)/shard_map/ppermute | solution.py:30
  21.6 1.9 %latent_pack.1 = bf16[16,96,128]{2,1,0:T(8,128)(2,1)} custom-call(s32[1,256]{1,0:T(1,128)} %bitcast.3, bf16[32,2048]{1,0:T(8,128)(2,1)} %q_ref.1, bf16[32,2048]{1,0:T(8,128)(2,1)} %k_ref.1, bf16[32,2048]{1,0:T(8,128)(2,1)} %v_ref.1), custom_call_target="tpu_custom_call" | custom-call | flops 1000 | bytes 1000 | tf_op jit(solution)/shard_map/latent_pack/pallas_call | solution.py:59
  23.5 7.1 %all-to-all-start = ((bf16[16,96,128]{2,1,0:T(8,128)(2,1)}), bf16[16,96,128]{2,1,0:T(8,128)(2,1)S(1)}, u32[]{:S(2)}, u32[]{:S(2)}) async-start(bf16[16,96,128]{2,1,0:T(8,128)(2,1)} %latent_pack.1), calls=%async_computation | async-start | bytes 786432 | tf_op jit(solution)/shard_map/all_to_all | solution.py:374
  30.6 8.5 %own_attention.1 = (bf16[256,1024]{1,0:T(8,128)(2,1)}, f32[256,1024]{1,0:T(8,128)}, f32[256,1024]{1,0:T(8,128)}, f32[256,1024]{1,0:T(8,128)}) custom-call(bf16[256,1024]{1,0:T(8,128)(2,1)} %own_ref.3, bf16[1024,3072]{1,0:T(8,128)(2,1)} %wv_ref.5, bf16[1024,3072]{1,0:T(8,128)(2,1)} %wv_ref.5, bf16[1024,3072]{1,0:T(8,128)(2,1)} %wv_ref.5), custom_call_target="tpu_custom_call" | custom-call | flops 30000001024 | bytes 1000 | tf_op jit(solution)/shard_map/own_attention/pallas_call | solution.py:222
  39.1 62.9 %all-to-all-done.own_ref = bf16[16,96,128]{2,1,0:T(8,128)(2,1)S(1)} async-done(((bf16[16,96,128]{2,1,0:T(8,128)(2,1)}), bf16[16,96,128]{2,1,0:T(8,128)(2,1)S(1)}, u32[]{:S(2)}, u32[]{:S(2)}) %all-to-all-start) | async-done | bytes 393248 | tf_op jit(solution)/shard_map/all_to_all | solution.py:374
  102.1 2.5 %collective-permute-start.3 = (bf16[16,64,128]{2,1,0:T(8,128)(2,1)S(1)}, bf16[16,64,128]{2,1,0:T(8,128)(2,1)S(1)}, u32[]{:S(2)}, u32[]{:S(2)}) collective-permute-start(bf16[16,64,128]{2,1,0:T(8,128)(2,1)S(1)} %slice.4), channel_id=1, source_target_pairs={{0,4},{4,0},{1,5},{5,1},{2,6},{6,2},{3,7},{7,3},{8,12},{12,8},{9,1... | collective-permute-start | bytes 786440 | tf_op jit(solution)/shard_map/ppermute | solution.py:375
  104.6 0.0 collective-permute-done.1.before_ref
  104.6 0.0 copy-start.4
  104.6 0.8 copy-done.4
  105.4 10.9 %before_attention.1 = (f32[256,1024]{1,0:T(8,128)}, f32[256,1024]{1,0:T(8,128)}, f32[256,1024]{1,0:T(8,128)}) custom-call(s32[1]{0:T(128)} %bitcast.block_ref, bf16[256,1024]{1,0:T(8,128)(2,1)} %copy-done.4, bf16[256,1024]{1,0:T(8,128)(2,1)} %get-tuple-element.14.q_ref, f32[256,1024]{1,0:T(8,128)} %get-tuple-element.15.acc_ref, ...), custom_call_target="tpu_custom_call" | custom-call | flops 10000000000 | bytes 1000 | tf_op jit(solution)/shard_map/before_attention/pallas_call | solution.py:238
  116.3 0.0 collective-permute-done.3.other_ref
  116.3 2.2 %latent_attend.1 = bf16[16,32,128]{2,1,0:T(8,128)(2,1)} custom-call(s32[1]{0:T(128)} %bitcast.2.side_ref, bf16[16,96,128]{2,1,0:T(8,128)(2,1)S(1)} %all-to-all-done.own_ref, bf16[16,64,128]{2,1,0:T(8,128)(2,1)S(1)} %collective-permute-done.3.other_ref), custom_call_target="tpu_custom_call" | custom-call | flops 1000 | bytes 1000 | tf_op jit(solution)/shard_map/latent_attend/pallas_call | solution.py:107
  118.5 6.4 %all-to-all-start.1 = ((bf16[16,32,128]{2,1,0:T(8,128)(2,1)}), bf16[16,32,128]{2,1,0:T(8,128)(2,1)S(1)}, u32[]{:S(2)}, u32[]{:S(2)}) async-start(bf16[16,32,128]{2,1,0:T(8,128)(2,1)} %latent_attend.1), calls=%async_computation.1 | async-start | bytes 262144 | tf_op jit(solution)/shard_map/all_to_all | solution.py:377
  124.9 0.0 collective-permute-done.far_ref
  124.9 0.0 copy-start.3
  124.9 0.8 copy-done.3
  125.7 0.0 copy-start.2
  125.7 12.3 %far_attention.1 = (bf16[256,1024]{1,0:T(8,128)(2,1)}, f32[32,1024]{1,0:T(8,128)}, f32[1,1152]{1,0:T(1,128)}, f32[32,128]{1,0:T(8,128)}) custom-call(s32[1]{0:T(128)} %bitcast.block_ref, s32[1,256]{1,0:T(1,128)} %bitcast.4, bf16[256,1024]{1,0:T(8,128)(2,1)} %own_ref.3, bf16[256,1024]{1,0:T(8,128)(2,1)} %copy-done.3, ...), custom_call_target="tpu_custom_call" | custom-call | flops 30000001024 | bytes 1000 | tf_op jit(solution)/shard_map/far_attention/pallas_call | solution.py:311
  138.0 7.9 %collective-permute-start.2 = (f32[1,1152]{1,0:T(1,128)}, f32[1,1152]{1,0:T(1,128)S(1)}, u32[]{:S(2)}, u32[]{:S(2)}) collective-permute-start(f32[1,1152]{1,0:T(1,128)} %get-tuple-element.24), channel_id=1, source_target_pairs={{1,0},{2,1},{3,2},{4,3},{5,4},{6,5},{7,6},{8,7},{9,8},{10,9},{11,1... | collective-permute-start | bytes 13832 | tf_op jit(solution)/shard_map/ppermute | solution.py:30
  145.9 1.5 %collective-permute-done.2.extra_ref = f32[1,1152]{1,0:T(1,128)S(1)} collective-permute-done((f32[1,1152]{1,0:T(1,128)}, f32[1,1152]{1,0:T(1,128)S(1)}, u32[]{:S(2)}, u32[]{:S(2)}) %collective-permute-start.2) | collective-permute-done | bytes 4640 | tf_op jit(solution)/shard_map/ppermute | solution.py:30
  147.4 0.0 copy-done.2
  147.4 0.0 copy-start
  147.4 0.9 copy-done
  148.3 0.0 copy-start.1
  148.3 0.7 copy-done.1
  149.0 0.9 patch_pool.1
  149.9 0.0 all-to-all-done.1.heads_ref
  149.9 0.8 latent_unpack.1
  (1 shorter events, 0.0 us)
Async XLA Ops:
  0.6 104.0 %collective-permute-start.1 = (bf16[256,1024]{1,0:T(8,128)(2,1)}, bf16[256,1024]{1,0:T(8,128)(2,1)S(1)}, u32[]{:S(2)}, u32[]{:S(2)}) collective-permute-start(bf16[256,1024]{1,0:T(8,128)(2,1)} %own_ref.3), channel_id=1, source_target_pairs={{0,1},{1,2},{2,3},{3,4},{4,5},{5,6},{6,7},{7,8},{8,9},{9,10},{10,1... | collective-permute-start | bytes 1572872 | tf_op jit(solution)/shard_map/ppermute | solution.py:30
  8.5 116.3 %collective-permute-start = (bf16[256,1024]{1,0:T(8,128)(2,1)}, bf16[256,1024]{1,0:T(8,128)(2,1)S(1)}, u32[]{:S(2)}, u32[]{:S(2)}) collective-permute-start(bf16[256,1024]{1,0:T(8,128)(2,1)} %own_ref.3), channel_id=1, source_target_pairs={{0,2},{1,3},{2,4},{3,5},{4,6},{5,7},{6,8},{7,9},{8,10},{9,11},{10,... | collective-permute-start | bytes 1572872 | tf_op jit(solution)/shard_map/ppermute | solution.py:30
  23.5 78.5 %all-to-all-start = ((bf16[16,96,128]{2,1,0:T(8,128)(2,1)}), bf16[16,96,128]{2,1,0:T(8,128)(2,1)S(1)}, u32[]{:S(2)}, u32[]{:S(2)}) async-start(bf16[16,96,128]{2,1,0:T(8,128)(2,1)} %latent_pack.1), calls=%async_computation | async-start | bytes 786432 | tf_op jit(solution)/shard_map/all_to_all | solution.py:374
  102.1 14.2 %collective-permute-start.3 = (bf16[16,64,128]{2,1,0:T(8,128)(2,1)S(1)}, bf16[16,64,128]{2,1,0:T(8,128)(2,1)S(1)}, u32[]{:S(2)}, u32[]{:S(2)}) collective-permute-start(bf16[16,64,128]{2,1,0:T(8,128)(2,1)S(1)} %slice.4), channel_id=1, source_target_pairs={{0,4},{4,0},{1,5},{5,1},{2,6},{6,2},{3,7},{7,3},{8,12},{12,8},{9,1... | collective-permute-start | bytes 786440 | tf_op jit(solution)/shard_map/ppermute | solution.py:375
  104.6 0.8 copy-start.4
  118.5 31.4 %all-to-all-start.1 = ((bf16[16,32,128]{2,1,0:T(8,128)(2,1)}), bf16[16,32,128]{2,1,0:T(8,128)(2,1)S(1)}, u32[]{:S(2)}, u32[]{:S(2)}) async-start(bf16[16,32,128]{2,1,0:T(8,128)(2,1)} %latent_attend.1), calls=%async_computation.1 | async-start | bytes 262144 | tf_op jit(solution)/shard_map/all_to_all | solution.py:377
  124.9 0.8 copy-start.3
  125.7 21.7 %copy-start.2 = (s32[256]{0:T(256)S(1)}, s32[256]{0:T(256)}, u32[]{:S(2)}) copy-start(s32[256]{0:T(256)} %param.10) | copy-start | bytes 3076
  138.0 9.4 %collective-permute-start.2 = (f32[1,1152]{1,0:T(1,128)}, f32[1,1152]{1,0:T(1,128)S(1)}, u32[]{:S(2)}, u32[]{:S(2)}) collective-permute-start(f32[1,1152]{1,0:T(1,128)} %get-tuple-element.24), channel_id=1, source_target_pairs={{1,0},{2,1},{3,2},{4,3},{5,4},{6,5},{7,6},{8,7},{9,8},{10,9},{11,1... | collective-permute-start | bytes 13832 | tf_op jit(solution)/shard_map/ppermute | solution.py:30
  147.4 0.9 copy-start
  148.3 0.7 copy-start.1

commit v6 on v4

--- a/solution.py
+++ b/solution.py
@@ -11,7 +11,8 @@
 LAT_HEAD = 128
 GROUP = 256
 NEGATIVE = -1e30
-UP_ROWS = 96
+UP_ROWS = 144
+DOWN_FROM = 112
 MARK = 1024.0
 SEQ = ("yh", "yl", "zh")
 PACK_COST = 1000
@@ -31,15 +32,16 @@
     return lax.ppermute(x, SEQ, [(i, i + by) for i in range(count) if 0 <= i + by < count])
 
 
-def down(x):
+def down(x, second):
     count, ring = lax.axis_size(SEQ), lax.axis_size("zh")
 
     def after(source, steps):
         return source - source % ring + (source - steps) % ring
 
     sources = range(count - 2)
-    relayed = lax.ppermute(x, SEQ, [(s, after(s, 1)) for s in sources])
-    return relayed, lax.ppermute(relayed, SEQ, [(after(s, 1), s + ring - 2) for s in sources])
+    if second:
+        return lax.ppermute(x, SEQ, [(after(s, 1), s + ring - 2) for s in sources])
+    return lax.ppermute(x, SEQ, [(s, after(s, 1)) for s in sources])
 
 
 def dot(a, b):
@@ -225,13 +227,15 @@
 
 
 def before_kernel(
-    block_ref, before_ref, q_ref, acc_ref, peak_ref, norm_ref, wk_ref, wv_ref, acc_out, peak_out, norm_out, up_out
+    block_ref, before_ref, relayed_ref, q_ref, acc_ref, peak_ref, norm_ref, wk_ref, wv_ref,
+    acc_out, peak_out, norm_out, up_out, relayed_out,
 ):
     rows = before_ref.shape[0]
 
     @pl.when(pl.program_id(0) == 0)
     def _():
         up_out[...] = before_ref[0:UP_ROWS]
+        relayed_out[...] = relayed_ref[...]
 
     before = before_ref[...]
     key = dot(before, wk_ref[...]).astype(jnp.bfloat16)
@@ -266,22 +270,23 @@
     )(own, w_qkv, w_qkv, w_qkv)
 
 
-def before_attend(block, before, parts, w_qkv):
+def before_attend(block, before, relayed, parts, w_qkv):
     rows, width = before.shape
     piece = pl.BlockSpec((rows, GROUP), lambda i: (0, i))
     kept = jax.ShapeDtypeStruct((rows, width), jnp.float32)
     return pl.pallas_call(
         before_kernel,
         grid=(width // GROUP,),
-        out_shape=(kept, kept, kept, jax.ShapeDtypeStruct((UP_ROWS, width), before.dtype)),
-        in_specs=[pl.BlockSpec(memory_space=pltpu.SMEM), pl.BlockSpec((rows, width), lambda i: (0, 0))]
+        out_shape=(kept, kept, kept, jax.ShapeDtypeStruct((UP_ROWS, width), before.dtype), jax.ShapeDtypeStruct(relayed.shape, relayed.dtype)),
+        in_specs=[pl.BlockSpec(memory_space=pltpu.SMEM), pl.BlockSpec((rows, width), lambda i: (0, 0)), pl.BlockSpec(relayed.shape, lambda i: (0, 0))]
         + [piece] * 4
         + [weight_part(width, part) for part in (1, 2)],
-        out_specs=(piece,) * 3 + (pl.BlockSpec((UP_ROWS, width), lambda i: (0, 0)),),
+        out_specs=(piece,) * 3
+        + (pl.BlockSpec((UP_ROWS, width), lambda i: (0, 0)), pl.BlockSpec(relayed.shape, lambda i: (0, 0))),
         compiler_params=params(VMEM_ALL),
         cost_estimate=pl.CostEstimate(flops=BEFORE_COST, bytes_accessed=1000, transcendentals=0),
         name="before_attention",
-    )(block, before, *parts, w_qkv, w_qkv)
+    )(block, before, relayed, *parts, w_qkv, w_qkv)
 
 
 def far_kernel(
@@ -290,7 +295,7 @@
 ):
     step = pl.program_id(0)
     rows = own_ref.shape[0]
-    far = jnp.concatenate([up_ref[...], down_ref[...]], axis=0)
+    far = jnp.concatenate([up_ref[0 : rows // 2], down_ref[rows // 2 - DOWN_FROM :]], axis=0)
     key = dot(far, wk_ref[...]).astype(jnp.bfloat16)
     value = dot(far, wv_ref[...]).astype(jnp.bfloat16)
     row = lax.broadcasted_iota(jnp.int32, (rows, rows), 0)
@@ -402,10 +407,11 @@
     start_row = patch_start.reshape(1, rows)
 
     before = shift(byte_states, 1)
-    relayed, far_down = down(byte_states[UP_ROWS:])
+    relayed = down(byte_states[DOWN_FROM:], False)
     query, *parts = own_attend(byte_states, w_qkv)
-    *parts, up = before_attend(block, before, (query, *parts), w_qkv)
+    *parts, up, relayed = before_attend(block, before, relayed, (query, *parts), w_qkv)
     far_up = shift(up, 1)
+    far_down = down(relayed, True)
 
     packed = pack(start_row, latent_q, latent_k, latent_v)
     own = lax.all_to_all(packed, ("yh", "zh"), 0, 0, tiled=True)

time: 121 us -> 135 us (1.12)
  waiting for transfers between devices: 18 us -> 27.4 us
  starting transfers between devices: 59.7 us -> 62.7 us
    ppermute x1, waiting for transfers between devices: 3.64 us -> 15.8 us  [local(): other = lax.ppermute(split(own, up), 'yl', [(0, 1), (1, 0)])]
    ppermute x3, starting transfers between devices: 18 us -> 28.9 us  [shift(): lax.ppermute(x, SEQ, [(i, i + by) for i in range(count) if 0 <= i + by <...]
    ppermute x2, waiting for transfers between devices: 12.8 us -> 2.62 us  [the longest x1 2.62 us: down(): return lax.ppermute(x, SEQ, [(s, after(s, 1)) for s in sources])]
    ppermute x3, waiting for transfers between devices: 1.53 us -> 8.95 us  [shift(): lax.ppermute(x, SEQ, [(i, i + by) for i in range(count) if 0 <= i + by <...]
    ppermute x2, starting transfers between devices: 19.3 us -> 13 us  [the longest x1 8.59 us: down(): return lax.ppermute(x, SEQ, [(s, after(s, 1)) for s in sources])]
    all_to_all x1, starting transfers between devices: 8.3 us -> 6.77 us  [local(): returned = lax.all_to_all(heads, ('yh', 'zh'), 0, 0, tiled=True)]
    unnamed x12 -> x16, local copies, waits for them, and re-layouts: 3.18 us -> 4.19 us
  transfers between devices with their start and end apart: 8 -> 8, of which waited for: 3 -> 4; matrix products, arithmetic and copies ran while one was open for 1% -> 1% of each run, Pallas kernels for 31% -> 28%
where the time goes in v6:
time: 135 us; the launch traced here: 134 us
  starting transfers between devices  62.7 us (46%)
  Pallas kernels  38 us (28%)
  waiting for transfers between devices  27.4 us (20%)
  local copies, waits for them, and re-layouts  5.18 us (4%)
    ppermute x3, starting transfers between devices, shift(): lax.ppermute(x, SEQ, [(i, i + by) for i in range(count) if 0 <= i + by <...  28.9 us
    ppermute x1, waiting for transfers between devices, local(): other = lax.ppermute(split(own, up), 'yl', [(0, 1), (1, 0)])  15.8 us
    pallas_call x1, Pallas kernels, far_attend(): pl.pallas_call(far_kernel, grid=(steps,), out_shape=(jax.ShapeDtypeStruct...  12.3 us
    all_to_all x1, starting transfers between devices, local(): own = lax.all_to_all(packed, ('yh', 'zh'), 0, 0, tiled=True)  12 us
    pallas_call x1, Pallas kernels, before_attend(): pl.pallas_call(before_kernel, grid=(width // GROUP,), out_shape=(kept, ke...  11.3 us
    ppermute x3, waiting for transfers between devices, shift(): lax.ppermute(x, SEQ, [(i, i + by) for i in range(count) if 0 <= i + by <...  8.95 us
    ppermute x1, starting transfers between devices, down(): return lax.ppermute(x, SEQ, [(s, after(s, 1)) for s in sources])  8.59 us
    pallas_call x1, Pallas kernels, own_attend(): pl.pallas_call(own_kernel, grid=(width // GROUP,), out_shape=(jax.ShapeDt...  8.55 us
  transfers between devices with their start and end apart: 8, of which 4 were waited for; matrix products, arithmetic and copies ran while one was open for 1% of the time, Pallas kernels for 28%

profile of v6, /device:TPU:52, one launch (start us, length us, event | category | flops | bytes accessed | tf_op | source)
XLA Modules:
  0.0 133.9 jit_solution(5070146358150372872)
XLA Ops:
  0.6 7.9 %collective-permute-start = (bf16[256,1024]{1,0:T(8,128)(2,1)}, bf16[256,1024]{1,0:T(8,128)(2,1)S(1)}, u32[]{:S(2)}, u32[]{:S(2)}) collective-permute-start(bf16[256,1024]{1,0:T(8,128)(2,1)} %own_ref.3), channel_id=1, source_target_pairs={{0,1},{1,2},{2,3},{3,4},{4,5},{5,6},{6,7},{7,8},{8,9},{9,10},{10,1... | collective-permute-start | bytes 1572872 | tf_op jit(solution)/shard_map/ppermute | solution.py:32
  8.5 1.0 slice.3
  9.5 8.6 %collective-permute-start.1 = (bf16[144,1024]{1,0:T(8,128)(2,1)S(1)}, bf16[144,1024]{1,0:T(8,128)(2,1)S(1)}, u32[]{:S(2)}, u32[]{:S(2)}) collective-permute-start(bf16[144,1024]{1,0:T(8,128)(2,1)S(1)} %slice.3), channel_id=1, source_target_pairs={{0,3},{1,0},{2,1},{3,2},{4,7},{5,4},{6,5},{7,6},{8,11},{9,8},{10,9... | collective-permute-start | bytes 884744 | tf_op jit(solution)/shard_map/ppermute | solution.py:44
  18.1 1.9 %latent_pack.1 = bf16[16,96,128]{2,1,0:T(8,128)(2,1)} custom-call(s32[1,256]{1,0:T(1,128)} %bitcast.3, bf16[32,2048]{1,0:T(8,128)(2,1)} %q_ref.1, bf16[32,2048]{1,0:T(8,128)(2,1)} %k_ref.1, bf16[32,2048]{1,0:T(8,128)(2,1)} %v_ref.1), custom_call_target="tpu_custom_call" | custom-call | flops 1000 | bytes 1000 | tf_op jit(solution)/shard_map/latent_pack/pallas_call | solution.py:73
  20.1 12.0 %all-to-all-start = ((bf16[16,96,128]{2,1,0:T(8,128)(2,1)}), bf16[16,96,128]{2,1,0:T(8,128)(2,1)S(1)}, u32[]{:S(2)}, u32[]{:S(2)}) async-start(bf16[16,96,128]{2,1,0:T(8,128)(2,1)} %latent_pack.1), calls=%async_computation | async-start | bytes 786432 | tf_op jit(solution)/shard_map/all_to_all | solution.py:417
  32.1 8.5 %own_attention.1 = (bf16[256,1024]{1,0:T(8,128)(2,1)}, f32[256,1024]{1,0:T(8,128)}, f32[256,1024]{1,0:T(8,128)}, f32[256,1024]{1,0:T(8,128)}) custom-call(bf16[256,1024]{1,0:T(8,128)(2,1)} %own_ref.3, bf16[1024,3072]{1,0:T(8,128)(2,1)} %wv_ref.5, bf16[1024,3072]{1,0:T(8,128)(2,1)} %wv_ref.5, bf16[1024,3072]{1,0:T(8,128)(2,1)} %wv_ref.5), custom_call_target="tpu_custom_call" | custom-call | flops 30000001024 | bytes 1000 | tf_op jit(solution)/shard_map/own_attention/pallas_call | solution.py:261
  40.6 2.6 %collective-permute-done.1.relayed_ref = bf16[144,1024]{1,0:T(8,128)(2,1)S(1)} collective-permute-done((bf16[144,1024]{1,0:T(8,128)(2,1)S(1)}, bf16[144,1024]{1,0:T(8,128)(2,1)S(1)}, u32[]{:S(2)}, u32[]{:S(2)}) %collective-permute-start.1) | collective-permute-done | bytes 294944 | tf_op jit(solution)/shard_map/ppermute | solution.py:44
  43.3 0.0 copy-start.5
  43.3 7.4 %collective-permute-done.before_ref = bf16[256,1024]{1,0:T(8,128)(2,1)S(1)} collective-permute-done((bf16[256,1024]{1,0:T(8,128)(2,1)}, bf16[256,1024]{1,0:T(8,128)(2,1)S(1)}, u32[]{:S(2)}, u32[]{:S(2)}) %collective-permute-start) | collective-permute-done | bytes 524320 | tf_op jit(solution)/shard_map/ppermute | solution.py:32
  50.7 0.0 copy-start.4
  50.7 0.0 copy-done.5
  50.7 0.8 copy-done.4
  51.5 11.3 %before_attention.1 = (f32[256,1024]{1,0:T(8,128)}, f32[256,1024]{1,0:T(8,128)}, f32[256,1024]{1,0:T(8,128)}, bf16[144,1024]{1,0:T(8,128)(2,1)}, bf16[144,1024]{1,0:T(8,128)(2,1)}) custom-call(s32[1]{0:T(128)} %bitcast.block_ref, bf16[256,1024]{1,0:T(8,128)(2,1)} %copy-done.4, bf16[144,1024]{1,0:T(8,128)(2,1)} %copy-done.5, ...), custom_call_target="tpu_custom_call" | custom-call | flops 10000000000 | bytes 1000 | tf_op jit(solution)/shard_map/before_attention/pallas_call | solution.py:277
  62.8 11.9 %collective-permute-start.2 = (bf16[144,1024]{1,0:T(8,128)(2,1)}, bf16[144,1024]{1,0:T(8,128)(2,1)S(1)}, u32[]{:S(2)}, u32[]{:S(2)}) collective-permute-start(bf16[144,1024]{1,0:T(8,128)(2,1)} %get-tuple-element.20.after_ref), channel_id=1, source_target_pairs={{0,1},{1,2},{2,3},{3,4},{4,5},{5,6},{6,7},{7,8},{8,9},{9,10},{10,1... | collective-permute-start | bytes 884744 | tf_op jit(solution)/shard_map/ppermute | solution.py:32
  74.6 4.4 %collective-permute-start.3 = (bf16[144,1024]{1,0:T(8,128)(2,1)}, bf16[144,1024]{1,0:T(8,128)(2,1)S(1)}, u32[]{:S(2)}, u32[]{:S(2)}) collective-permute-start(bf16[144,1024]{1,0:T(8,128)(2,1)} %get-tuple-element.21), channel_id=1, source_target_pairs={{3,2},{0,3},{1,4},{2,5},{7,6},{4,7},{5,8},{6,9},{11,10},{8,11},{9,... | collective-permute-start | bytes 884744 | tf_op jit(solution)/shard_map/ppermute | solution.py:43
  79.0 0.0 all-to-all-done.own_ref
  79.0 0.0 copy-start
  79.0 1.0 copy-done
  80.0 1.9 %collective-permute-start.5 = (bf16[16,64,128]{2,1,0:T(8,128)(2,1)S(1)}, bf16[16,64,128]{2,1,0:T(8,128)(2,1)S(1)}, u32[]{:S(2)}, u32[]{:S(2)}) collective-permute-start(bf16[16,64,128]{2,1,0:T(8,128)(2,1)S(1)} %latent_split.1), channel_id=1, source_target_pairs={{0,4},{4,0},{1,5},{5,1},{2,6},{6,2},{3,7},{7,3},{8,12},{12,8},{9,1... | collective-permute-start | bytes 786440 | tf_op jit(solution)/shard_map/ppermute | solution.py:418
  81.9 15.8 %collective-permute-done.5.other_ref = bf16[16,64,128]{2,1,0:T(8,128)(2,1)S(1)} collective-permute-done((bf16[16,64,128]{2,1,0:T(8,128)(2,1)S(1)}, bf16[16,64,128]{2,1,0:T(8,128)(2,1)S(1)}, u32[]{:S(2)}, u32[]{:S(2)}) %collective-permute-start.5) | collective-permute-done | bytes 262176 | tf_op jit(solution)/shard_map/ppermute | solution.py:418
  97.7 2.2 %latent_attend.1 = bf16[16,32,128]{2,1,0:T(8,128)(2,1)} custom-call(s32[1]{0:T(128)} %bitcast.2.side_ref, bf16[16,96,128]{2,1,0:T(8,128)(2,1)S(1)} %all-to-all-done.own_ref, bf16[16,64,128]{2,1,0:T(8,128)(2,1)S(1)} %collective-permute-done.5.other_ref), custom_call_target="tpu_custom_call" | custom-call | flops 1000 | bytes 1000 | tf_op jit(solution)/shard_map/latent_attend/pallas_call | solution.py:121
  100.0 6.8 %all-to-all-start.1 = ((bf16[16,32,128]{2,1,0:T(8,128)(2,1)}), bf16[16,32,128]{2,1,0:T(8,128)(2,1)S(1)}, u32[]{:S(2)}, u32[]{:S(2)}) async-start(bf16[16,32,128]{2,1,0:T(8,128)(2,1)} %latent_attend.1), calls=%async_computation.1 | async-start | bytes 262144 | tf_op jit(solution)/shard_map/all_to_all | solution.py:420
  106.7 0.0 collective-permute-done.2.up_ref
  106.7 0.0 copy-start.6
  106.8 0.0 collective-permute-done.3.down_ref
  106.8 0.0 copy-start.7
  106.8 0.7 copy-done.6
  107.5 0.1 copy-done.7
  107.6 0.0 copy-start.3
  107.6 12.3 %far_attention.1 = (bf16[256,1024]{1,0:T(8,128)(2,1)}, f32[32,1024]{1,0:T(8,128)}, f32[1,1152]{1,0:T(1,128)}, f32[32,128]{1,0:T(8,128)}) custom-call(s32[1]{0:T(128)} %bitcast.block_ref, s32[1,256]{1,0:T(1,128)} %bitcast.4, bf16[256,1024]{1,0:T(8,128)(2,1)} %own_ref.3, bf16[144,1024]{1,0:T(8,128)(2,1)} %copy-done.6, bf16[144,1024]{1,0:T(8,128)(2,1)} %copy-done.7, ...), custom_call_target="tpu_custom_call" | custom-call | flops 30000001024 | bytes 1000 | tf_op jit(solution)/shard_map/far_attention/pallas_call | solution.py:351
  119.9 9.2 %collective-permute-start.4 = (f32[1,1152]{1,0:T(1,128)}, f32[1,1152]{1,0:T(1,128)S(1)}, u32[]{:S(2)}, u32[]{:S(2)}) collective-permute-start(f32[1,1152]{1,0:T(1,128)} %get-tuple-element.28), channel_id=1, source_target_pairs={{1,0},{2,1},{3,2},{4,3},{5,4},{6,5},{7,6},{8,7},{9,8},{10,9},{11,1... | collective-permute-start | bytes 13832 | tf_op jit(solution)/shard_map/ppermute | solution.py:32
  129.1 1.5 %collective-permute-done.4.extra_ref = f32[1,1152]{1,0:T(1,128)S(1)} collective-permute-done((f32[1,1152]{1,0:T(1,128)}, f32[1,1152]{1,0:T(1,128)S(1)}, u32[]{:S(2)}, u32[]{:S(2)}) %collective-permute-start.4) | collective-permute-done | bytes 4640 | tf_op jit(solution)/shard_map/ppermute | solution.py:32
  130.6 0.0 copy-done.3
  130.6 0.0 copy-start.1
  130.6 0.9 copy-done.1
  131.5 0.0 copy-start.2
  131.5 0.7 copy-done.2
  132.3 0.9 patch_pool.1
  133.1 0.0 all-to-all-done.1.heads_ref
  133.1 0.8 latent_unpack.1
  (1 shorter events, 0.0 us)
Async XLA Ops:
  0.6 50.1 %collective-permute-start = (bf16[256,1024]{1,0:T(8,128)(2,1)}, bf16[256,1024]{1,0:T(8,128)(2,1)S(1)}, u32[]{:S(2)}, u32[]{:S(2)}) collective-permute-start(bf16[256,1024]{1,0:T(8,128)(2,1)} %own_ref.3), channel_id=1, source_target_pairs={{0,1},{1,2},{2,3},{3,4},{4,5},{5,6},{6,7},{7,8},{8,9},{9,10},{10,1... | collective-permute-start | bytes 1572872 | tf_op jit(solution)/shard_map/ppermute | solution.py:32
  9.5 33.7 %collective-permute-start.1 = (bf16[144,1024]{1,0:T(8,128)(2,1)S(1)}, bf16[144,1024]{1,0:T(8,128)(2,1)S(1)}, u32[]{:S(2)}, u32[]{:S(2)}) collective-permute-start(bf16[144,1024]{1,0:T(8,128)(2,1)S(1)} %slice.3), channel_id=1, source_target_pairs={{0,3},{1,0},{2,1},{3,2},{4,7},{5,4},{6,5},{7,6},{8,11},{9,8},{10,9... | collective-permute-start | bytes 884744 | tf_op jit(solution)/shard_map/ppermute | solution.py:44
  20.1 58.9 %all-to-all-start = ((bf16[16,96,128]{2,1,0:T(8,128)(2,1)}), bf16[16,96,128]{2,1,0:T(8,128)(2,1)S(1)}, u32[]{:S(2)}, u32[]{:S(2)}) async-start(bf16[16,96,128]{2,1,0:T(8,128)(2,1)} %latent_pack.1), calls=%async_computation | async-start | bytes 786432 | tf_op jit(solution)/shard_map/all_to_all | solution.py:417
  43.3 7.4 %copy-start.5 = (bf16[144,1024]{1,0:T(8,128)(2,1)}, bf16[144,1024]{1,0:T(8,128)(2,1)S(1)}, u32[]{:S(2)}) copy-start(bf16[144,1024]{1,0:T(8,128)(2,1)S(1)} %collective-permute-done.1.relayed_ref) | copy-start | bytes 884740
  50.7 0.8 copy-start.4
  62.8 44.0 %collective-permute-start.2 = (bf16[144,1024]{1,0:T(8,128)(2,1)}, bf16[144,1024]{1,0:T(8,128)(2,1)S(1)}, u32[]{:S(2)}, u32[]{:S(2)}) collective-permute-start(bf16[144,1024]{1,0:T(8,128)(2,1)} %get-tuple-element.20.after_ref), channel_id=1, source_target_pairs={{0,1},{1,2},{2,3},{3,4},{4,5},{5,6},{6,7},{7,8},{8,9},{9,10},{10,1... | collective-permute-start | bytes 884744 | tf_op jit(solution)/shard_map/ppermute | solution.py:32
  74.6 32.1 %collective-permute-start.3 = (bf16[144,1024]{1,0:T(8,128)(2,1)}, bf16[144,1024]{1,0:T(8,128)(2,1)S(1)}, u32[]{:S(2)}, u32[]{:S(2)}) collective-permute-start(bf16[144,1024]{1,0:T(8,128)(2,1)} %get-tuple-element.21), channel_id=1, source_target_pairs={{3,2},{0,3},{1,4},{2,5},{7,6},{4,7},{5,8},{6,9},{11,10},{8,11},{9,... | collective-permute-start | bytes 884744 | tf_op jit(solution)/shard_map/ppermute | solution.py:43
  79.0 1.0 copy-start
  80.0 17.7 %collective-permute-start.5 = (bf16[16,64,128]{2,1,0:T(8,128)(2,1)S(1)}, bf16[16,64,128]{2,1,0:T(8,128)(2,1)S(1)}, u32[]{:S(2)}, u32[]{:S(2)}) collective-permute-start(bf16[16,64,128]{2,1,0:T(8,128)(2,1)S(1)} %latent_split.1), channel_id=1, source_target_pairs={{0,4},{4,0},{1,5},{5,1},{2,6},{6,2},{3,7},{7,3},{8,12},{12,8},{9,1... | collective-permute-start | bytes 786440 | tf_op jit(solution)/shard_map/ppermute | solution.py:418
  100.0 33.2 %all-to-all-start.1 = ((bf16[16,32,128]{2,1,0:T(8,128)(2,1)}), bf16[16,32,128]{2,1,0:T(8,128)(2,1)S(1)}, u32[]{:S(2)}, u32[]{:S(2)}) async-start(bf16[16,32,128]{2,1,0:T(8,128)(2,1)} %latent_attend.1), calls=%async_computation.1 | async-start | bytes 262144 | tf_op jit(solution)/shard_map/all_to_all | solution.py:420
  106.7 0.7 copy-start.6
  106.8 0.8 copy-start.7
  107.6 23.1 %copy-start.3 = (s32[256]{0:T(256)S(1)}, s32[256]{0:T(256)}, u32[]{:S(2)}) copy-start(s32[256]{0:T(256)} %param.10) | copy-start | bytes 3076
  119.9 10.7 %collective-permute-start.4 = (f32[1,1152]{1,0:T(1,128)}, f32[1,1152]{1,0:T(1,128)S(1)}, u32[]{:S(2)}, u32[]{:S(2)}) collective-permute-start(f32[1,1152]{1,0:T(1,128)} %get-tuple-element.28), channel_id=1, source_target_pairs={{1,0},{2,1},{3,2},{4,3},{5,4},{6,5},{7,6},{8,7},{9,8},{10,9},{11,1... | collective-permute-start | bytes 13832 | tf_op jit(solution)/shard_map/ppermute | solution.py:32
  130.6 0.9 copy-start.1
  131.5 0.7 copy-start.2

commit v7 on v3

--- a/solution.py
+++ b/solution.py
@@ -11,7 +11,7 @@
 LAT_HEAD = 128
 GROUP = 256
 NEGATIVE = -1e30
-UP_ROWS = 128
+UP_ROWS = 112
 MARK = 1024.0
 SEQ = ("yh", "yl", "zh")
 PACK_COST = 1000
@@ -77,7 +77,8 @@
     )(start_row, q, k, v)
 
 
-def latent_kernel(side_ref, own_ref, other_ref, out_ref):
+def latent_kernel(side_ref, own_ref, other_ref, after_ref, out_ref):
+    del after_ref
     blocks, rows3, _ = own_ref.shape
     rows = rows3 // 3
     total = blocks * rows
@@ -112,7 +113,7 @@
     out_ref[...] = (summed / norm).astype(jnp.bfloat16).reshape(blocks, rows, LAT_HEAD)
 
 
-def latent_attend(side, own, other):
+def latent_attend(side, own, other, after):
     blocks, rows3, width = own.shape
     rows = rows3 // 3
     total = blocks * rows
@@ -123,11 +124,12 @@
             pl.BlockSpec(memory_space=pltpu.SMEM),
             pl.BlockSpec(memory_space=pltpu.VMEM),
             pl.BlockSpec(memory_space=pltpu.VMEM),
+            pl.BlockSpec(memory_space=pl.ANY),
         ],
         compiler_params=params(VMEM_SOME),
         cost_estimate=pl.CostEstimate(flops=LATENT_COST, bytes_accessed=1000, transcendentals=0),
         name="latent_attend",
-    )(side, own, other)
+    )(side, own, other, after)
 
 
 def unpack_kernel(start_ref, heads_ref, out_ref):
@@ -207,9 +209,14 @@
 
 
 def before_kernel(
-    block_ref, before_ref, q_ref, acc_ref, peak_ref, norm_ref, wk_ref, wv_ref, acc_out, peak_out, norm_out
+    block_ref, before_ref, q_ref, acc_ref, peak_ref, norm_ref, wk_ref, wv_ref, acc_out, peak_out, norm_out, up_out
 ):
     rows = before_ref.shape[0]
+
+    @pl.when(pl.program_id(0) == 0)
+    def _():
+        up_out[...] = before_ref[0:UP_ROWS]
+
     before = before_ref[...]
     key = dot(before, wk_ref[...]).astype(jnp.bfloat16)
     value = dot(before, wv_ref[...]).astype(jnp.bfloat16)
@@ -250,11 +257,11 @@
     return pl.pallas_call(
         before_kernel,
         grid=(width // GROUP,),
-        out_shape=(kept, kept, kept),
+        out_shape=(kept, kept, kept, jax.ShapeDtypeStruct((UP_ROWS, width), before.dtype)),
         in_specs=[pl.BlockSpec(memory_space=pltpu.SMEM), pl.BlockSpec((rows, width), lambda i: (0, 0))]
         + [piece] * 4
         + [weight_part(width, part) for part in (1, 2)],
-        out_specs=(piece,) * 3,
+        out_specs=(piece,) * 3 + (pl.BlockSpec((UP_ROWS, width), lambda i: (0, 0)),),
         compiler_params=params(VMEM_ALL),
         cost_estimate=pl.CostEstimate(flops=BEFORE_COST, bytes_accessed=1000, transcendentals=0),
         name="before_attention",
@@ -380,21 +387,20 @@
 
     before = shift(byte_states, 1)
     relayed, far_down = down(byte_states[UP_ROWS:])
-    far_up = shift(before[:UP_ROWS], 1)
     query, *parts = own_attend(byte_states, w_qkv)
-    parts = before_attend(block, before, (query, *parts), w_qkv)
+    *parts, up = before_attend(block, before, (query, *parts), w_qkv)
+    far_up = shift(up, 1)
 
     packed = pack(start_row, latent_q, latent_k, latent_v)
     own = lax.all_to_all(packed, ("yh", "zh"), 0, 0, tiled=True)
     other = lax.ppermute(own[:, slots:], "yl", [(0, 1), (1, 0)])
-    heads = latent_attend(side, own, other)
-    returned = lax.all_to_all(heads, ("yh", "zh"), 0, 0, tiled=True)
-    latent_out = unpack(start_row, returned)
-
     encoded, sums, lead, count = far_attend(
         block, start_row, byte_states, far_up, far_down, (query, *parts), w_qkv, w_out, slots
     )
     extra = shift(lead, -1)
+    heads = latent_attend(side, own, other, count)
+    returned = lax.all_to_all(heads, ("yh", "zh"), 0, 0, tiled=True)
+    latent_out = unpack(start_row, returned)
     patch_embed = pool(start_row, sums, count, extra)
     return encoded, patch_embed, latent_out
 

time: 128 us -> 131 us (1.023)
  the two profiles are of different devices: /device:TPU:52 before, /device:TPU:14 now
where the time goes in v7:
time: 131 us; the launch traced here: 130 us
  starting transfers between devices  66.1 us (50%)
  Pallas kernels  37.7 us (29%)
  waiting for transfers between devices  20.5 us (16%)
  local copies, waits for them, and re-layouts  4.82 us (4%)
    ppermute x3, starting transfers between devices, shift(): lax.ppermute(x, SEQ, [(i, i + by) for i in range(count) if 0 <= i + by <...  19.5 us
    all_to_all x1, starting transfers between devices, local(): returned = lax.all_to_all(heads, ('yh', 'zh'), 0, 0, tiled=True)  14.2 us
    pallas_call x1, Pallas kernels, far_attend(): pl.pallas_call(far_kernel, grid=(steps,), out_shape=(jax.ShapeDtypeStruct...  12.3 us
    all_to_all x1, starting transfers between devices, local(): own = lax.all_to_all(packed, ('yh', 'zh'), 0, 0, tiled=True)  11.3 us
    pallas_call x1, Pallas kernels, before_attend(): pl.pallas_call(before_kernel, grid=(width // GROUP,), out_shape=(kept, ke...  11 us
    ppermute x1, starting transfers between devices, down(): lax.ppermute(relayed, SEQ, [(after(s, 1), s + ring - 2) for s in sources])  9.92 us
    ppermute x3, waiting for transfers between devices, shift(): lax.ppermute(x, SEQ, [(i, i + by) for i in range(count) if 0 <= i + by <...  8.65 us
    ppermute x1, starting transfers between devices, down(): relayed = lax.ppermute(x, SEQ, [(s, after(s, 1)) for s in sources])  8.59 us
  transfers between devices with their start and end apart: 8, of which 4 were waited for; matrix products, arithmetic and copies ran while one was open for 1% of the time, Pallas kernels for 27%

profile of v7, /device:TPU:14, one launch (start us, length us, event | category | flops | bytes accessed | tf_op | source)
XLA Modules:
  0.0 129.8 jit_solution(1722451798452114328)
XLA Ops:
  0.6 7.9 %collective-permute-start = (bf16[256,1024]{1,0:T(8,128)(2,1)}, bf16[256,1024]{1,0:T(8,128)(2,1)S(1)}, u32[]{:S(2)}, u32[]{:S(2)}) collective-permute-start(bf16[256,1024]{1,0:T(8,128)(2,1)} %own_ref.3), channel_id=1, source_target_pairs={{0,1},{1,2},{2,3},{3,4},{4,5},{5,6},{6,7},{7,8},{8,9},{9,10},{10,1... | collective-permute-start | bytes 1572872 | tf_op jit(solution)/shard_map/ppermute | solution.py:31
  8.5 1.0 slice.6
  9.5 8.6 %collective-permute-start.2 = (bf16[144,1024]{1,0:T(8,128)(2,1)S(1)}, bf16[144,1024]{1,0:T(8,128)(2,1)S(1)}, u32[]{:S(2)}, u32[]{:S(2)}) collective-permute-start(bf16[144,1024]{1,0:T(8,128)(2,1)S(1)} %slice.6), channel_id=1, source_target_pairs={{0,3},{1,0},{2,1},{3,2},{4,7},{5,4},{6,5},{7,6},{8,11},{9,8},{10,9... | collective-permute-start | bytes 884744 | tf_op jit(solution)/shard_map/ppermute | solution.py:41
  18.1 1.9 %latent_pack.1 = bf16[16,96,128]{2,1,0:T(8,128)(2,1)} custom-call(s32[1,256]{1,0:T(1,128)} %bitcast.3, bf16[32,2048]{1,0:T(8,128)(2,1)} %q_ref.1, bf16[32,2048]{1,0:T(8,128)(2,1)} %k_ref.1, bf16[32,2048]{1,0:T(8,128)(2,1)} %v_ref.1), custom_call_target="tpu_custom_call" | custom-call | flops 1000 | bytes 1000 | tf_op jit(solution)/shard_map/latent_pack/pallas_call | solution.py:71
  20.1 11.3 %all-to-all-start = ((bf16[16,96,128]{2,1,0:T(8,128)(2,1)}), bf16[16,96,128]{2,1,0:T(8,128)(2,1)S(1)}, u32[]{:S(2)}, u32[]{:S(2)}) async-start(bf16[16,96,128]{2,1,0:T(8,128)(2,1)} %latent_pack.1), calls=%async_computation | async-start | bytes 786432 | tf_op jit(solution)/shard_map/all_to_all | solution.py:395
  31.4 8.6 %own_attention.1 = (bf16[256,1024]{1,0:T(8,128)(2,1)}, f32[256,1024]{1,0:T(8,128)}, f32[256,1024]{1,0:T(8,128)}, f32[256,1024]{1,0:T(8,128)}) custom-call(bf16[256,1024]{1,0:T(8,128)(2,1)} %own_ref.3, bf16[1024,3072]{1,0:T(8,128)(2,1)} %wv_ref.5, bf16[1024,3072]{1,0:T(8,128)(2,1)} %wv_ref.5, bf16[1024,3072]{1,0:T(8,128)(2,1)} %wv_ref.5), custom_call_target="tpu_custom_call" | custom-call | flops 30000001024 | bytes 1000 | tf_op jit(solution)/shard_map/own_attention/pallas_call | solution.py:241
  40.0 7.0 %collective-permute-done.2 = bf16[144,1024]{1,0:T(8,128)(2,1)S(1)} collective-permute-done((bf16[144,1024]{1,0:T(8,128)(2,1)S(1)}, bf16[144,1024]{1,0:T(8,128)(2,1)S(1)}, u32[]{:S(2)}, u32[]{:S(2)}) %collective-permute-start.2) | collective-permute-done | bytes 294944 | tf_op jit(solution)/shard_map/ppermute | solution.py:41
  47.0 9.9 %collective-permute-start.3 = (bf16[144,1024]{1,0:T(8,128)(2,1)S(1)}, bf16[144,1024]{1,0:T(8,128)(2,1)S(1)}, u32[]{:S(2)}, u32[]{:S(2)}) collective-permute-start(bf16[144,1024]{1,0:T(8,128)(2,1)S(1)} %collective-permute-done.2), channel_id=1, source_target_pairs={{3,2},{0,3},{1,4},{2,5},{7,6},{4,7},{5,8},{6,9},{11,10},{8,11},{9,... | collective-permute-start | bytes 884744 | tf_op jit(solution)/shard_map/ppermute | solution.py:42
  56.9 0.0 collective-permute-done.before_ref
  56.9 0.0 copy-start.4
  56.9 0.8 copy-done.4
  57.7 11.0 %before_attention.1 = (f32[256,1024]{1,0:T(8,128)}, f32[256,1024]{1,0:T(8,128)}, f32[256,1024]{1,0:T(8,128)}, bf16[112,1024]{1,0:T(8,128)(2,1)}) custom-call(s32[1]{0:T(128)} %bitcast.block_ref, bf16[256,1024]{1,0:T(8,128)(2,1)} %copy-done.4, bf16[256,1024]{1,0:T(8,128)(2,1)} %get-tuple-element.15.q_ref, f32[256,1024]{1,0:T(8,128)} %get-tuple-element.16.acc_ref, ...), custom_call_target="tpu_custom_call" | custom-call | flops 10000000000 | bytes 1000 | tf_op jit(solution)/shard_map/before_attention/pallas_call | solution.py:257
  68.7 5.6 %collective-permute-start.1 = (bf16[112,1024]{1,0:T(8,128)(2,1)}, bf16[112,1024]{1,0:T(8,128)(2,1)S(1)}, u32[]{:S(2)}, u32[]{:S(2)}) collective-permute-start(bf16[112,1024]{1,0:T(8,128)(2,1)} %get-tuple-element.19), channel_id=1, source_target_pairs={{0,1},{1,2},{2,3},{3,4},{4,5},{5,6},{6,7},{7,8},{8,9},{9,10},{10,1... | collective-permute-start | bytes 688136 | tf_op jit(solution)/shard_map/ppermute | solution.py:31
  74.3 0.0 all-to-all-done.own_ref
  74.3 2.5 %collective-permute-start.5 = (bf16[16,64,128]{2,1,0:T(8,128)(2,1)S(1)}, bf16[16,64,128]{2,1,0:T(8,128)(2,1)S(1)}, u32[]{:S(2)}, u32[]{:S(2)}) collective-permute-start(bf16[16,64,128]{2,1,0:T(8,128)(2,1)S(1)} %slice.8), channel_id=1, source_target_pairs={{0,4},{4,0},{1,5},{5,1},{2,6},{6,2},{3,7},{7,3},{8,12},{12,8},{9,1... | collective-permute-start | bytes 786440 | tf_op jit(solution)/shard_map/ppermute | solution.py:396
  76.8 0.0 collective-permute-done.3.down_ref
  76.8 0.0 copy-start.5
  76.8 7.1 %collective-permute-done.1.up_ref = bf16[112,1024]{1,0:T(8,128)(2,1)S(1)} collective-permute-done((bf16[112,1024]{1,0:T(8,128)(2,1)}, bf16[112,1024]{1,0:T(8,128)(2,1)S(1)}, u32[]{:S(2)}, u32[]{:S(2)}) %collective-permute-start.1) | collective-permute-done | bytes 229408 | tf_op jit(solution)/shard_map/ppermute | solution.py:31
  83.9 0.0 copy-start.6
  83.9 0.0 copy-done.5
  83.9 0.7 copy-done.6
  84.6 0.0 copy-start.3
  84.6 12.3 %far_attention.1 = (bf16[256,1024]{1,0:T(8,128)(2,1)}, f32[32,1024]{1,0:T(8,128)}, f32[1,1152]{1,0:T(1,128)}, f32[32,128]{1,0:T(8,128)}) custom-call(s32[1]{0:T(128)} %bitcast.block_ref, s32[1,256]{1,0:T(1,128)} %bitcast.4, bf16[256,1024]{1,0:T(8,128)(2,1)} %own_ref.3, bf16[112,1024]{1,0:T(8,128)(2,1)} %copy-done.6, bf16[144,1024]{1,0:T(8,128)(2,1)} %copy-done.5, ...), custom_call_target="tpu_custom_call" | custom-call | flops 30000001024 | bytes 1000 | tf_op jit(solution)/shard_map/far_attention/pallas_call | solution.py:330
  96.9 0.0 collective-permute-done.5.other_ref
  96.9 0.0 copy-start.1
  96.9 0.7 copy-done.1
  97.6 2.2 %latent_attend.1 = bf16[16,32,128]{2,1,0:T(8,128)(2,1)} custom-call(s32[1]{0:T(128)} %bitcast.2.side_ref, bf16[16,96,128]{2,1,0:T(8,128)(2,1)S(1)} %all-to-all-done.own_ref, bf16[16,64,128]{2,1,0:T(8,128)(2,1)S(1)} %collective-permute-done.5.other_ref, f32[32,128]{1,0:T(8,128)S(1)} %copy-done.1), custom_call_target="tpu_custom_call" | custom-call | flops 1000 | bytes 1000 | tf_op jit(solution)/shard_map/latent_attend/pallas_call | solution.py:120
  99.8 14.2 %all-to-all-start.1 = ((bf16[16,32,128]{2,1,0:T(8,128)(2,1)}), bf16[16,32,128]{2,1,0:T(8,128)(2,1)S(1)}, u32[]{:S(2)}, u32[]{:S(2)}) async-start(bf16[16,32,128]{2,1,0:T(8,128)(2,1)} %latent_attend.1), calls=%async_computation.1 | async-start | bytes 262144 | tf_op jit(solution)/shard_map/all_to_all | solution.py:402
  114.1 6.1 %collective-permute-start.4 = (f32[1,1152]{1,0:T(1,128)}, f32[1,1152]{1,0:T(1,128)S(1)}, u32[]{:S(2)}, u32[]{:S(2)}) collective-permute-start(f32[1,1152]{1,0:T(1,128)} %get-tuple-element.26), channel_id=1, source_target_pairs={{1,0},{2,1},{3,2},{4,3},{5,4},{6,5},{7,6},{8,7},{9,8},{10,9},{11,1... | collective-permute-start | bytes 13832 | tf_op jit(solution)/shard_map/ppermute | solution.py:31
  120.2 1.5 %collective-permute-done.4.extra_ref = f32[1,1152]{1,0:T(1,128)S(1)} collective-permute-done((f32[1,1152]{1,0:T(1,128)}, f32[1,1152]{1,0:T(1,128)S(1)}, u32[]{:S(2)}, u32[]{:S(2)}) %collective-permute-start.4) | collective-permute-done | bytes 4640 | tf_op jit(solution)/shard_map/ppermute | solution.py:31
  121.7 0.0 copy-done.3
  121.7 0.0 copy-start
  121.7 0.9 copy-done
  122.6 0.0 copy-start.2
  122.6 0.7 copy-done.2
  123.3 0.9 patch_pool.1
  124.2 4.9 %all-to-all-done.1.heads_ref = bf16[16,32,128]{2,1,0:T(8,128)(2,1)S(1)} async-done(((bf16[16,32,128]{2,1,0:T(8,128)(2,1)}), bf16[16,32,128]{2,1,0:T(8,128)(2,1)S(1)}, u32[]{:S(2)}, u32[]{:S(2)}) %all-to-all-start.1) | async-done | bytes 131104 | tf_op jit(solution)/shard_map/all_to_all | solution.py:402
  129.0 0.8 latent_unpack.1
  (1 shorter events, 0.0 us)
Async XLA Ops:
  0.6 56.3 %collective-permute-start = (bf16[256,1024]{1,0:T(8,128)(2,1)}, bf16[256,1024]{1,0:T(8,128)(2,1)S(1)}, u32[]{:S(2)}, u32[]{:S(2)}) collective-permute-start(bf16[256,1024]{1,0:T(8,128)(2,1)} %own_ref.3), channel_id=1, source_target_pairs={{0,1},{1,2},{2,3},{3,4},{4,5},{5,6},{6,7},{7,8},{8,9},{9,10},{10,1... | collective-permute-start | bytes 1572872 | tf_op jit(solution)/shard_map/ppermute | solution.py:31
  9.5 37.4 %collective-permute-start.2 = (bf16[144,1024]{1,0:T(8,128)(2,1)S(1)}, bf16[144,1024]{1,0:T(8,128)(2,1)S(1)}, u32[]{:S(2)}, u32[]{:S(2)}) collective-permute-start(bf16[144,1024]{1,0:T(8,128)(2,1)S(1)} %slice.6), channel_id=1, source_target_pairs={{0,3},{1,0},{2,1},{3,2},{4,7},{5,4},{6,5},{7,6},{8,11},{9,8},{10,9... | collective-permute-start | bytes 884744 | tf_op jit(solution)/shard_map/ppermute | solution.py:41
  20.1 54.2 %all-to-all-start = ((bf16[16,96,128]{2,1,0:T(8,128)(2,1)}), bf16[16,96,128]{2,1,0:T(8,128)(2,1)S(1)}, u32[]{:S(2)}, u32[]{:S(2)}) async-start(bf16[16,96,128]{2,1,0:T(8,128)(2,1)} %latent_pack.1), calls=%async_computation | async-start | bytes 786432 | tf_op jit(solution)/shard_map/all_to_all | solution.py:395
  47.0 29.8 %collective-permute-start.3 = (bf16[144,1024]{1,0:T(8,128)(2,1)S(1)}, bf16[144,1024]{1,0:T(8,128)(2,1)S(1)}, u32[]{:S(2)}, u32[]{:S(2)}) collective-permute-start(bf16[144,1024]{1,0:T(8,128)(2,1)S(1)} %collective-permute-done.2), channel_id=1, source_target_pairs={{3,2},{0,3},{1,4},{2,5},{7,6},{4,7},{5,8},{6,9},{11,10},{8,11},{9,... | collective-permute-start | bytes 884744 | tf_op jit(solution)/shard_map/ppermute | solution.py:42
  56.9 0.8 copy-start.4
  68.7 15.2 %collective-permute-start.1 = (bf16[112,1024]{1,0:T(8,128)(2,1)}, bf16[112,1024]{1,0:T(8,128)(2,1)S(1)}, u32[]{:S(2)}, u32[]{:S(2)}) collective-permute-start(bf16[112,1024]{1,0:T(8,128)(2,1)} %get-tuple-element.19), channel_id=1, source_target_pairs={{0,1},{1,2},{2,3},{3,4},{4,5},{5,6},{6,7},{7,8},{8,9},{9,10},{10,1... | collective-permute-start | bytes 688136 | tf_op jit(solution)/shard_map/ppermute | solution.py:31
  74.3 22.6 %collective-permute-start.5 = (bf16[16,64,128]{2,1,0:T(8,128)(2,1)S(1)}, bf16[16,64,128]{2,1,0:T(8,128)(2,1)S(1)}, u32[]{:S(2)}, u32[]{:S(2)}) collective-permute-start(bf16[16,64,128]{2,1,0:T(8,128)(2,1)S(1)} %slice.8), channel_id=1, source_target_pairs={{0,4},{4,0},{1,5},{5,1},{2,6},{6,2},{3,7},{7,3},{8,12},{12,8},{9,1... | collective-permute-start | bytes 786440 | tf_op jit(solution)/shard_map/ppermute | solution.py:396
  76.8 7.1 %copy-start.5 = (bf16[144,1024]{1,0:T(8,128)(2,1)}, bf16[144,1024]{1,0:T(8,128)(2,1)S(1)}, u32[]{:S(2)}) copy-start(bf16[144,1024]{1,0:T(8,128)(2,1)S(1)} %collective-permute-done.3.down_ref) | copy-start | bytes 884740
  83.9 0.7 copy-start.6
  84.6 37.1 %copy-start.3 = (s32[256]{0:T(256)S(1)}, s32[256]{0:T(256)}, u32[]{:S(2)}) copy-start(s32[256]{0:T(256)} %param.10) | copy-start | bytes 3076
  96.9 0.7 copy-start.1
  99.8 29.2 %all-to-all-start.1 = ((bf16[16,32,128]{2,1,0:T(8,128)(2,1)}), bf16[16,32,128]{2,1,0:T(8,128)(2,1)S(1)}, u32[]{:S(2)}, u32[]{:S(2)}) async-start(bf16[16,32,128]{2,1,0:T(8,128)(2,1)} %latent_attend.1), calls=%async_computation.1 | async-start | bytes 262144 | tf_op jit(solution)/shard_map/all_to_all | solution.py:402
  114.1 7.6 %collective-permute-start.4 = (f32[1,1152]{1,0:T(1,128)}, f32[1,1152]{1,0:T(1,128)S(1)}, u32[]{:S(2)}, u32[]{:S(2)}) collective-permute-start(f32[1,1152]{1,0:T(1,128)} %get-tuple-element.26), channel_id=1, source_target_pairs={{1,0},{2,1},{3,2},{4,3},{5,4},{6,5},{7,6},{8,7},{9,8},{10,9},{11,1... | collective-permute-start | bytes 13832 | tf_op jit(solution)/shard_map/ppermute | solution.py:31
  121.7 0.9 copy-start
  122.6 0.7 copy-start.2

commit v8 on v4

--- a/solution.py
+++ b/solution.py
@@ -11,7 +11,7 @@
 LAT_HEAD = 128
 GROUP = 256
 NEGATIVE = -1e30
-UP_ROWS = 96
+UP_ROWS = 112
 MARK = 1024.0
 SEQ = ("yh", "yl", "zh")
 PACK_COST = 1000
@@ -374,7 +374,8 @@
     )(block, start_row, own, far_up, far_down, *parts, w_qkv, w_qkv, w_out)
 
 
-def pool_kernel(start_ref, sums_ref, count_ref, extra_ref, out_ref):
+def pool_kernel(start_ref, sums_ref, count_ref, extra_ref, after_ref, out_ref):
+    del after_ref
     slots, width = sums_ref.shape
     used = jnp.sum(start_ref[...])
     last = lax.broadcasted_iota(jnp.int32, (slots, 1), 0) == used - 1
@@ -385,13 +386,14 @@
     out_ref[...] = jnp.where(count > 0, mean, 0.0).astype(jnp.bfloat16)
 
 
-def pool(start_row, sums, count, extra):
+def pool(start_row, sums, count, extra, after):
     return pl.pallas_call(
         pool_kernel,
         out_shape=jax.ShapeDtypeStruct(sums.shape, jnp.bfloat16),
+        in_specs=[pl.BlockSpec(memory_space=pltpu.VMEM)] * 4 + [pl.BlockSpec(memory_space=pl.ANY)],
         compiler_params=params(VMEM_SOME),
         name="patch_pool",
-    )(start_row, sums, count, extra)
+    )(start_row, sums, count, extra, after)
 
 
 def local(byte_states, w_qkv, w_out, patch_start, latent_q, latent_k, latent_v):
@@ -418,7 +420,7 @@
         block, start_row, byte_states, far_up, far_down, (query, *parts), w_qkv, w_out, slots
     )
     extra = shift(lead, -1)
-    patch_embed = pool(start_row, sums, count, extra)
+    patch_embed = pool(start_row, sums, count, extra, latent_out)
     return encoded, patch_embed, latent_out
 
 

time: 121 us -> 120 us (level)
  waiting for transfers between devices: 18 us -> 5.81 us
  starting transfers between devices: 59.7 us -> 70.5 us
    ppermute x1, waiting for transfers between devices: 12.8 us -> 2.61 us  [down(): relayed = lax.ppermute(x, SEQ, [(s, after(s, 1)) for s in sources])]
    all_to_all x1, starting transfers between devices: 8.3 us -> 14.6 us  [local(): returned = lax.all_to_all(heads, ('yh', 'zh'), 0, 0, tiled=True)]
    ppermute x3, starting transfers between devices: 18 us -> 21.6 us  [shift(): lax.ppermute(x, SEQ, [(i, i + by) for i in range(count) if 0 <= i + by <...]
    ppermute x1, waiting for transfers between devices: 3.64 us -> 0.15 us  [local(): other = lax.ppermute(split(own, up), 'yl', [(0, 1), (1, 0)])]
    all_to_all x1, waiting for transfers between devices: 0.01 us -> 2.35 us  [local(): own = lax.all_to_all(packed, ('yh', 'zh'), 0, 0, tiled=True)]
    unnamed x12 -> x14, local copies, waits for them, and re-layouts: 3.18 us -> 4.08 us
  transfers between devices with their start and end apart: 8 -> 8, of which waited for: 3 -> 4; matrix products, arithmetic and copies ran while one was open for 1% -> 1% of each run, Pallas kernels for 31% -> 31%
where the time goes in v8:
time: 120 us
  starting transfers between devices  70.5 us (59%)
  Pallas kernels  37.7 us (31%)
  waiting for transfers between devices  5.81 us (5%)
  local copies, waits for them, and re-layouts  5.07 us (4%)
    ppermute x3, starting transfers between devices, shift(): lax.ppermute(x, SEQ, [(i, i + by) for i in range(count) if 0 <= i + by <...  21.6 us
    all_to_all x1, starting transfers between devices, local(): returned = lax.all_to_all(heads, ('yh', 'zh'), 0, 0, tiled=True)  14.6 us
    pallas_call x1, Pallas kernels, far_attend(): pl.pallas_call(far_kernel, grid=(steps,), out_shape=(jax.ShapeDtypeStruct...  12.3 us
    all_to_all x1, starting transfers between devices, local(): own = lax.all_to_all(packed, ('yh', 'zh'), 0, 0, tiled=True)  12 us
    pallas_call x1, Pallas kernels, before_attend(): pl.pallas_call(before_kernel, grid=(width // GROUP,), out_shape=(kept, ke...  11 us
    ppermute x1, starting transfers between devices, down(): lax.ppermute(relayed, SEQ, [(after(s, 1), s + ring - 2) for s in sources])  11 us
    ppermute x1, starting transfers between devices, down(): relayed = lax.ppermute(x, SEQ, [(s, after(s, 1)) for s in sources])  8.59 us
    pallas_call x1, Pallas kernels, own_attend(): pl.pallas_call(own_kernel, grid=(width // GROUP,), out_shape=(jax.ShapeDt...  8.54 us
  transfers between devices with their start and end apart: 8, of which 4 were waited for; matrix products, arithmetic and copies ran while one was open for 1% of the time, Pallas kernels for 31%

profile of v8, /device:TPU:52, one launch (start us, length us, event | category | flops | bytes accessed | tf_op | source)
XLA Modules:
  0.0 119.8 jit_solution(15116169051262104793)
XLA Ops:
  0.6 7.9 %collective-permute-start = (bf16[256,1024]{1,0:T(8,128)(2,1)}, bf16[256,1024]{1,0:T(8,128)(2,1)S(1)}, u32[]{:S(2)}, u32[]{:S(2)}) collective-permute-start(bf16[256,1024]{1,0:T(8,128)(2,1)} %own_ref.3), channel_id=1, source_target_pairs={{0,1},{1,2},{2,3},{3,4},{4,5},{5,6},{6,7},{7,8},{8,9},{9,10},{10,1... | collective-permute-start | bytes 1572872 | tf_op jit(solution)/shard_map/ppermute | solution.py:31
  8.5 1.0 slice.3
  9.5 8.6 %collective-permute-start.2 = (bf16[144,1024]{1,0:T(8,128)(2,1)S(1)}, bf16[144,1024]{1,0:T(8,128)(2,1)S(1)}, u32[]{:S(2)}, u32[]{:S(2)}) collective-permute-start(bf16[144,1024]{1,0:T(8,128)(2,1)S(1)} %slice.3), channel_id=1, source_target_pairs={{0,3},{1,0},{2,1},{3,2},{4,7},{5,4},{6,5},{7,6},{8,11},{9,8},{10,9... | collective-permute-start | bytes 884744 | tf_op jit(solution)/shard_map/ppermute | solution.py:41
  18.1 1.9 %latent_pack.1 = bf16[16,96,128]{2,1,0:T(8,128)(2,1)} custom-call(s32[1,256]{1,0:T(1,128)} %bitcast.3, bf16[32,2048]{1,0:T(8,128)(2,1)} %q_ref.1, bf16[32,2048]{1,0:T(8,128)(2,1)} %k_ref.1, bf16[32,2048]{1,0:T(8,128)(2,1)} %v_ref.1), custom_call_target="tpu_custom_call" | custom-call | flops 1000 | bytes 1000 | tf_op jit(solution)/shard_map/latent_pack/pallas_call | solution.py:71
  20.1 12.0 %all-to-all-start = ((bf16[16,96,128]{2,1,0:T(8,128)(2,1)}), bf16[16,96,128]{2,1,0:T(8,128)(2,1)S(1)}, u32[]{:S(2)}, u32[]{:S(2)}) async-start(bf16[16,96,128]{2,1,0:T(8,128)(2,1)} %latent_pack.1), calls=%async_computation | async-start | bytes 786432 | tf_op jit(solution)/shard_map/all_to_all | solution.py:413
  32.1 8.5 %own_attention.1 = (bf16[256,1024]{1,0:T(8,128)(2,1)}, f32[256,1024]{1,0:T(8,128)}, f32[256,1024]{1,0:T(8,128)}, f32[256,1024]{1,0:T(8,128)}) custom-call(bf16[256,1024]{1,0:T(8,128)(2,1)} %own_ref.3, bf16[1024,3072]{1,0:T(8,128)(2,1)} %wv_ref.5, bf16[1024,3072]{1,0:T(8,128)(2,1)} %wv_ref.5, bf16[1024,3072]{1,0:T(8,128)(2,1)} %wv_ref.5), custom_call_target="tpu_custom_call" | custom-call | flops 30000001024 | bytes 1000 | tf_op jit(solution)/shard_map/own_attention/pallas_call | solution.py:257
  40.6 2.6 %collective-permute-done.2 = bf16[144,1024]{1,0:T(8,128)(2,1)S(1)} collective-permute-done((bf16[144,1024]{1,0:T(8,128)(2,1)S(1)}, bf16[144,1024]{1,0:T(8,128)(2,1)S(1)}, u32[]{:S(2)}, u32[]{:S(2)}) %collective-permute-start.2) | collective-permute-done | bytes 294944 | tf_op jit(solution)/shard_map/ppermute | solution.py:41
  43.3 11.0 %collective-permute-start.3 = (bf16[144,1024]{1,0:T(8,128)(2,1)S(1)}, bf16[144,1024]{1,0:T(8,128)(2,1)S(1)}, u32[]{:S(2)}, u32[]{:S(2)}) collective-permute-start(bf16[144,1024]{1,0:T(8,128)(2,1)S(1)} %collective-permute-done.2), channel_id=1, source_target_pairs={{3,2},{0,3},{1,4},{2,5},{7,6},{4,7},{5,8},{6,9},{11,10},{8,11},{9,... | collective-permute-start | bytes 884744 | tf_op jit(solution)/shard_map/ppermute | solution.py:42
  54.2 0.0 collective-permute-done.before_ref
  54.2 0.0 copy-start.4
  54.3 0.8 copy-done.4
  55.0 11.0 %before_attention.1 = (f32[256,1024]{1,0:T(8,128)}, f32[256,1024]{1,0:T(8,128)}, f32[256,1024]{1,0:T(8,128)}, bf16[112,1024]{1,0:T(8,128)(2,1)}) custom-call(s32[1]{0:T(128)} %bitcast.block_ref, bf16[256,1024]{1,0:T(8,128)(2,1)} %copy-done.4, bf16[256,1024]{1,0:T(8,128)(2,1)} %get-tuple-element.15.q_ref, f32[256,1024]{1,0:T(8,128)} %get-tuple-element.16.acc_ref, ...), custom_call_target="tpu_custom_call" | custom-call | flops 10000000000 | bytes 1000 | tf_op jit(solution)/shard_map/before_attention/pallas_call | solution.py:273
  66.0 2.4 %all-to-all-done.own_ref = bf16[16,96,128]{2,1,0:T(8,128)(2,1)S(1)} async-done(((bf16[16,96,128]{2,1,0:T(8,128)(2,1)}), bf16[16,96,128]{2,1,0:T(8,128)(2,1)S(1)}, u32[]{:S(2)}, u32[]{:S(2)}) %all-to-all-start) | async-done | bytes 393248 | tf_op jit(solution)/shard_map/all_to_all | solution.py:413
  68.4 2.7 %collective-permute-start.5 = (bf16[16,64,128]{2,1,0:T(8,128)(2,1)S(1)}, bf16[16,64,128]{2,1,0:T(8,128)(2,1)S(1)}, u32[]{:S(2)}, u32[]{:S(2)}) collective-permute-start(bf16[16,64,128]{2,1,0:T(8,128)(2,1)S(1)} %latent_split.1), channel_id=1, source_target_pairs={{0,4},{4,0},{1,5},{5,1},{2,6},{6,2},{3,7},{7,3},{8,12},{12,8},{9,1... | collective-permute-start | bytes 786440 | tf_op jit(solution)/shard_map/ppermute | solution.py:414
  71.1 6.3 %collective-permute-start.1 = (bf16[112,1024]{1,0:T(8,128)(2,1)}, bf16[112,1024]{1,0:T(8,128)(2,1)S(1)}, u32[]{:S(2)}, u32[]{:S(2)}) collective-permute-start(bf16[112,1024]{1,0:T(8,128)(2,1)} %get-tuple-element.19.after_ref), channel_id=1, source_target_pairs={{0,1},{1,2},{2,3},{3,4},{4,5},{5,6},{6,7},{7,8},{8,9},{9,10},{10,1... | collective-permute-start | bytes 688136 | tf_op jit(solution)/shard_map/ppermute | solution.py:31
  77.4 0.1 collective-permute-done.5.other_ref
  77.6 2.2 %latent_attend.1 = bf16[16,32,128]{2,1,0:T(8,128)(2,1)} custom-call(s32[1]{0:T(128)} %bitcast.2.side_ref, bf16[16,96,128]{2,1,0:T(8,128)(2,1)S(1)} %all-to-all-done.own_ref, bf16[16,64,128]{2,1,0:T(8,128)(2,1)S(1)} %collective-permute-done.5.other_ref), custom_call_target="tpu_custom_call" | custom-call | flops 1000 | bytes 1000 | tf_op jit(solution)/shard_map/latent_attend/pallas_call | solution.py:119
  79.8 14.6 %all-to-all-start.1 = ((bf16[16,32,128]{2,1,0:T(8,128)(2,1)}), bf16[16,32,128]{2,1,0:T(8,128)(2,1)S(1)}, u32[]{:S(2)}, u32[]{:S(2)}) async-start(bf16[16,32,128]{2,1,0:T(8,128)(2,1)} %latent_attend.1), calls=%async_computation.1 | async-start | bytes 262144 | tf_op jit(solution)/shard_map/all_to_all | solution.py:416
  94.4 0.0 collective-permute-done.3.down_ref
  94.4 0.0 copy-start.5
  94.4 0.0 collective-permute-done.1.up_ref
  94.4 0.0 copy-start.6
  94.4 0.7 copy-done.5
  95.1 0.1 copy-done.6
  95.2 0.0 copy-start.3
  95.2 12.3 %far_attention.1 = (bf16[256,1024]{1,0:T(8,128)(2,1)}, f32[32,1024]{1,0:T(8,128)}, f32[1,1152]{1,0:T(1,128)}, f32[32,128]{1,0:T(8,128)}) custom-call(s32[1]{0:T(128)} %bitcast.block_ref, s32[1,256]{1,0:T(1,128)} %bitcast.4, bf16[256,1024]{1,0:T(8,128)(2,1)} %own_ref.3, bf16[112,1024]{1,0:T(8,128)(2,1)} %copy-done.6, bf16[144,1024]{1,0:T(8,128)(2,1)} %copy-done.5, ...), custom_call_target="tpu_custom_call" | custom-call | flops 30000001024 | bytes 1000 | tf_op jit(solution)/shard_map/far_attention/pallas_call | solution.py:346
  107.5 7.4 %collective-permute-start.4 = (f32[1,1152]{1,0:T(1,128)}, f32[1,1152]{1,0:T(1,128)S(1)}, u32[]{:S(2)}, u32[]{:S(2)}) collective-permute-start(f32[1,1152]{1,0:T(1,128)} %get-tuple-element.26), channel_id=1, source_target_pairs={{1,0},{2,1},{3,2},{4,3},{5,4},{6,5},{7,6},{8,7},{9,8},{10,9},{11,1... | collective-permute-start | bytes 13832 | tf_op jit(solution)/shard_map/ppermute | solution.py:31
  114.9 0.0 all-to-all-done.1.heads_ref
  114.9 0.0 copy-done.3
  114.9 0.8 latent_unpack.1.after_ref
  115.7 0.7 collective-permute-done.4.extra_ref
  116.4 0.0 copy-start
  116.4 0.9 copy-done
  117.3 0.0 copy-start.1
  117.3 0.9 copy-done.1
  118.2 0.0 copy-start.2
  118.2 0.7 copy-done.2
  118.9 0.9 patch_pool.1
  (1 shorter events, 0.0 us)
Async XLA Ops:
  0.6 53.6 %collective-permute-start = (bf16[256,1024]{1,0:T(8,128)(2,1)}, bf16[256,1024]{1,0:T(8,128)(2,1)S(1)}, u32[]{:S(2)}, u32[]{:S(2)}) collective-permute-start(bf16[256,1024]{1,0:T(8,128)(2,1)} %own_ref.3), channel_id=1, source_target_pairs={{0,1},{1,2},{2,3},{3,4},{4,5},{5,6},{6,7},{7,8},{8,9},{9,10},{10,1... | collective-permute-start | bytes 1572872 | tf_op jit(solution)/shard_map/ppermute | solution.py:31
  9.5 33.7 %collective-permute-start.2 = (bf16[144,1024]{1,0:T(8,128)(2,1)S(1)}, bf16[144,1024]{1,0:T(8,128)(2,1)S(1)}, u32[]{:S(2)}, u32[]{:S(2)}) collective-permute-start(bf16[144,1024]{1,0:T(8,128)(2,1)S(1)} %slice.3), channel_id=1, source_target_pairs={{0,3},{1,0},{2,1},{3,2},{4,7},{5,4},{6,5},{7,6},{8,11},{9,8},{10,9... | collective-permute-start | bytes 884744 | tf_op jit(solution)/shard_map/ppermute | solution.py:41
  20.1 48.3 %all-to-all-start = ((bf16[16,96,128]{2,1,0:T(8,128)(2,1)}), bf16[16,96,128]{2,1,0:T(8,128)(2,1)S(1)}, u32[]{:S(2)}, u32[]{:S(2)}) async-start(bf16[16,96,128]{2,1,0:T(8,128)(2,1)} %latent_pack.1), calls=%async_computation | async-start | bytes 786432 | tf_op jit(solution)/shard_map/all_to_all | solution.py:413
  43.3 51.1 %collective-permute-start.3 = (bf16[144,1024]{1,0:T(8,128)(2,1)S(1)}, bf16[144,1024]{1,0:T(8,128)(2,1)S(1)}, u32[]{:S(2)}, u32[]{:S(2)}) collective-permute-start(bf16[144,1024]{1,0:T(8,128)(2,1)S(1)} %collective-permute-done.2), channel_id=1, source_target_pairs={{3,2},{0,3},{1,4},{2,5},{7,6},{4,7},{5,8},{6,9},{11,10},{8,11},{9,... | collective-permute-start | bytes 884744 | tf_op jit(solution)/shard_map/ppermute | solution.py:42
  54.2 0.8 copy-start.4
  68.4 9.2 %collective-permute-start.5 = (bf16[16,64,128]{2,1,0:T(8,128)(2,1)S(1)}, bf16[16,64,128]{2,1,0:T(8,128)(2,1)S(1)}, u32[]{:S(2)}, u32[]{:S(2)}) collective-permute-start(bf16[16,64,128]{2,1,0:T(8,128)(2,1)S(1)} %latent_split.1), channel_id=1, source_target_pairs={{0,4},{4,0},{1,5},{5,1},{2,6},{6,2},{3,7},{7,3},{8,12},{12,8},{9,1... | collective-permute-start | bytes 786440 | tf_op jit(solution)/shard_map/ppermute | solution.py:414
  71.1 23.3 %collective-permute-start.1 = (bf16[112,1024]{1,0:T(8,128)(2,1)}, bf16[112,1024]{1,0:T(8,128)(2,1)S(1)}, u32[]{:S(2)}, u32[]{:S(2)}) collective-permute-start(bf16[112,1024]{1,0:T(8,128)(2,1)} %get-tuple-element.19.after_ref), channel_id=1, source_target_pairs={{0,1},{1,2},{2,3},{3,4},{4,5},{5,6},{6,7},{7,8},{8,9},{9,10},{10,1... | collective-permute-start | bytes 688136 | tf_op jit(solution)/shard_map/ppermute | solution.py:31
  79.8 35.0 %all-to-all-start.1 = ((bf16[16,32,128]{2,1,0:T(8,128)(2,1)}), bf16[16,32,128]{2,1,0:T(8,128)(2,1)S(1)}, u32[]{:S(2)}, u32[]{:S(2)}) async-start(bf16[16,32,128]{2,1,0:T(8,128)(2,1)} %latent_attend.1), calls=%async_computation.1 | async-start | bytes 262144 | tf_op jit(solution)/shard_map/all_to_all | solution.py:416
  94.4 0.7 copy-start.5
  94.4 0.8 copy-start.6
  95.2 19.7 %copy-start.3 = (s32[256]{0:T(256)S(1)}, s32[256]{0:T(256)}, u32[]{:S(2)}) copy-start(s32[256]{0:T(256)} %param.10) | copy-start | bytes 3076
  107.5 8.9 %collective-permute-start.4 = (f32[1,1152]{1,0:T(1,128)}, f32[1,1152]{1,0:T(1,128)S(1)}, u32[]{:S(2)}, u32[]{:S(2)}) collective-permute-start(f32[1,1152]{1,0:T(1,128)} %get-tuple-element.26), channel_id=1, source_target_pairs={{1,0},{2,1},{3,2},{4,3},{5,4},{6,5},{7,6},{8,7},{9,8},{10,9},{11,1... | collective-permute-start | bytes 13832 | tf_op jit(solution)/shard_map/ppermute | solution.py:31
  116.4 0.9 copy-start
  117.3 0.9 copy-start.1
  118.2 0.7 copy-start.2

commit v9 on v8

--- a/solution.py
+++ b/solution.py
@@ -286,7 +286,7 @@
 
 def far_kernel(
     block_ref, start_ref, own_ref, up_ref, down_ref, q_ref, acc_ref, peak_ref, norm_ref, wk_ref, wv_ref, wo_ref,
-    enc_ref, sums_ref, lead_ref, count_ref, total_ref,
+    enc_ref, sums_ref, lead_ref, total_ref,
 ):
     step = pl.program_id(0)
     rows = own_ref.shape[0]
@@ -325,9 +325,11 @@
         onehot = (rank == slot).astype(jnp.float32)
         summed = dot(onehot.astype(jnp.bfloat16), encoded)
         counts = jnp.sum(onehot, axis=1, keepdims=True)
-        sums_ref[...] = summed[0:slots]
-        count_ref[...] = jnp.broadcast_to(counts[0:slots], (slots, 128))
         width = own_ref.shape[1]
+        used = jnp.sum(start_ref[...].astype(jnp.float32), axis=1, keepdims=True)
+        sums_ref[:, 0:width] = summed[0:slots]
+        first_lanes = lax.broadcasted_iota(jnp.int32, (slots, 128), 1) < 64
+        sums_ref[:, width : width + 128] = jnp.where(first_lanes, counts[0:slots], used)
         lead_ref[:, 0:width] = summed[slots : slots + 1]
         lead_ref[:, width : width + 128] = jnp.broadcast_to(counts[slots : slots + 1], (1, 128))
 
@@ -348,9 +350,8 @@
         grid=(steps,),
         out_shape=(
             jax.ShapeDtypeStruct((rows, width), jnp.bfloat16),
-            jax.ShapeDtypeStruct((slots, width), jnp.float32),
+            jax.ShapeDtypeStruct((slots, width + 128), jnp.float32),
             jax.ShapeDtypeStruct((1, width + 128), jnp.float32),
-            jax.ShapeDtypeStruct((slots, 128), jnp.float32),
         ),
         in_specs=[
             pl.BlockSpec(memory_space=pltpu.SMEM),
@@ -366,7 +367,7 @@
             weight(2),
             pl.BlockSpec((GROUP, width), lambda i: (i, 0)),
         ],
-        out_specs=(full((rows, width)), full((slots, width)), full((1, width + 128)), full((slots, 128))),
+        out_specs=(full((rows, width)), full((slots, width + 128)), full((1, width + 128))),
         scratch_shapes=[pltpu.VMEM((rows, width), jnp.float32)],
         compiler_params=params(VMEM_ALL),
         cost_estimate=pl.CostEstimate(flops=FAR_COST, bytes_accessed=1000, transcendentals=0),
@@ -374,26 +375,27 @@
     )(block, start_row, own, far_up, far_down, *parts, w_qkv, w_qkv, w_out)
 
 
-def pool_kernel(start_ref, sums_ref, count_ref, extra_ref, after_ref, out_ref):
+def pool_kernel(sums_ref, extra_ref, after_ref, out_ref):
     del after_ref
-    slots, width = sums_ref.shape
-    used = jnp.sum(start_ref[...])
+    slots, width = out_ref.shape
+    used = sums_ref[:, width + 64 : width + 65].astype(jnp.int32)
     last = lax.broadcasted_iota(jnp.int32, (slots, 1), 0) == used - 1
     extra = extra_ref[...]
-    sums = sums_ref[...] + jnp.where(last, extra[:, 0:width], 0.0)
-    count = count_ref[:, 0:1] + jnp.where(last, extra[:, width : width + 1], 0.0)
+    sums = sums_ref[:, 0:width] + jnp.where(last, extra[:, 0:width], 0.0)
+    count = sums_ref[:, width : width + 1] + jnp.where(last, extra[:, width : width + 1], 0.0)
     mean = sums / jnp.maximum(count, 1.0)
     out_ref[...] = jnp.where(count > 0, mean, 0.0).astype(jnp.bfloat16)
 
 
-def pool(start_row, sums, count, extra, after):
+def pool(sums, extra, after):
+    slots, spread = sums.shape
     return pl.pallas_call(
         pool_kernel,
-        out_shape=jax.ShapeDtypeStruct(sums.shape, jnp.bfloat16),
-        in_specs=[pl.BlockSpec(memory_space=pltpu.VMEM)] * 4 + [pl.BlockSpec(memory_space=pl.ANY)],
+        out_shape=jax.ShapeDtypeStruct((slots, spread - 128), jnp.bfloat16),
+        in_specs=[pl.BlockSpec(memory_space=pltpu.VMEM)] * 2 + [pl.BlockSpec(memory_space=pl.ANY)],
         compiler_params=params(VMEM_SOME),
         name="patch_pool",
-    )(start_row, sums, count, extra, after)
+    )(sums, extra, after)
 
 
 def local(byte_states, w_qkv, w_out, patch_start, latent_q, latent_k, latent_v):
@@ -416,11 +418,11 @@
     returned = lax.all_to_all(heads, ("yh", "zh"), 0, 0, tiled=True)
     latent_out = unpack(start_row, returned)
 
-    encoded, sums, lead, count = far_attend(
+    encoded, sums, lead = far_attend(
         block, start_row, byte_states, far_up, far_down, (query, *parts), w_qkv, w_out, slots
     )
     extra = shift(lead, -1)
-    patch_embed = pool(start_row, sums, count, extra, latent_out)
+    patch_embed = pool(sums, extra, latent_out)
     return encoded, patch_embed, latent_out
 
 

time: 120 us -> 120 us (level)
  the two profiles are of different devices: /device:TPU:52 before, /device:TPU:42 now
where the time goes in v9:
time: 120 us; the launch traced here: 119 us
  starting transfers between devices  68.4 us (57%)
  Pallas kernels  37.7 us (31%)
  waiting for transfers between devices  7.88 us (7%)
  local copies, waits for them, and re-layouts  4.37 us (4%)
    ppermute x3, starting transfers between devices, shift(): lax.ppermute(x, SEQ, [(i, i + by) for i in range(count) if 0 <= i + by <...  22.3 us
    all_to_all x1, starting transfers between devices, local(): returned = lax.all_to_all(heads, ('yh', 'zh'), 0, 0, tiled=True)  15.2 us
    pallas_call x1, Pallas kernels, far_attend(): pl.pallas_call(far_kernel, grid=(steps,), out_shape=(jax.ShapeDtypeStruct...  12.3 us
    all_to_all x1, starting transfers between devices, local(): own = lax.all_to_all(packed, ('yh', 'zh'), 0, 0, tiled=True)  12.3 us
    pallas_call x1, Pallas kernels, before_attend(): pl.pallas_call(before_kernel, grid=(width // GROUP,), out_shape=(kept, ke...  11 us
    ppermute x1, starting transfers between devices, down(): relayed = lax.ppermute(x, SEQ, [(s, after(s, 1)) for s in sources])  8.59 us
    pallas_call x1, Pallas kernels, own_attend(): pl.pallas_call(own_kernel, grid=(width // GROUP,), out_shape=(jax.ShapeDt...  8.55 us
    ppermute x1, starting transfers between devices, down(): lax.ppermute(relayed, SEQ, [(after(s, 1), s + ring - 2) for s in sources])  7.73 us
  transfers between devices with their start and end apart: 8, of which 4 were waited for; matrix products, arithmetic and copies ran while one was open for 1% of the time, Pallas kernels for 31%

profile of v9, /device:TPU:42, one launch (start us, length us, event | category | flops | bytes accessed | tf_op | source)
XLA Modules:
  0.0 119.1 jit_solution(11460788510721064095)
XLA Ops:
  0.6 7.9 %collective-permute-start = (bf16[256,1024]{1,0:T(8,128)(2,1)}, bf16[256,1024]{1,0:T(8,128)(2,1)S(1)}, u32[]{:S(2)}, u32[]{:S(2)}) collective-permute-start(bf16[256,1024]{1,0:T(8,128)(2,1)} %own_ref.3), channel_id=1, source_target_pairs={{0,1},{1,2},{2,3},{3,4},{4,5},{5,6},{6,7},{7,8},{8,9},{9,10},{10,1... | collective-permute-start | bytes 1572872 | tf_op jit(solution)/shard_map/ppermute | solution.py:31
  8.5 1.0 slice.3
  9.5 8.6 %collective-permute-start.2 = (bf16[144,1024]{1,0:T(8,128)(2,1)S(1)}, bf16[144,1024]{1,0:T(8,128)(2,1)S(1)}, u32[]{:S(2)}, u32[]{:S(2)}) collective-permute-start(bf16[144,1024]{1,0:T(8,128)(2,1)S(1)} %slice.3), channel_id=1, source_target_pairs={{0,3},{1,0},{2,1},{3,2},{4,7},{5,4},{6,5},{7,6},{8,11},{9,8},{10,9... | collective-permute-start | bytes 884744 | tf_op jit(solution)/shard_map/ppermute | solution.py:41
  18.1 1.9 %latent_pack.1 = bf16[16,96,128]{2,1,0:T(8,128)(2,1)} custom-call(s32[1,256]{1,0:T(1,128)} %bitcast.3, bf16[32,2048]{1,0:T(8,128)(2,1)} %q_ref.1, bf16[32,2048]{1,0:T(8,128)(2,1)} %k_ref.1, bf16[32,2048]{1,0:T(8,128)(2,1)} %v_ref.1), custom_call_target="tpu_custom_call" | custom-call | flops 1000 | bytes 1000 | tf_op jit(solution)/shard_map/latent_pack/pallas_call | solution.py:71
  20.1 12.3 %all-to-all-start = ((bf16[16,96,128]{2,1,0:T(8,128)(2,1)}), bf16[16,96,128]{2,1,0:T(8,128)(2,1)S(1)}, u32[]{:S(2)}, u32[]{:S(2)}) async-start(bf16[16,96,128]{2,1,0:T(8,128)(2,1)} %latent_pack.1), calls=%async_computation | async-start | bytes 786432 | tf_op jit(solution)/shard_map/all_to_all | solution.py:415
  32.3 8.6 %own_attention.1 = (bf16[256,1024]{1,0:T(8,128)(2,1)}, f32[256,1024]{1,0:T(8,128)}, f32[256,1024]{1,0:T(8,128)}, f32[256,1024]{1,0:T(8,128)}) custom-call(bf16[256,1024]{1,0:T(8,128)(2,1)} %own_ref.3, bf16[1024,3072]{1,0:T(8,128)(2,1)} %wv_ref.5, bf16[1024,3072]{1,0:T(8,128)(2,1)} %wv_ref.5, bf16[1024,3072]{1,0:T(8,128)(2,1)} %wv_ref.5), custom_call_target="tpu_custom_call" | custom-call | flops 30000001024 | bytes 1000 | tf_op jit(solution)/shard_map/own_attention/pallas_call | solution.py:257
  40.9 1.9 %collective-permute-done.2 = bf16[144,1024]{1,0:T(8,128)(2,1)S(1)} collective-permute-done((bf16[144,1024]{1,0:T(8,128)(2,1)S(1)}, bf16[144,1024]{1,0:T(8,128)(2,1)S(1)}, u32[]{:S(2)}, u32[]{:S(2)}) %collective-permute-start.2) | collective-permute-done | bytes 294944 | tf_op jit(solution)/shard_map/ppermute | solution.py:41
  42.8 7.7 %collective-permute-start.3 = (bf16[144,1024]{1,0:T(8,128)(2,1)S(1)}, bf16[144,1024]{1,0:T(8,128)(2,1)S(1)}, u32[]{:S(2)}, u32[]{:S(2)}) collective-permute-start(bf16[144,1024]{1,0:T(8,128)(2,1)S(1)} %collective-permute-done.2), channel_id=1, source_target_pairs={{3,2},{0,3},{1,4},{2,5},{7,6},{4,7},{5,8},{6,9},{11,10},{8,11},{9,... | collective-permute-start | bytes 884744 | tf_op jit(solution)/shard_map/ppermute | solution.py:42
  50.5 0.2 collective-permute-done.before_ref
  50.7 0.0 copy-start.3
  50.7 0.8 copy-done.3
  51.5 11.0 %before_attention.1 = (f32[256,1024]{1,0:T(8,128)}, f32[256,1024]{1,0:T(8,128)}, f32[256,1024]{1,0:T(8,128)}, bf16[112,1024]{1,0:T(8,128)(2,1)}) custom-call(s32[1]{0:T(128)} %bitcast.block_ref, bf16[256,1024]{1,0:T(8,128)(2,1)} %copy-done.3, bf16[256,1024]{1,0:T(8,128)(2,1)} %get-tuple-element.14.q_ref, f32[256,1024]{1,0:T(8,128)} %get-tuple-element.15.acc_ref, ...), custom_call_target="tpu_custom_call" | custom-call | flops 10000000000 | bytes 1000 | tf_op jit(solution)/shard_map/before_attention/pallas_call | solution.py:273
  62.5 5.1 %all-to-all-done.own_ref = bf16[16,96,128]{2,1,0:T(8,128)(2,1)S(1)} async-done(((bf16[16,96,128]{2,1,0:T(8,128)(2,1)}), bf16[16,96,128]{2,1,0:T(8,128)(2,1)S(1)}, u32[]{:S(2)}, u32[]{:S(2)}) %all-to-all-start) | async-done | bytes 393248 | tf_op jit(solution)/shard_map/all_to_all | solution.py:415
  67.6 2.3 %collective-permute-start.5 = (bf16[16,64,128]{2,1,0:T(8,128)(2,1)S(1)}, bf16[16,64,128]{2,1,0:T(8,128)(2,1)S(1)}, u32[]{:S(2)}, u32[]{:S(2)}) collective-permute-start(bf16[16,64,128]{2,1,0:T(8,128)(2,1)S(1)} %latent_split.1), channel_id=1, source_target_pairs={{0,4},{4,0},{1,5},{5,1},{2,6},{6,2},{3,7},{7,3},{8,12},{12,8},{9,1... | collective-permute-start | bytes 786440 | tf_op jit(solution)/shard_map/ppermute | solution.py:416
  69.9 7.2 %collective-permute-start.1 = (bf16[112,1024]{1,0:T(8,128)(2,1)}, bf16[112,1024]{1,0:T(8,128)(2,1)S(1)}, u32[]{:S(2)}, u32[]{:S(2)}) collective-permute-start(bf16[112,1024]{1,0:T(8,128)(2,1)} %get-tuple-element.18.after_ref), channel_id=1, source_target_pairs={{0,1},{1,2},{2,3},{3,4},{4,5},{5,6},{6,7},{7,8},{8,9},{9,10},{10,1... | collective-permute-start | bytes 688136 | tf_op jit(solution)/shard_map/ppermute | solution.py:31
  77.1 0.0 collective-permute-done.5.other_ref
  77.1 2.2 %latent_attend.1 = bf16[16,32,128]{2,1,0:T(8,128)(2,1)} custom-call(s32[1]{0:T(128)} %bitcast.2.side_ref, bf16[16,96,128]{2,1,0:T(8,128)(2,1)S(1)} %all-to-all-done.own_ref, bf16[16,64,128]{2,1,0:T(8,128)(2,1)S(1)} %collective-permute-done.5.other_ref), custom_call_target="tpu_custom_call" | custom-call | flops 1000 | bytes 1000 | tf_op jit(solution)/shard_map/latent_attend/pallas_call | solution.py:119
  79.4 15.2 %all-to-all-start.1 = ((bf16[16,32,128]{2,1,0:T(8,128)(2,1)}), bf16[16,32,128]{2,1,0:T(8,128)(2,1)S(1)}, u32[]{:S(2)}, u32[]{:S(2)}) async-start(bf16[16,32,128]{2,1,0:T(8,128)(2,1)} %latent_attend.1), calls=%async_computation.1 | async-start | bytes 262144 | tf_op jit(solution)/shard_map/all_to_all | solution.py:418
  94.6 0.0 collective-permute-done.3.down_ref
  94.6 0.0 copy-start.4
  94.6 0.0 collective-permute-done.1.up_ref
  94.6 0.0 copy-start.5
  94.6 0.7 copy-done.4
  95.3 0.1 copy-done.5
  95.4 0.0 copy-start.2
  95.4 12.3 %far_attention.1 = (bf16[256,1024]{1,0:T(8,128)(2,1)}, f32[32,1152]{1,0:T(8,128)}, f32[1,1152]{1,0:T(1,128)}) custom-call(s32[1]{0:T(128)} %bitcast.block_ref, s32[1,256]{1,0:T(1,128)} %bitcast.4, bf16[256,1024]{1,0:T(8,128)(2,1)} %own_ref.3, bf16[112,1024]{1,0:T(8,128)(2,1)} %copy-done.5, bf16[144,1024]{1,0:T(8,128)(2,1)} %copy-done.4, ...), custom_call_target="tpu_custom_call" | custom-call | flops 30000001024 | bytes 1000 | tf_op jit(solution)/shard_map/far_attention/pallas_call | solution.py:348
  107.7 7.2 %collective-permute-start.4 = (f32[1,1152]{1,0:T(1,128)}, f32[1,1152]{1,0:T(1,128)S(1)}, u32[]{:S(2)}, u32[]{:S(2)}) collective-permute-start(f32[1,1152]{1,0:T(1,128)} %get-tuple-element.24), channel_id=1, source_target_pairs={{1,0},{2,1},{3,2},{4,3},{5,4},{6,5},{7,6},{8,7},{9,8},{10,9},{11,1... | collective-permute-start | bytes 13832 | tf_op jit(solution)/shard_map/ppermute | solution.py:31
  114.9 0.0 all-to-all-done.1.heads_ref
  114.9 0.0 copy-done.2
  114.9 0.8 latent_unpack.1.after_ref
  115.7 0.7 collective-permute-done.4.extra_ref
  116.4 0.0 copy-start
  116.4 0.9 copy-done
  117.3 0.0 copy-start.1
  117.3 0.9 copy-done.1
  118.2 0.9 patch_pool.1
  (1 shorter events, 0.0 us)
Async XLA Ops:
  0.6 50.1 %collective-permute-start = (bf16[256,1024]{1,0:T(8,128)(2,1)}, bf16[256,1024]{1,0:T(8,128)(2,1)S(1)}, u32[]{:S(2)}, u32[]{:S(2)}) collective-permute-start(bf16[256,1024]{1,0:T(8,128)(2,1)} %own_ref.3), channel_id=1, source_target_pairs={{0,1},{1,2},{2,3},{3,4},{4,5},{5,6},{6,7},{7,8},{8,9},{9,10},{10,1... | collective-permute-start | bytes 1572872 | tf_op jit(solution)/shard_map/ppermute | solution.py:31
  9.5 33.3 %collective-permute-start.2 = (bf16[144,1024]{1,0:T(8,128)(2,1)S(1)}, bf16[144,1024]{1,0:T(8,128)(2,1)S(1)}, u32[]{:S(2)}, u32[]{:S(2)}) collective-permute-start(bf16[144,1024]{1,0:T(8,128)(2,1)S(1)} %slice.3), channel_id=1, source_target_pairs={{0,3},{1,0},{2,1},{3,2},{4,7},{5,4},{6,5},{7,6},{8,11},{9,8},{10,9... | collective-permute-start | bytes 884744 | tf_op jit(solution)/shard_map/ppermute | solution.py:41
  20.1 47.5 %all-to-all-start = ((bf16[16,96,128]{2,1,0:T(8,128)(2,1)}), bf16[16,96,128]{2,1,0:T(8,128)(2,1)S(1)}, u32[]{:S(2)}, u32[]{:S(2)}) async-start(bf16[16,96,128]{2,1,0:T(8,128)(2,1)} %latent_pack.1), calls=%async_computation | async-start | bytes 786432 | tf_op jit(solution)/shard_map/all_to_all | solution.py:415
  42.8 51.8 %collective-permute-start.3 = (bf16[144,1024]{1,0:T(8,128)(2,1)S(1)}, bf16[144,1024]{1,0:T(8,128)(2,1)S(1)}, u32[]{:S(2)}, u32[]{:S(2)}) collective-permute-start(bf16[144,1024]{1,0:T(8,128)(2,1)S(1)} %collective-permute-done.2), channel_id=1, source_target_pairs={{3,2},{0,3},{1,4},{2,5},{7,6},{4,7},{5,8},{6,9},{11,10},{8,11},{9,... | collective-permute-start | bytes 884744 | tf_op jit(solution)/shard_map/ppermute | solution.py:42
  50.7 0.8 copy-start.3
  67.6 9.5 %collective-permute-start.5 = (bf16[16,64,128]{2,1,0:T(8,128)(2,1)S(1)}, bf16[16,64,128]{2,1,0:T(8,128)(2,1)S(1)}, u32[]{:S(2)}, u32[]{:S(2)}) collective-permute-start(bf16[16,64,128]{2,1,0:T(8,128)(2,1)S(1)} %latent_split.1), channel_id=1, source_target_pairs={{0,4},{4,0},{1,5},{5,1},{2,6},{6,2},{3,7},{7,3},{8,12},{12,8},{9,1... | collective-permute-start | bytes 786440 | tf_op jit(solution)/shard_map/ppermute | solution.py:416
  69.9 24.7 %collective-permute-start.1 = (bf16[112,1024]{1,0:T(8,128)(2,1)}, bf16[112,1024]{1,0:T(8,128)(2,1)S(1)}, u32[]{:S(2)}, u32[]{:S(2)}) collective-permute-start(bf16[112,1024]{1,0:T(8,128)(2,1)} %get-tuple-element.18.after_ref), channel_id=1, source_target_pairs={{0,1},{1,2},{2,3},{3,4},{4,5},{5,6},{6,7},{7,8},{8,9},{9,10},{10,1... | collective-permute-start | bytes 688136 | tf_op jit(solution)/shard_map/ppermute | solution.py:31
  79.4 35.5 %all-to-all-start.1 = ((bf16[16,32,128]{2,1,0:T(8,128)(2,1)}), bf16[16,32,128]{2,1,0:T(8,128)(2,1)S(1)}, u32[]{:S(2)}, u32[]{:S(2)}) async-start(bf16[16,32,128]{2,1,0:T(8,128)(2,1)} %latent_attend.1), calls=%async_computation.1 | async-start | bytes 262144 | tf_op jit(solution)/shard_map/all_to_all | solution.py:418
  94.6 0.7 copy-start.4
  94.6 0.8 copy-start.5
  95.4 19.5 %copy-start.2 = (s32[256]{0:T(256)S(1)}, s32[256]{0:T(256)}, u32[]{:S(2)}) copy-start(s32[256]{0:T(256)} %param.10) | copy-start | bytes 3076
  107.7 8.7 %collective-permute-start.4 = (f32[1,1152]{1,0:T(1,128)}, f32[1,1152]{1,0:T(1,128)S(1)}, u32[]{:S(2)}, u32[]{:S(2)}) collective-permute-start(f32[1,1152]{1,0:T(1,128)} %get-tuple-element.24), channel_id=1, source_target_pairs={{1,0},{2,1},{3,2},{4,3},{5,4},{6,5},{7,6},{8,7},{9,8},{10,9},{11,1... | collective-permute-start | bytes 13832 | tf_op jit(solution)/shard_map/ppermute | solution.py:31
  116.4 0.9 copy-start
  117.3 0.9 copy-start.1
